TPU v7x, 128 devices: a whole 4x4x4 slice. The times are simulated.
128 devices in a mesh: cube: 8 (over z, x_lo), blk: 16 (over y, x_hi, core).
Axes of the slice: x: 4 (x_hi: 2, x_lo: 2; x = x_hi * 2 + x_lo), y: 4, z: 4, core: 2. Of those that a mesh axis runs over, the one named last changes fastest.
Arguments:
- rows: bfloat16 [196608, 1024], P(('cube', 'blk')), may hold values from -10 to 10
- start_vec: float32 [1024], replicated, may hold values from -6 to 6
- leave: int32 [2, 196608], P(None, ('cube', 'blk')), may hold values from 0 to 1, as said below
- owner: int32 [196608, 1], P(('cube', 'blk')), may hold values from 0 to 15; in each aligned block of 1536 rows (0 to 1535, 1536 to 3071, ...) at most 192 rows name the same one
Outputs:
- scores: float32 [2, 196608], P(None, ('cube', 'blk'))
- leaf_rows: bfloat16 [393216, 1024], P(('cube', 'blk'))
Inputs may be any that keep to these rules, and one draw needn't show every extreme that they name: `leave`: at each level a device marks exactly as many rows as the device with the same blk index whose cube index differs in bit l; at most 768 rows of one device are marked, and some device marks 768 at every level. Among the 1536 rows of one device at most 192 name one owner; some owner is named by 192 rows.
All inputs are finite; a program needn't handle non-finite values.
Results may differ from a plain program's by a relative error of at most 0.001.
Values may be sent and summed in bfloat16 or wider, within the bound.
No kernel may reach another device: no remote copies, remote signals or barrier semaphores. Data moves between devices by JAX's collectives and lax.ppermute only.
A program may use at most 128 MiB of HBM per device.

v0:
```python
import jax
import jax.numpy as jnp
from jax import lax
from jax.sharding import PartitionSpec as P

LEVELS = 2
ITERS = 8
CAPP = 192


def from_partner(value, axis, apart):
    return lax.ppermute(value, axis, [(i, i ^ 1 << apart) for i in range(lax.axis_size(axis))])


def pack_rows(current, leaving, capacity):
    running = jnp.cumsum(leaving)
    slot_ids = jnp.arange(capacity, dtype=jnp.int32)
    source_idx = jnp.sum((running[None, :] <= slot_ids[:, None]).astype(jnp.int32), axis=1)
    filled = slot_ids < running[-1]
    picked = jnp.take(current, jnp.minimum(source_idx, current.shape[0] - 1), axis=0)
    return jnp.where(filled[:, None], picked, jnp.zeros_like(picked))


def place_rows(current, leaving, arrived):
    arrival = jnp.cumsum(leaving) - 1
    fetched = jnp.take(arrived, jnp.clip(arrival, 0, arrived.shape[0] - 1), axis=0)
    return jnp.where(leaving[:, None] == 1, fetched, current)


def leaf_blocks(current, owners, targets, capacity):
    onehot = (owners[:, None] == jnp.arange(targets, dtype=jnp.int32)[None, :]).astype(jnp.int32)
    running = jnp.cumsum(onehot, axis=0)
    slot_ids = jnp.arange(capacity, dtype=jnp.int32)
    source_idx = jnp.sum((running[None, :, :] <= slot_ids[:, None, None]).astype(jnp.int32), axis=1)
    filled = slot_ids[:, None] < running[-1][None, :]
    picked = jnp.take(current, jnp.minimum(source_idx.T, current.shape[0] - 1), axis=0)
    return jnp.where(filled.T[:, :, None], picked, jnp.zeros_like(picked))


def power_iterate(operate, row_sum, members, start_vec):
    direction = start_vec / jnp.sqrt(jnp.sum(start_vec * start_vec))
    for step_no in range(ITERS):
        along = jnp.dot(row_sum, direction, precision=lax.Precision.HIGHEST)
        image_vec = operate(direction) - row_sum * (along / members)
        direction = image_vec / jnp.sqrt(jnp.sum(image_vec * image_vec))
    return direction


def cell_pair(gram_sum, row_sum, tree_level, cube_bits):
    if tree_level == 0:
        return lax.psum((gram_sum, row_sum), ("cube", "blk"))
    gram_sum, row_sum = lax.psum((gram_sum, row_sum), "blk")
    for cube_bit in range(tree_level, cube_bits):
        other_gram, other_sum = from_partner((gram_sum, row_sum), "cube", cube_bit)
        gram_sum = gram_sum + other_gram
        row_sum = row_sum + other_sum
    return (gram_sum, row_sum)


def per_device(rows, start_vec, leave, owner):
    current = rows
    local_rows = current.shape[0]
    cube_bits = lax.axis_size("cube").bit_length() - 1
    scores = []
    for tree_level in range(LEVELS):
        members = local_rows * lax.axis_size("blk") * (lax.axis_size("cube") >> tree_level)
        row_sum = jnp.sum(current, axis=0, dtype=jnp.float32)
        gram_sum = lax.dot_general(
            current, current, (((0,), (0,)), ((), ())), preferred_element_type=jnp.float32
        )
        gram_sum, row_sum = cell_pair(gram_sum, row_sum, tree_level, cube_bits)

        def operate(vector, matrix=gram_sum):
            return jnp.dot(matrix, vector, precision=lax.Precision.HIGHEST)

        direction = power_iterate(operate, row_sum, members, start_vec)
        offset = jnp.dot(row_sum, direction, precision=lax.Precision.HIGHEST) / members
        projected = jnp.dot(
            current, direction, precision=lax.Precision.HIGHEST, preferred_element_type=jnp.float32
        )
        scores.append(projected - offset)
        leaving = leave[tree_level]
        packed = pack_rows(current, leaving, local_rows // 2)
        arrived = from_partner(packed, "cube", tree_level)
        current = place_rows(current, leaving, arrived)
    blocks = leaf_blocks(current, owner[:, 0], lax.axis_size("blk"), CAPP)
    leaf_rows = lax.all_to_all(
        blocks.reshape(-1, current.shape[1]), "blk", split_axis=0, concat_axis=0, tiled=True
    )
    return (jnp.stack(scores), leaf_rows)


def solution(mesh):
    placed = (P(("cube", "blk"), None), P(), P(None, ("cube", "blk")), P(("cube", "blk"), None))
    return jax.shard_map(
        per_device,
        mesh=mesh,
        in_specs=placed,
        out_specs=(P(None, ("cube", "blk")), P(("cube", "blk"), None)),
        check_vma=False,
    )
```

profile of v0, /device:TPU:6, one launch (start us, length us, event | category | flops | bytes accessed | tf_op | source)
XLA Modules:
  0.0 629.0 jit_solution(53172767065992792)
XLA Ops:
  10.4 6.1 gather_fusion.1
  17.9 35.2 %collective-permute-done = bf16[768,1024]{1,0:T(8,128)(2,1)S(1)} collective-permute-done((bf16[768,1024]{1,0:T(8,128)(2,1)S(1)}, bf16[768,1024]{1,0:T(8,128)(2,1)S(1)}, u32[]{:S(2)}, u32[]{:S(2)}) %collective-permute-start) | collective-permute-done | bytes 1572896 | tf_op jit(solution)/shard_map/ppermute | solution.py:12
  53.1 5.8 gather_fusion.2
  69.2 8.3 %fusion.1 = f32[1024,1024]{1,0:T(8,128)} fusion(bf16[1536,1024]{1,0:T(8,128)(2,1)} %param.8), kind=kOutput, calls=%fused_computation.123 | convolution fusion | flops 3221225472 | bytes 7340032 | tf_op jit(solution)/shard_map/dot_general | solution.py:68
  96.0 127.8 %all-reduce.5.cloned.1.call-done = f32[1024,1024]{1,0:T(8,128)} async-done(((f32[1024,1024]{1,0:T(8,128)}), f32[1024,1024]{1,0:T(8,128)}) %all-reduce.5.cloned.1.call-update) | async-done | bytes 4194320 | tf_op jit(solution)/shard_map/psum | solution.py:52
  225.8 35.8 %psum.31 = f32[1024]{0:T(1024)S(1)} all-reduce(f32[1024]{0:T(1024)S(1)} %get-tuple-element.46), channel_id=1, replica_groups=mesh['cube'=8,'blk'=16] {'blk'}, use_global_device_ids=true, to_apply=%region_17.20 | all-reduce | flops 1024 | bytes 8192 | tf_op jit(solution)/shard_map/psum | solution.py:52
  263.4 119.7 %psum.29 = f32[1024]{0:T(1024)S(1)} all-reduce(f32[1024]{0:T(1024)S(1)} %get-tuple-element.50), channel_id=1, replica_groups=mesh['cube'=8,'blk'=16] {'cube','blk'}, use_global_device_ids=true, to_apply=%region_3.0 | all-reduce | flops 1024 | bytes 8192 | tf_op jit(solution)/shard_map/psum | solution.py:51
  385.1 5.8 gather_fusion.4
  394.3 13.9 %gather_fusion = bf16[3072,1024]{1,0:T(8,128)(2,1)} fusion(bf16[1536,1024]{1,0:T(8,128)(2,1)S(1)} %select_select_fusion.1, s32[3072]{0:T(1024)S(1)} %broadcast_clamp_fusion), kind=kCustom, calls=%fused_computation.4 | custom fusion | bytes 12595200 | tf_op jit(solution)/shard_map/jit(_take)/gather | solution.py:36
  408.2 6.9 %select_select_fusion = bf16[16,192,1024]{2,1,0:T(8,128)(2,1)} fusion(bf16[16,192,1024]{2,1,0:T(8,128)(2,1)} %bitcast.99, pred[16,192]{1,0:T(8,128)(4,1)S(1)} %copy.10, pred[16,192]{1,0:T(8,128)(4,1)S(1)} %iota_compare_fusion.4), kind=kLoop, calls=%fused_computation.7 | loop fusion | flops 6291456 | bytes 12589056 | tf_op jit(solution)/shard_map/jit(_where)/select_n | solution.py:37
  415.0 5.9 all-to-all-start
  423.0 5.8 fusion.2
  431.3 5.8 fusion.3
  439.0 6.9 %add.42 = f32[1024,1024]{1,0:T(8,128)} add(f32[1024,1024]{1,0:T(8,128)} %all-reduce.5.cloned.1.call-done, f32[1024,1024]{1,0:T(8,128)} %collective-permute-done.1) | non-fusion elementwise | flops 1048576 | bytes 12582912 | tf_op jit(solution)/shard_map/add | solution.py:55
  455.2 5.8 fusion.5
  463.5 5.8 fusion.6
  471.9 5.8 fusion.7
  480.2 6.1 fusion.8
  488.9 5.8 fusion.9
  499.8 41.0 %collective-permute-done.2 = f32[1024,1024]{1,0:T(8,128)} collective-permute-done((f32[1024,1024]{1,0:T(8,128)}, f32[1024,1024]{1,0:T(8,128)}, u32[]{:S(2)}, u32[]{:S(2)}) %collective-permute-start.2) | collective-permute-done | bytes 4194336 | tf_op jit(solution)/shard_map/ppermute | solution.py:12
  552.8 6.0 fusion.12
  586.3 6.0 fusion.16
  594.9 5.9 fusion.17
  615.5 6.2 copy.54
  (129 shorter events, 106.8 us)
Async XLA Ops:
  7.2 216.6 %all-reduce.5.cloned.1.call-start = ((), (), s32[]{:S(2)}) async-start(), calls=%async_computation.2 | async-start | bytes 8388608 | tf_op jit(solution)/shard_map/psum | solution.py:52
  10.4 7.4 %copy-start.5 = (s32[2,1536]{1,0:T(2,128)S(1)}, s32[2,1536]{1,0:T(2,128)}, u32[]{:S(2)}) copy-start(s32[2,1536]{1,0:T(2,128)} %param.10) | copy-start | bytes 36868
  16.9 36.2 %collective-permute-start = (bf16[768,1024]{1,0:T(8,128)(2,1)S(1)}, bf16[768,1024]{1,0:T(8,128)(2,1)S(1)}, u32[]{:S(2)}, u32[]{:S(2)}) collective-permute-start(bf16[768,1024]{1,0:T(8,128)(2,1)S(1)} %select_select_fusion.4), channel_id=1, source_target_pairs={{0,16},{16,0},{32,48},{48,32},{64,80},{80,64},{96,112},{112,96},{1... | collective-permute-start | bytes 4718600 | tf_op jit(solution)/shard_map/ppermute | solution.py:12
  64.0 21.4 %copy-start.2 = (bf16[1536,1024]{1,0:T(8,128)(2,1)}, bf16[1536,1024]{1,0:T(8,128)(2,1)S(1)}, u32[]{:S(2)}) copy-start(bf16[1536,1024]{1,0:T(8,128)(2,1)S(1)} %get-tuple-element.47) | copy-start | bytes 9437188
  69.0 354.0 %all-reduce.3.cloned.1.call-start = ((), (), s32[]{:S(2)}) async-start(), calls=%async_computation.1 | async-start | bytes 8388608 | tf_op jit(solution)/shard_map/psum | solution.py:51
  77.5 2.4 copy-start.7
  85.3 176.7 %copy-start.6 = (f32[1024]{0:T(1024)S(1)}, f32[1024]{0:T(1024)}, u32[]{:S(2)}) copy-start(f32[1024]{0:T(1024)} %param.9) | copy-start | bytes 12292
  90.6 294.5 %collective-permute-start.5 = (bf16[768,1024]{1,0:T(8,128)(2,1)S(1)}, bf16[768,1024]{1,0:T(8,128)(2,1)S(1)}, u32[]{:S(2)}, u32[]{:S(2)}) collective-permute-start(bf16[768,1024]{1,0:T(8,128)(2,1)S(1)} %select_select_fusion.3), channel_id=1, source_target_pairs={{0,32},{16,48},{32,0},{48,16},{64,96},{80,112},{96,64},{112,80},{1... | collective-permute-start | bytes 4718600 | tf_op jit(solution)/shard_map/ppermute | solution.py:12
  223.8 215.3 %collective-permute-start.1 = (f32[1024,1024]{1,0:T(8,128)}, f32[1024,1024]{1,0:T(8,128)}, u32[]{:S(2)}, u32[]{:S(2)}) collective-permute-start(f32[1024,1024]{1,0:T(8,128)} %all-reduce.5.cloned.1.call-done), channel_id=1, source_target_pairs={{0,32},{16,48},{32,0},{48,16},{64,96},{80,112},{96,64},{112,80},{1... | collective-permute-start | bytes 12582920 | tf_op jit(solution)/shard_map/ppermute | solution.py:12
  261.6 121.5 %collective-permute-start.3 = (f32[1024]{0:T(1024)S(1)}, f32[1024]{0:T(1024)S(1)}, u32[]{:S(2)}, u32[]{:S(2)}) collective-permute-start(f32[1024]{0:T(1024)S(1)} %psum.31), channel_id=1, source_target_pairs={{0,32},{16,48},{32,0},{48,16},{64,96},{80,112},{96,64},{112,80},{1... | collective-permute-start | bytes 12296 | tf_op jit(solution)/shard_map/ppermute | solution.py:12
  383.1 37.9 %collective-permute-start.4 = (f32[1024]{0:T(1024)S(1)}, f32[1024]{0:T(1024)S(1)}, u32[]{:S(2)}, u32[]{:S(2)}) collective-permute-start(f32[1024]{0:T(1024)S(1)} %add.44), channel_id=1, source_target_pairs={{0,64},{16,80},{32,96},{48,112},{64,0},{80,16},{96,32},{112,48},{1... | collective-permute-start | bytes 12296 | tf_op jit(solution)/shard_map/ppermute | solution.py:12
  415.0 84.7 %all-to-all-start = ((bf16[16,192,1024]{2,1,0:T(8,128)(2,1)}), bf16[16,192,1024]{2,1,0:T(8,128)(2,1)}, u32[]{:S(2)}, u32[]{:S(2)}) async-start(bf16[16,192,1024]{2,1,0:T(8,128)(2,1)} %select_select_fusion), calls=%async_computation | async-start | bytes 12582912 | tf_op jit(solution)/shard_map/all_to_all | solution.py:87
  439.0 9.3 %copy-start.1 = (f32[1024,1024]{1,0:T(8,128)S(1)}, f32[1024,1024]{1,0:T(8,128)}, u32[]{:S(2)}) copy-start(f32[1024,1024]{1,0:T(8,128)} %all-reduce.3.cloned.1.call-done) | copy-start | bytes 12582916
  446.0 94.8 %collective-permute-start.2 = (f32[1024,1024]{1,0:T(8,128)}, f32[1024,1024]{1,0:T(8,128)}, u32[]{:S(2)}, u32[]{:S(2)}) collective-permute-start(f32[1024,1024]{1,0:T(8,128)} %add.42), channel_id=1, source_target_pairs={{0,64},{16,80},{32,96},{48,112},{64,0},{80,16},{96,32},{112,48},{1... | collective-permute-start | bytes 12582920 | tf_op jit(solution)/shard_map/ppermute | solution.py:12
  480.2 17.0 %copy-start.4 = (bf16[1536,1024]{1,0:T(8,128)(2,1)S(1)}, bf16[1536,1024]{1,0:T(8,128)(2,1)}, u32[]{:S(2)}) copy-start(bf16[1536,1024]{1,0:T(8,128)(2,1)} %param.8) | copy-start | bytes 9437188
  545.2 2.0 copy-start
  594.9 16.8 %copy-start.3 = (bf16[1536,1024]{1,0:T(8,128)(2,1)S(1)}, bf16[1536,1024]{1,0:T(8,128)(2,1)}, u32[]{:S(2)}) copy-start(bf16[1536,1024]{1,0:T(8,128)(2,1)} %copy-done.2) | copy-start | bytes 9437188
Sparse Core Ops, SparseCore 0:
  69.1 154.5 all-reduce.4
  228.7 160.0 all-reduce.2
where the time goes:
time: 635 us; the launch traced here: 629 us
  waiting for transfers between devices  204 us (32%)
  blocking collectives  155 us (24%)
  matrix products  107 us (17%)
  other arithmetic  61.8 us (10%)
  local copies, waits for them, and re-layouts  46.6 us (7%)
  between operations  38.5 us (6%)
  starting transfers between devices  15.4 us (2%)
    psum x1, waiting for transfers between devices, cell_pair(): gram_sum, row_sum = lax.psum((gram_sum, row_sum), 'blk')  128 us
    psum x1, blocking collectives, cell_pair(): return lax.psum((gram_sum, row_sum), ('cube', 'blk'))  120 us
    dot_general x16, matrix products, operate(): return jnp.dot(matrix, vector, precision=lax.Precision.HIGHEST)  88.7 us
    ppermute x6, waiting for transfers between devices, from_partner(): lax.ppermute(value, axis, [(i, i ^ 1 << apart) for i in range(lax.axis_si...  76.2 us
    psum x1, blocking collectives, cell_pair(): gram_sum, row_sum = lax.psum((gram_sum, row_sum), 'blk')  35.8 us
    gather x1, local copies, waits for them, and re-layouts, leaf_blocks(): jnp.take(current, jnp.minimum(source_idx.T, current.shape[0] - 1), axis=0)  13.9 us
    dot_general x2, matrix products, per_device(): lax.dot_general(current, current, (((0,), (0,)), ((), ())), preferred_ele...  13.3 us
  transfers between devices with their start and end apart: 9, of which 3 were waited for; matrix products, arithmetic and copies ran while one was open for 19% of the time, Pallas kernels for 0%

commit v1 on v0

v1 whole, which is shorter than its diff:
```python
import jax
import jax.numpy as jnp
from jax import lax
from jax.experimental import pallas as pl
from jax.experimental.pallas import tpu as pltpu
from jax.sharding import PartitionSpec as P

D = 1024
ROWS = 1536
CAP = 768
CAPP = 192
N_BLK = 16
N_CUBE = 8
ITERS = 8
HALF = 512
LANES = 128
BLOCKS = [(i, j) for i in range(8) for j in range(i, 8)]
CHUNK = 9 * LANES
PIECE = CHUNK // 4
F32 = jnp.float32
BF16 = jnp.bfloat16
PARAMS = pltpu.CompilerParams(vmem_limit_bytes=56 * 2**20)
VMEM = pl.BlockSpec(memory_space=pltpu.VMEM)
SMEM = pl.BlockSpec(memory_space=pltpu.SMEM)
ANY = pl.BlockSpec(memory_space=pl.ANY)


def iota(shape, dim):
    return lax.broadcasted_iota(jnp.int32, shape, dim)


def shape_of(shape, dtype):
    return jax.ShapeDtypeStruct(shape, dtype)


def running_count(flags):
    upper = jnp.where(iota((LANES, LANES), 0) <= iota((LANES, LANES), 1), 1.0, 0.0).astype(BF16)
    parts = []
    before = jnp.zeros((flags.shape[0], 1), F32)
    for b in range(ROWS // LANES):
        part = flags[:, b * LANES : (b + 1) * LANES].astype(BF16)
        part = jnp.dot(part, upper, preferred_element_type=F32) + before
        before = part[:, LANES - 1 : LANES]
        parts.append(part)
    return jnp.concatenate(parts, axis=1)


def slot_row(leave_ref, level):
    flags = jnp.broadcast_to(leave_ref[level : level + 1, :].astype(F32), (8, ROWS))
    return jnp.where(flags > 0.5, running_count(flags) - 1.0, -1.0)


def store_column(row, col_ref):
    for b in range(ROWS // LANES):
        part = jnp.broadcast_to(row[0:1, b * LANES : (b + 1) * LANES], (LANES, LANES))
        col_ref[b * LANES : (b + 1) * LANES, :] = part.T


def picker(row, first, count):
    slots = (iota((count, ROWS), 0) + first).astype(F32)
    return jnp.where(slots == row[0:1, :], 1.0, 0.0).astype(BF16)


def spreader(col, slots):
    parts = []
    for t in range(slots // LANES):
        lanes = (iota(col.shape, 1) + t * LANES).astype(F32)
        parts.append(jnp.where(col == lanes, 1.0, 0.0).astype(BF16))
    return jnp.concatenate(parts, axis=1)


def pack_first_kernel(leave_ref, rows_ref, out_ref):
    row = slot_row(leave_ref, 0)
    for t in range(CAP // 256):
        hot = picker(row, t * 256, 256)
        out_ref[t * 256 : (t + 1) * 256, :] = jnp.dot(hot, rows_ref[...], preferred_element_type=F32).astype(BF16)


def pack_first(leave, rows, half):
    return pl.pallas_call(
        pack_first_kernel,
        grid=(1,),
        in_specs=[pl.BlockSpec((2, ROWS), lambda i: (0, 0)), pl.BlockSpec((ROWS, HALF), lambda i: (0, half))],
        out_specs=pl.BlockSpec((CAP, HALF), lambda i: (0, 0)),
        out_shape=shape_of((CAP, HALF), BF16),
        compiler_params=PARAMS,
        name="pack_first",
    )(leave, rows)


def slots_kernel(leave_ref, owner_ref, row_ref, col_ref):
    for level in range(2):
        row = slot_row(leave_ref, level)
        row_ref[level * 8 : (level + 1) * 8, :] = row
        store_column(row, col_ref.at[level])
    owner = jnp.broadcast_to(owner_ref[...], (N_BLK, ROWS))
    named = jnp.where(owner == iota((N_BLK, ROWS), 0), 1.0, 0.0)
    place = named * (running_count(named) - 1.0 + (iota((N_BLK, ROWS), 0) * CAPP).astype(F32))
    row_ref[16:24, :] = jnp.broadcast_to(jnp.sum(place, axis=0, keepdims=True), (8, ROWS))


def slots(leave, owner):
    return pl.pallas_call(
        slots_kernel,
        in_specs=[VMEM, VMEM],
        out_specs=[VMEM, VMEM],
        out_shape=[shape_of((24, ROWS), F32), shape_of((2, ROWS, LANES), F32)],
        compiler_params=PARAMS,
        name="slots",
    )(leave, owner)


def placed(col, arrived, stay):
    moved = jnp.dot(spreader(col, CAP), arrived, preferred_element_type=F32).astype(BF16)
    leaves = jnp.concatenate([col] * (HALF // LANES), axis=1) >= 0.0
    return jnp.where(leaves, moved.astype(F32), stay.astype(F32)).astype(BF16)


def swap_kernel(row_ref, col_ref, rows_ref, arrived_ref, next_ref, packed_ref):
    arrived = arrived_ref[...]
    for t in range(ROWS // 256):
        here = slice(t * 256, (t + 1) * 256)
        next_ref[here, :] = placed(col_ref[0, here, :], arrived, rows_ref[here, :])
    row = row_ref[8:16, :]
    for t in range(CAP // 256):
        hot = picker(row, t * 256, 256)
        packed_ref[t * 256 : (t + 1) * 256, :] = jnp.dot(hot, next_ref[...], preferred_element_type=F32).astype(BF16)


def swap(row, col, rows, arrived, half):
    whole = lambda shape: pl.BlockSpec(shape, lambda i: (0,) * len(shape))
    return pl.pallas_call(
        swap_kernel,
        grid=(1,),
        in_specs=[
            whole((24, ROWS)),
            whole((1, ROWS, LANES)),
            pl.BlockSpec((ROWS, HALF), lambda i: (0, half)),
            whole((CAP, HALF)),
        ],
        out_specs=[whole((ROWS, HALF)), whole((CAP, HALF))],
        out_shape=[shape_of((ROWS, HALF), BF16), shape_of((CAP, HALF), BF16)],
        compiler_params=PARAMS,
        name="swap",
    )(row, col, rows, arrived)


def leaf_kernel(row_ref, col_ref, rows_ref, arrived_ref, out_ref, last_ref):
    arrived = arrived_ref[...]
    for t in range(ROWS // 256):
        here = slice(t * 256, (t + 1) * 256)
        last_ref[here, :] = placed(col_ref[0, here, :], arrived, rows_ref[here, :])
    row = row_ref[16:24, :]
    for t in range(N_BLK * CAPP // 256):
        hot = picker(row, t * 256, 256)
        out_ref[t * 256 : (t + 1) * 256, :] = jnp.dot(hot, last_ref[...], preferred_element_type=F32).astype(BF16)


def leaf_pack(row, col, rows, arrived):
    whole = lambda shape: pl.BlockSpec(shape, lambda i: (0,) * len(shape))
    return pl.pallas_call(
        leaf_kernel,
        grid=(1,),
        in_specs=[
            whole((24, ROWS)),
            pl.BlockSpec((1, ROWS, LANES), lambda i: (1, 0, 0)),
            whole((ROWS, HALF)),
            whole((CAP, HALF)),
        ],
        out_specs=whole((N_BLK * CAPP, HALF)),
        out_shape=shape_of((N_BLK * CAPP, HALF), BF16),
        scratch_shapes=[pltpu.VMEM((ROWS, HALF), BF16)],
        compiler_params=PARAMS,
        name="leaf_pack",
    )(row, col, rows, arrived)


def gram_kernel(flip_ref, leave_ref, rows_ref, keep_ref, send_ref, turned_ref, masked_ref):
    turned_ref[...] = rows_ref[...].T
    flag = jnp.bitwise_xor(jnp.broadcast_to(leave_ref[0:1, :], (8, ROWS)), flip_ref[0]).astype(F32)
    lane = iota((8, LANES), 1)
    sub = iota((8, LANES), 0)
    for out_ref, weight in ((keep_ref, flag), (send_ref, 1.0 - flag)):
        masked_ref[...] = turned_ref[...] * weight[0:1, :].astype(BF16)
        sums = jnp.dot(weight.astype(BF16), rows_ref[...], preferred_element_type=F32)
        for r in range(4):
            strip = jnp.dot(
                masked_ref[r * 256 : (r + 1) * 256, :], rows_ref[:, r * 256 :], preferred_element_type=F32
            )
            for i in (2 * r, 2 * r + 1):
                for j in range(i, 8):
                    at = BLOCKS.index((i, j))
                    top = (at % 9) * LANES
                    out_ref[at // 9, top : top + LANES, :] = strip[
                        (i - 2 * r) * LANES : (i - 2 * r + 1) * LANES, (j - 2 * r) * LANES : (j - 2 * r + 1) * LANES
                    ]
        for i in range(8):
            at = BLOCKS.index((i, i))
            top = (at % 9) * LANES + 120
            own = sums[:, i * LANES : (i + 1) * LANES]
            held = jnp.where((sub == 7) & (lane < 64), own, out_ref[at // 9, top : top + 8, :])
            out_ref[at // 9, top : top + 8, :] = jnp.where((sub == 6) & (lane < 64), pltpu.roll(own, 64, 1), held)


def gram(flip, leave, rows):
    return pl.pallas_call(
        gram_kernel,
        in_specs=[SMEM, VMEM, VMEM],
        out_specs=[VMEM, VMEM],
        out_shape=[shape_of((4, CHUNK, LANES), F32)] * 2,
        scratch_shapes=[pltpu.VMEM((D, ROWS), BF16)] * 2,
        compiler_params=PARAMS,
        name="gram",
    )(flip, leave, rows)


def power_kernel(place_ref, members_ref, start_ref, a_ref, b_ref, c_ref, d_ref, out_ref, packed_ref, mat_ref):
    y, z = place_ref[0], place_ref[1]
    for k, part_ref in enumerate((a_ref, b_ref, c_ref, d_ref)):
        for m in range(4):
            at = (lax.rem(y + m, 4) * 4 + lax.rem(z + k, 4)) * PIECE
            packed_ref[pl.ds(pl.multiple_of(at, 8), PIECE), :] = part_ref[m]
    members = members_ref[0]
    lane = iota((8, LANES), 1)
    wide_lane, wide_sub = iota((LANES, LANES), 1), iota((LANES, LANES), 0)
    sums_row, sums_col = [], []
    for i in range(8):
        top = BLOCKS.index((i, i)) * LANES
        tail = packed_ref[top + 120 : top + 128, :]
        row = jnp.where(lane[0:1] < 64, tail[7:8, :], pltpu.roll(tail, 64, 1)[6:7, :])
        sums_row.append(row)
        sums_col.append(jnp.broadcast_to(row, (LANES, LANES)).T)
    for i in range(8):
        for j in range(i, 8):
            top = BLOCKS.index((i, j)) * LANES
            block = packed_ref[top : top + LANES, :]
            other = block.T
            if i == j:
                block = jnp.where((wide_sub >= 126) & (wide_lane < 64), other, block)
            hi, hj = slice(i * LANES, (i + 1) * LANES), slice(j * LANES, (j + 1) * LANES)
            mat_ref[hi, hj] = block - sums_col[i] * (sums_row[j] / members)
            if i != j:
                mat_ref[hj, hi] = other - sums_col[j] * (sums_row[i] / members)
    start = start_ref[...]
    vec = start / jnp.sqrt(jnp.sum(start * start, axis=1, keepdims=True))
    for _ in range(ITERS // 2):
        cols = []
        square = jnp.zeros((8, 1), F32)
        for i in range(8):
            total = jnp.zeros((LANES, LANES), F32)
            for j in range(8):
                total = total + mat_ref[i * LANES : (i + 1) * LANES, j * LANES : (j + 1) * LANES] * vec[
                    :, j * LANES : (j + 1) * LANES
                ]
            col = jnp.sum(total, axis=1, keepdims=True)
            cols.append(col)
        norm = sum(jnp.sum(col * col, axis=0, keepdims=True) for col in cols)
        norm = jnp.sqrt(norm)
        total = jnp.zeros((8, D), F32)
        for i in range(8):
            col = cols[i] / norm
            for s in range(LANES // 8):
                at = i * LANES + s * 8
                total = total + mat_ref[at : at + 8, :] * col[s * 8 : (s + 1) * 8, :]
        vec = jnp.sum(total, axis=0, keepdims=True)
        vec = vec / jnp.sqrt(jnp.sum(vec * vec, axis=1, keepdims=True))
    sums = jnp.concatenate(sums_row, axis=1)
    offset = jnp.sum(sums * vec, axis=1, keepdims=True) / members
    out_ref[0:8, :] = jnp.where(iota((8, D), 0) == 0, vec, offset)


def power(place, members, start, parts):
    return pl.pallas_call(
        power_kernel,
        in_specs=[SMEM, SMEM, VMEM] + [VMEM] * 4,
        out_specs=VMEM,
        out_shape=shape_of((8, D), F32),
        scratch_shapes=[pltpu.VMEM((len(BLOCKS) * LANES, LANES), F32), pltpu.VMEM((D, D), F32)],
        compiler_params=PARAMS,
        name="power",
    )(place, members, start, *parts)


def project(vec, blocks):
    sub = None
    total = None
    at = 0
    for block in blocks:
        here = vec[:, at : at + block.shape[1]]
        at += block.shape[1]
        high = here.astype(BF16)
        rest = here - high.astype(F32)
        mid = rest.astype(BF16)
        low = (rest - mid.astype(F32)).astype(BF16)
        sub = iota((8, here.shape[1]), 0)
        terms = jnp.where(
            sub == 0,
            high.astype(F32),
            jnp.where(sub == 1, mid.astype(F32), jnp.where(sub == 2, low.astype(F32), 0.0)),
        ).astype(BF16)
        part = lax.dot_general(terms, block, (((1,), (1,)), ((), ())), preferred_element_type=F32)
        total = part if total is None else total + part
    return total[0:1, :] + total[1:2, :] + total[2:3, :]


def scores_kernel(core_ref, mine_ref, other_ref, rows_ref, left_ref, right_ref, out_ref):
    first = core_ref[0] == 0
    top = jnp.where(first, mine_ref[...], other_ref[...])
    low = jnp.where(first, other_ref[...], mine_ref[...])
    out_ref[0:1, :] = project(top[0:1, :], [rows_ref[...]]) - top[1:2, 0:1]
    out_ref[1:2, :] = project(low[0:1, :], [left_ref[...], right_ref[...]]) - low[1:2, 0:1]


def all_scores(core, mine, other, rows, left, right):
    return pl.pallas_call(
        scores_kernel,
        in_specs=[SMEM] + [VMEM] * 5,
        out_specs=VMEM,
        out_shape=shape_of((2, ROWS), F32),
        compiler_params=PARAMS,
        name="scores",
    )(core, mine, other, rows, left, right)


def join_first_kernel(part_ref, out_ref):
    out_ref[...] = part_ref[...]


def join_second_kernel(part_ref, held_ref, out_ref):
    out_ref[...] = part_ref[...]


def join(left, right):
    count = left.shape[0]
    block = pl.BlockSpec((512, HALF), lambda i: (i, 0))
    held = pl.pallas_call(
        join_first_kernel,
        grid=(count // 512,),
        in_specs=[block],
        out_specs=pl.BlockSpec((512, HALF), lambda i: (i, 0)),
        out_shape=shape_of((count, D), BF16),
        compiler_params=PARAMS,
        name="join_first",
    )(left)
    return pl.pallas_call(
        join_second_kernel,
        grid=(count // 512,),
        in_specs=[block, ANY],
        out_specs=pl.BlockSpec((512, HALF), lambda i: (i, 1)),
        out_shape=shape_of((count, D), BF16),
        input_output_aliases={1: 0},
        compiler_params=PARAMS,
        name="join_second",
    )(right, held)


def along_y(value, k):
    return lax.ppermute(value, "blk", [(i, (i // 4 + k) % 4 * 4 + i % 4) for i in range(N_BLK)])


def along_z(value, k):
    return lax.ppermute(value, "cube", [(i, (i // 2 + k) % 4 * 2 + i % 2) for i in range(N_CUBE)])


def across(value, axis, bit):
    return lax.ppermute(value, axis, [(i, i ^ bit) for i in range(lax.axis_size(axis))])


def after(value, earlier):
    return lax.optimization_barrier((value, earlier))[0]


def per_device(rows, start_vec, leave, owner):
    cube, blk = lax.axis_index("cube"), lax.axis_index("blk")
    z, x_lo = cube // 2, cube % 2
    y, core = blk // 4, blk % 2

    packed_l = pack_first(leave, rows, 0)
    arrived_l = across(packed_l, "cube", 1)
    packed_r = pack_first(leave, rows, 1)

    flip = jnp.bitwise_xor(x_lo, core).astype(jnp.int32).reshape(1)
    keep, send = gram(flip, leave, rows)
    got = across(send, "blk", 1)
    row, col = slots(leave, owner.reshape(1, ROWS))

    def part(k):
        at = (y + k) % 4
        return lax.dynamic_index_in_dim(keep, at, 0, False) + lax.dynamic_index_in_dim(got, at, 0, False)

    parts = [part(k) for k in range(4)]
    own = parts[0]
    for k in (1, 2, 3):
        own = own + along_y(parts[k], k)
    quarters = own.reshape(4, PIECE, LANES)
    own = lax.dynamic_index_in_dim(quarters, z, 0, False)
    for k in (1, 2, 3):
        own = own + along_z(lax.dynamic_index_in_dim(quarters, (z + k) % 4, 0, False), k)
    own = own + across(own, "cube", 1)
    own = own + across(own, "blk", 2)
    other = across(own, "blk", 1)
    piece = jnp.where(core == 0, own + other, jnp.where(x_lo == 0, own, other))
    stack = jnp.stack([piece] + [along_y(piece, -k) for k in (1, 2, 3)])
    gathered = [stack] + [along_z(stack, -k) for k in (1, 2, 3)]

    packed_r = after(packed_r, arrived_l)
    arrived_r = across(packed_r, "cube", 1)
    next_l, packed_l = swap(row, col, rows, arrived_l, 0)
    arrived2_l = across(packed_l, "cube", 2)
    next_r, packed_r = swap(row, col, rows, arrived_r, 1)
    packed_r = after(packed_r, arrived2_l)
    arrived2_r = across(packed_r, "cube", 2)
    leaf_l = leaf_pack(row, col, next_l, arrived2_l)
    out_l = lax.all_to_all(leaf_l, "blk", split_axis=0, concat_axis=0, tiled=True)
    leaf_r = leaf_pack(row, col, next_r, arrived2_r)
    out_r = lax.all_to_all(leaf_r, "blk", split_axis=0, concat_axis=0, tiled=True)

    place = jnp.stack([y, z]).astype(jnp.int32)
    members = jnp.where(core == 0, ROWS * N_BLK * N_CUBE, ROWS * N_BLK * N_CUBE // 2).astype(F32).reshape(1)
    mine = power(place, members, start_vec.reshape(1, D), gathered)
    theirs = across(mine, "blk", 1)
    scores = all_scores(core.astype(jnp.int32).reshape(1), mine, theirs, rows, next_l, next_r)
    return scores, join(out_l, out_r)


def solution(mesh):
    placed_at = (P(("cube", "blk"), None), P(), P(None, ("cube", "blk")), P(("cube", "blk"), None))
    return jax.shard_map(
        per_device,
        mesh=mesh,
        in_specs=placed_at,
        out_specs=(P(None, ("cube", "blk")), P(("cube", "blk"), None)),
        check_vma=False,
    )
```

time: 635 us -> 286 us (0.45)
  blocking collectives: 155 us -> 0 us
  matrix products: 107 us -> 0 us
  Pallas kernels: 0 us -> 73 us
  other arithmetic: 61.8 us -> 5.87 us
  waiting for transfers between devices: 204 us -> 155 us
  local copies, waits for them, and re-layouts: 46.6 us -> 5.85 us
  between operations: 38.5 us -> 0.75 us
  starting transfers between devices: 15.4 us -> 43.7 us
    psum x2 -> x0, blocking collectives: 155 us -> none  [the longest x1 120 us: cell_pair(): return lax.psum((gram_sum, row_sum), ('cube', 'blk'))]
    psum x2 -> x0, waiting for transfers between devices: 128 us -> none  [the longest x1 128 us: cell_pair(): gram_sum, row_sum = lax.psum((gram_sum, row_sum), 'blk')]
    dot_general x20 -> x0, matrix products: 107 us -> none  [the longest x16 88.7 us: operate(): return jnp.dot(matrix, vector, precision=lax.Precision.HIGHEST)]
    ppermute x6 -> x21, waiting for transfers between devices: 76.2 us -> 155 us  [the longest x9 114 us: across(): lax.ppermute(value, axis, [(i, i ^ bit) for i in range(lax.axis_size(axis...]
    pallas_call x0 -> x12, Pallas kernels: none -> 73 us  [the longest x2 19.6 us: leaf_pack(): pl.pallas_call(leaf_kernel, grid=(1,), in_specs=[whole((24, ROWS)), pl.Bl...]
    gather x5 -> x0, local copies, waits for them, and re-layouts: 35.1 us -> none  [the longest x1 13.9 us: leaf_blocks(): jnp.take(current, jnp.minimum(source_idx.T, current.shape[0] - 1), axis=0)]
    ppermute x6 -> x21, starting transfers between devices: 9.25 us -> 29.3 us  [the longest x6 11.6 us: along_z(): lax.ppermute(value, 'cube', [(i, (i // 2 + k) % 4 * 2 + i % 2) for i in r...]
    reduce_sum x21 -> x0, other arithmetic: 19.9 us -> none  [the longest x16 9.78 us: power_iterate(): direction = image_vec / jnp.sqrt(jnp.sum(image_vec * image_vec))]
  transfers between devices with their start and end apart: 9 -> 23, of which waited for: 3 -> 15; matrix products, arithmetic and copies ran while one was open for 19% -> 2% of each run, Pallas kernels for 0% -> 17%
where the time goes in v1:
time: 286 us; the launch traced here: 284 us
  waiting for transfers between devices  155 us (54%)
  Pallas kernels  73 us (26%)
  starting transfers between devices  43.7 us (15%)
  other arithmetic  5.87 us (2%)
  local copies, waits for them, and re-layouts  5.85 us (2%)
    ppermute x9, waiting for transfers between devices, across(): lax.ppermute(value, axis, [(i, i ^ bit) for i in range(lax.axis_size(axis...  114 us
    ppermute x6, waiting for transfers between devices, along_z(): lax.ppermute(value, 'cube', [(i, (i // 2 + k) % 4 * 2 + i % 2) for i in r...  33 us
    pallas_call x2, Pallas kernels, leaf_pack(): pl.pallas_call(leaf_kernel, grid=(1,), in_specs=[whole((24, ROWS)), pl.Bl...  19.6 us
    ppermute x6, starting transfers between devices, along_z(): lax.ppermute(value, 'cube', [(i, (i // 2 + k) % 4 * 2 + i % 2) for i in r...  11.6 us
    pallas_call x2, Pallas kernels, swap(): pl.pallas_call(swap_kernel, grid=(1,), in_specs=[whole((24, ROWS)), whole...  10.8 us
    ppermute x6, starting transfers between devices, along_y(): lax.ppermute(value, 'blk', [(i, (i // 4 + k) % 4 * 4 + i % 4) for i in ra...  9.47 us
    pallas_call x2, Pallas kernels, pack_first(): pl.pallas_call(pack_first_kernel, grid=(1,), in_specs=[pl.BlockSpec((2, R...  8.63 us
    pallas_call x1, Pallas kernels, gram(): pl.pallas_call(gram_kernel, in_specs=[SMEM, VMEM, VMEM], out_specs=[VMEM,...  8.47 us
  transfers between devices with their start and end apart: 23, of which 15 were waited for; matrix products, arithmetic and copies ran while one was open for 2% of the time, Pallas kernels for 17%

profile of v1, /device:TPU:6, one launch (start us, length us, event | category | flops | bytes accessed | tf_op | source)
XLA Modules:
  0.0 284.2 jit_solution(11764280082729690211)
XLA Ops:
  0.6 4.3 %pack_first.2 = bf16[768,512]{1,0:T(8,128)(2,1)} custom-call(s32[2,1536]{1,0:T(2,128)} %leave_ref.7, bf16[1536,1024]{1,0:T(8,128)(2,1)} %rows_ref.11), custom_call_target="tpu_custom_call" | custom-call | tf_op jit(solution)/shard_map/pack_first/pallas_call | solution.py:80
  9.0 15.5 %collective-permute-done.17.arrived_ref = bf16[768,512]{1,0:T(8,128)(2,1)S(1)} collective-permute-done((bf16[768,512]{1,0:T(8,128)(2,1)}, bf16[768,512]{1,0:T(8,128)(2,1)S(1)}, u32[]{:S(2)}, u32[]{:S(2)}) %collective-permute-start.17) | collective-permute-done | bytes 786464 | tf_op jit(solution)/shard_map/ppermute | solution.py:366
  25.3 5.4 %swap.2 = (bf16[1536,512]{1,0:T(8,128)(2,1)}, bf16[768,512]{1,0:T(8,128)(2,1)}) custom-call(f32[24,1536]{1,0:T(8,128)} %get-tuple-element.14.row_ref, f32[2,1536,128]{2,1,0:T(8,128)} %get-tuple-element.15.col_ref, bf16[1536,1024]{1,0:T(8,128)(2,1)} %rows_ref.11, bf16[768,512]{1,0:T(8,128)(2,1)} %copy-done.3), custom_call_target="tpu_custom_call" | custom-call | tf_op jit(solution)/shard_map/swap/pallas_call | solution.py:132
  32.6 16.9 %collective-permute-done.19.arrived_ref = bf16[768,512]{1,0:T(8,128)(2,1)S(1)} collective-permute-done((bf16[768,512]{1,0:T(8,128)(2,1)}, bf16[768,512]{1,0:T(8,128)(2,1)S(1)}, u32[]{:S(2)}, u32[]{:S(2)}) %collective-permute-start.19) | collective-permute-done | bytes 786464 | tf_op jit(solution)/shard_map/ppermute | solution.py:366
  50.4 9.8 %leaf_pack.3 = bf16[3072,512]{1,0:T(8,128)(2,1)} custom-call(f32[24,1536]{1,0:T(8,128)} %get-tuple-element.14.row_ref, f32[2,1536,128]{2,1,0:T(8,128)} %get-tuple-element.15.col_ref, bf16[1536,512]{1,0:T(8,128)(2,1)} %get-tuple-element.16.left_ref.rows_ref, bf16[768,512]{1,0:T(8,128)(2,1)} %copy-done.2), custom_call_target="tpu_custom_call" | custom-call | tf_op jit(solution)/shard_map/leaf_pack/pallas_call | solution.py:161
  60.2 7.5 %all-to-all-start.1 = ((bf16[16,192,512]{2,1,0:T(8,128)(2,1)}), bf16[16,192,512]{2,1,0:T(8,128)(2,1)S(1)}, u32[]{:S(2)}, u32[]{:S(2)}) async-start(bf16[16,192,512]{2,1,0:T(8,128)(2,1)} %bitcast.41), calls=%async_computation.1 | async-start | bytes 6291456 | tf_op jit(solution)/shard_map/all_to_all | solution.py:414
  67.6 8.5 %gram.1 = (f32[4,1152,128]{2,1,0:T(8,128)}, f32[4,1152,128]{2,1,0:T(8,128)}) custom-call(s32[1]{0:T(128)} %bitcast.5.flip_ref, s32[2,1536]{1,0:T(2,128)} %leave_ref.7, bf16[1536,1024]{1,0:T(8,128)(2,1)} %rows_ref.11), custom_call_target="tpu_custom_call" | custom-call | tf_op jit(solution)/shard_map/gram/pallas_call | solution.py:206
  76.3 4.3 %pack_first.3 = bf16[768,512]{1,0:T(8,128)(2,1)} custom-call(s32[2,1536]{1,0:T(2,128)} %leave_ref.7, bf16[1536,1024]{1,0:T(8,128)(2,1)} %rows_ref.11), custom_call_target="tpu_custom_call" | custom-call | tf_op jit(solution)/shard_map/pack_first/pallas_call | solution.py:80
  81.4 39.8 %collective-permute-done.18.arrived_ref = bf16[768,512]{1,0:T(8,128)(2,1)S(1)} collective-permute-done((bf16[768,512]{1,0:T(8,128)(2,1)}, bf16[768,512]{1,0:T(8,128)(2,1)S(1)}, u32[]{:S(2)}, u32[]{:S(2)}) %collective-permute-start.18) | collective-permute-done | bytes 786464 | tf_op jit(solution)/shard_map/ppermute | solution.py:366
  122.2 5.4 %swap.3 = (bf16[1536,512]{1,0:T(8,128)(2,1)}, bf16[768,512]{1,0:T(8,128)(2,1)}) custom-call(f32[24,1536]{1,0:T(8,128)} %get-tuple-element.14.row_ref, f32[2,1536,128]{2,1,0:T(8,128)} %get-tuple-element.15.col_ref, bf16[1536,1024]{1,0:T(8,128)(2,1)} %rows_ref.11, bf16[768,512]{1,0:T(8,128)(2,1)} %copy-done.4), custom_call_target="tpu_custom_call" | custom-call | tf_op jit(solution)/shard_map/swap/pallas_call | solution.py:132
  137.8 9.1 %collective-permute-done.20.arrived_ref = bf16[768,512]{1,0:T(8,128)(2,1)} collective-permute-done((bf16[768,512]{1,0:T(8,128)(2,1)}, bf16[768,512]{1,0:T(8,128)(2,1)}, u32[]{:S(2)}, u32[]{:S(2)}) %collective-permute-start.20) | collective-permute-done | bytes 786464 | tf_op jit(solution)/shard_map/ppermute | solution.py:366
  146.9 9.8 %leaf_pack.2 = bf16[3072,512]{1,0:T(8,128)(2,1)} custom-call(f32[24,1536]{1,0:T(8,128)} %get-tuple-element.14.row_ref, f32[2,1536,128]{2,1,0:T(8,128)} %get-tuple-element.15.col_ref, bf16[1536,512]{1,0:T(8,128)(2,1)} %get-tuple-element.18.right_ref.rows_ref, bf16[768,512]{1,0:T(8,128)(2,1)} %collective-permute-done.20.arrived_ref), custom_call_target="tpu_custom_call" | custom-call | tf_op jit(solution)/shard_map/leaf_pack/pallas_call | solution.py:161
  158.4 6.9 %all-to-all-start = ((bf16[16,192,512]{2,1,0:T(8,128)(2,1)}), bf16[16,192,512]{2,1,0:T(8,128)(2,1)}, u32[]{:S(2)}, u32[]{:S(2)}) async-start(bf16[16,192,512]{2,1,0:T(8,128)(2,1)} %bitcast.40), calls=%async_computation | async-start | bytes 6291456 | tf_op jit(solution)/shard_map/all_to_all | solution.py:416
  169.2 3.6 %collective-permute-start.5 = (f32[288,128]{1,0:T(8,128)S(1)}, f32[288,128]{1,0:T(8,128)S(1)}, u32[]{:S(2)}, u32[]{:S(2)}) collective-permute-start(f32[288,128]{1,0:T(8,128)S(1)} %get-tuple-element.27), channel_id=1, source_target_pairs={{0,64},{16,80},{32,96},{48,112},{64,0},{80,16},{96,32},{112,48},{1... | collective-permute-start | bytes 442376 | tf_op jit(solution)/shard_map/ppermute | solution.py:362
  175.4 4.3 %collective-permute-done.5 = f32[288,128]{1,0:T(8,128)S(1)} collective-permute-done((f32[288,128]{1,0:T(8,128)S(1)}, f32[288,128]{1,0:T(8,128)S(1)}, u32[]{:S(2)}, u32[]{:S(2)}) %collective-permute-start.5) | collective-permute-done | bytes 147488 | tf_op jit(solution)/shard_map/ppermute | solution.py:362
  181.1 24.6 %collective-permute-done.7 = f32[288,128]{1,0:T(8,128)S(1)} collective-permute-done((f32[288,128]{1,0:T(8,128)S(1)}, f32[288,128]{1,0:T(8,128)S(1)}, u32[]{:S(2)}, u32[]{:S(2)}) %collective-permute-start.7) | collective-permute-done | bytes 147488 | tf_op jit(solution)/shard_map/ppermute | solution.py:366
  207.1 5.6 %collective-permute-done.8 = f32[288,128]{1,0:T(8,128)S(1)} collective-permute-done((f32[288,128]{1,0:T(8,128)S(1)}, f32[288,128]{1,0:T(8,128)S(1)}, u32[]{:S(2)}, u32[]{:S(2)}) %collective-permute-start.8) | collective-permute-done | bytes 147488 | tf_op jit(solution)/shard_map/ppermute | solution.py:366
  226.3 3.9 %collective-permute-start.13 = (f32[4,288,128]{2,1,0:T(8,128)S(1)}, f32[4,288,128]{2,1,0:T(8,128)S(1)}, u32[]{:S(2)}, u32[]{:S(2)}) collective-permute-start(f32[4,288,128]{2,1,0:T(8,128)S(1)} %pad_maximum_fusion.a_ref), channel_id=1, source_target_pairs={{0,96},{16,112},{32,0},{48,16},{64,32},{80,48},{96,64},{112,80},{1... | collective-permute-start | bytes 1769480 | tf_op jit(solution)/shard_map/ppermute | solution.py:362
  232.1 23.5 %collective-permute-done.13.b_ref = f32[4,288,128]{2,1,0:T(8,128)S(1)} collective-permute-done((f32[4,288,128]{2,1,0:T(8,128)S(1)}, f32[4,288,128]{2,1,0:T(8,128)S(1)}, u32[]{:S(2)}, u32[]{:S(2)}) %collective-permute-start.13) | collective-permute-done | bytes 589856 | tf_op jit(solution)/shard_map/ppermute | solution.py:362
  255.6 3.4 %collective-permute-done.15.d_ref = f32[4,288,128]{2,1,0:T(8,128)S(1)} collective-permute-done((f32[4,288,128]{2,1,0:T(8,128)S(1)}, f32[4,288,128]{2,1,0:T(8,128)S(1)}, u32[]{:S(2)}, u32[]{:S(2)}) %collective-permute-start.15) | collective-permute-done | bytes 589856 | tf_op jit(solution)/shard_map/ppermute | solution.py:362
  259.8 6.6 %power.1.mine_ref = f32[8,1024]{1,0:T(8,128)} custom-call(s32[2]{0:T(128)} %pad_add_fusion.place_ref, f32[1]{0:T(128)} %bitcast.3.members_ref, f32[1,1024]{1,0:T(1,128)} %bitcast.50, f32[4,288,128]{2,1,0:T(8,128)} %copy-done.1, f32[4,288,128]{2,1,0:T(8,128)} %copy-done.5, f32[4,288,128]{2,1,0:T(8,128)} %copy-done.6, f32[4,288,128]{2,1,0:T(8,128)} %copy-done.7), custom_call_target="tpu_custom_call" | custom-call | tf_op jit(solution)/shard_map/power/pallas_call | solution.py:273
  268.5 5.2 %scores.1 = f32[2,1536]{1,0:T(2,128)} custom-call(s32[1]{0:T(128)} %bitcast.core_ref, f32[8,1024]{1,0:T(8,128)} %power.1.mine_ref, f32[8,1024]{1,0:T(8,128)} %copy-done.8, bf16[1536,1024]{1,0:T(8,128)(2,1)} %rows_ref.11, bf16[1536,512]{1,0:T(8,128)(2,1)} %get-tuple-element.16.left_ref.rows_ref, bf16[1536,512]{1,0:T(8,128)(2,1)} %get-tuple-element.18.right_ref.rows_ref), custom_call_target="tpu_custom_call" | custom-call | tf_op jit(solution)/shard_map/scores/pallas_call | solution.py:315
  273.7 5.3 %join_first.1.held_ref = bf16[3072,1024]{1,0:T(8,128)(2,1)} custom-call(bf16[3072,512]{1,0:T(8,128)(2,1)} %bitcast.42), custom_call_target="tpu_custom_call" | custom-call | tf_op jit(solution)/shard_map/join_first/pallas_call | solution.py:336
  279.0 5.3 %join_second.1 = bf16[3072,1024]{1,0:T(8,128)(2,1)} custom-call(bf16[3072,512]{1,0:T(8,128)(2,1)} %bitcast.21.part_ref, bf16[3072,1024]{1,0:T(8,128)(2,1)} %join_first.1.held_ref), custom_call_target="tpu_custom_call", output_to_operand_aliasing={{}: (1, {})} | custom-call | tf_op jit(solution)/shard_map/join_second/pallas_call | solution.py:345
  (61 shorter events, 49.1 us)
Async XLA Ops:
  4.9 19.5 %collective-permute-start.17 = (bf16[768,512]{1,0:T(8,128)(2,1)}, bf16[768,512]{1,0:T(8,128)(2,1)S(1)}, u32[]{:S(2)}, u32[]{:S(2)}) collective-permute-start(bf16[768,512]{1,0:T(8,128)(2,1)} %pack_first.2), channel_id=1, source_target_pairs={{0,16},{16,0},{32,48},{48,32},{64,80},{80,64},{96,112},{112,96},{1... | collective-permute-start | bytes 2359304 | tf_op jit(solution)/shard_map/ppermute | solution.py:366
  30.7 18.8 %collective-permute-start.19 = (bf16[768,512]{1,0:T(8,128)(2,1)}, bf16[768,512]{1,0:T(8,128)(2,1)S(1)}, u32[]{:S(2)}, u32[]{:S(2)}) collective-permute-start(bf16[768,512]{1,0:T(8,128)(2,1)} %get-tuple-element.20), channel_id=1, source_target_pairs={{0,32},{16,48},{32,0},{48,16},{64,96},{80,112},{96,64},{112,80},{1... | collective-permute-start | bytes 2359304 | tf_op jit(solution)/shard_map/ppermute | solution.py:366
  60.2 96.5 %all-to-all-start.1 = ((bf16[16,192,512]{2,1,0:T(8,128)(2,1)}), bf16[16,192,512]{2,1,0:T(8,128)(2,1)S(1)}, u32[]{:S(2)}, u32[]{:S(2)}) async-start(bf16[16,192,512]{2,1,0:T(8,128)(2,1)} %bitcast.41), calls=%async_computation.1 | async-start | bytes 6291456 | tf_op jit(solution)/shard_map/all_to_all | solution.py:414
  76.1 53.2 %collective-permute-start = (f32[4,1152,128]{2,1,0:T(8,128)}, f32[4,1152,128]{2,1,0:T(8,128)}, u32[]{:S(2)}, u32[]{:S(2)}) collective-permute-start(f32[4,1152,128]{2,1,0:T(8,128)} %get-tuple-element.13), channel_id=1, source_target_pairs={{0,1},{1,0},{2,3},{3,2},{4,5},{5,4},{6,7},{7,6},{8,9},{9,8},{10,11... | collective-permute-start | bytes 7077896 | tf_op jit(solution)/shard_map/ppermute | solution.py:366
  80.6 40.7 %collective-permute-start.18 = (bf16[768,512]{1,0:T(8,128)(2,1)}, bf16[768,512]{1,0:T(8,128)(2,1)S(1)}, u32[]{:S(2)}, u32[]{:S(2)}) collective-permute-start(bf16[768,512]{1,0:T(8,128)(2,1)} %pack_first.3), channel_id=1, source_target_pairs={{0,16},{16,0},{32,48},{48,32},{64,80},{80,64},{96,112},{112,96},{1... | collective-permute-start | bytes 2359304 | tf_op jit(solution)/shard_map/ppermute | solution.py:366
  127.5 19.4 %collective-permute-start.20 = (bf16[768,512]{1,0:T(8,128)(2,1)}, bf16[768,512]{1,0:T(8,128)(2,1)}, u32[]{:S(2)}, u32[]{:S(2)}) collective-permute-start(bf16[768,512]{1,0:T(8,128)(2,1)} %get-tuple-element.21), channel_id=1, source_target_pairs={{0,32},{16,48},{32,0},{48,16},{64,96},{80,112},{96,64},{112,80},{1... | collective-permute-start | bytes 2359304 | tf_op jit(solution)/shard_map/ppermute | solution.py:366
  132.5 32.8 %collective-permute-start.1 = (f32[1152,128]{1,0:T(8,128)}, f32[1152,128]{1,0:T(8,128)}, u32[]{:S(2)}, u32[]{:S(2)}) collective-permute-start(f32[1152,128]{1,0:T(8,128)} %get-tuple-element.22), channel_id=1, source_target_pairs={{0,4},{1,5},{2,6},{3,7},{4,8},{5,9},{6,10},{7,11},{8,12},{9,13},{1... | collective-permute-start | bytes 1769480 | tf_op jit(solution)/shard_map/ppermute | solution.py:358
  133.0 32.3 %collective-permute-start.2 = (f32[1152,128]{1,0:T(8,128)}, f32[1152,128]{1,0:T(8,128)}, u32[]{:S(2)}, u32[]{:S(2)}) collective-permute-start(f32[1152,128]{1,0:T(8,128)} %get-tuple-element.24), channel_id=1, source_target_pairs={{0,8},{1,9},{2,10},{3,11},{4,12},{5,13},{6,14},{7,15},{8,0},{9,1},... | collective-permute-start | bytes 1769480 | tf_op jit(solution)/shard_map/ppermute | solution.py:358
  135.7 29.7 %collective-permute-start.3 = (f32[1152,128]{1,0:T(8,128)}, f32[1152,128]{1,0:T(8,128)}, u32[]{:S(2)}, u32[]{:S(2)}) collective-permute-start(f32[1152,128]{1,0:T(8,128)} %get-tuple-element.23), channel_id=1, source_target_pairs={{0,12},{1,13},{2,14},{3,15},{4,0},{5,1},{6,2},{7,3},{8,4},{9,5},{1... | collective-permute-start | bytes 1769480 | tf_op jit(solution)/shard_map/ppermute | solution.py:358
  158.4 120.5 %all-to-all-start = ((bf16[16,192,512]{2,1,0:T(8,128)(2,1)}), bf16[16,192,512]{2,1,0:T(8,128)(2,1)}, u32[]{:S(2)}, u32[]{:S(2)}) async-start(bf16[16,192,512]{2,1,0:T(8,128)(2,1)} %bitcast.40), calls=%async_computation | async-start | bytes 6291456 | tf_op jit(solution)/shard_map/all_to_all | solution.py:416
  167.3 8.1 %collective-permute-start.4 = (f32[288,128]{1,0:T(8,128)S(1)}, f32[288,128]{1,0:T(8,128)S(1)}, u32[]{:S(2)}, u32[]{:S(2)}) collective-permute-start(f32[288,128]{1,0:T(8,128)S(1)} %get-tuple-element.25), channel_id=1, source_target_pairs={{0,32},{16,48},{32,64},{48,80},{64,96},{80,112},{96,0},{112,16},{1... | collective-permute-start | bytes 442376 | tf_op jit(solution)/shard_map/ppermute | solution.py:362
  169.2 10.6 %collective-permute-start.5 = (f32[288,128]{1,0:T(8,128)S(1)}, f32[288,128]{1,0:T(8,128)S(1)}, u32[]{:S(2)}, u32[]{:S(2)}) collective-permute-start(f32[288,128]{1,0:T(8,128)S(1)} %get-tuple-element.27), channel_id=1, source_target_pairs={{0,64},{16,80},{32,96},{48,112},{64,0},{80,16},{96,32},{112,48},{1... | collective-permute-start | bytes 442376 | tf_op jit(solution)/shard_map/ppermute | solution.py:362
  172.7 7.0 %collective-permute-start.6 = (f32[288,128]{1,0:T(8,128)S(1)}, f32[288,128]{1,0:T(8,128)S(1)}, u32[]{:S(2)}, u32[]{:S(2)}) collective-permute-start(f32[288,128]{1,0:T(8,128)S(1)} %get-tuple-element.26), channel_id=1, source_target_pairs={{0,96},{16,112},{32,0},{48,16},{64,32},{80,48},{96,64},{112,80},{1... | collective-permute-start | bytes 442376 | tf_op jit(solution)/shard_map/ppermute | solution.py:362
  179.8 25.8 %collective-permute-start.7 = (f32[288,128]{1,0:T(8,128)S(1)}, f32[288,128]{1,0:T(8,128)S(1)}, u32[]{:S(2)}, u32[]{:S(2)}) collective-permute-start(f32[288,128]{1,0:T(8,128)S(1)} %fusion.3), channel_id=1, source_target_pairs={{0,16},{16,0},{32,48},{48,32},{64,80},{80,64},{96,112},{112,96},{1... | collective-permute-start | bytes 442376 | tf_op jit(solution)/shard_map/ppermute | solution.py:366
  205.7 7.0 %collective-permute-start.8 = (f32[288,128]{1,0:T(8,128)S(1)}, f32[288,128]{1,0:T(8,128)S(1)}, u32[]{:S(2)}, u32[]{:S(2)}) collective-permute-start(f32[288,128]{1,0:T(8,128)S(1)} %add.166), channel_id=1, source_target_pairs={{0,2},{1,3},{2,0},{3,1},{4,6},{5,7},{6,4},{7,5},{8,10},{9,11},{10,... | collective-permute-start | bytes 442376 | tf_op jit(solution)/shard_map/ppermute | solution.py:366
  212.7 1.5 collective-permute-start.9
  214.2 6.8 %collective-permute-start.10 = (f32[288,128]{1,0:T(8,128)S(1)}, f32[288,128]{1,0:T(8,128)S(1)}, u32[]{:S(2)}, u32[]{:S(2)}) collective-permute-start(f32[288,128]{1,0:T(8,128)S(1)} %select_select_fusion), channel_id=1, source_target_pairs={{0,12},{1,13},{2,14},{3,15},{4,0},{5,1},{6,2},{7,3},{8,4},{9,5},{1... | collective-permute-start | bytes 442376 | tf_op jit(solution)/shard_map/ppermute | solution.py:358
  215.9 8.2 %collective-permute-start.11 = (f32[288,128]{1,0:T(8,128)S(1)}, f32[288,128]{1,0:T(8,128)S(1)}, u32[]{:S(2)}, u32[]{:S(2)}) collective-permute-start(f32[288,128]{1,0:T(8,128)S(1)} %select_select_fusion), channel_id=1, source_target_pairs={{0,8},{1,9},{2,10},{3,11},{4,12},{5,13},{6,14},{7,15},{8,0},{9,1},... | collective-permute-start | bytes 442376 | tf_op jit(solution)/shard_map/ppermute | solution.py:358
  217.0 9.2 %collective-permute-start.12 = (f32[288,128]{1,0:T(8,128)S(1)}, f32[288,128]{1,0:T(8,128)S(1)}, u32[]{:S(2)}, u32[]{:S(2)}) collective-permute-start(f32[288,128]{1,0:T(8,128)S(1)} %select_select_fusion), channel_id=1, source_target_pairs={{0,4},{1,5},{2,6},{3,7},{4,8},{5,9},{6,10},{7,11},{8,12},{9,13},{1... | collective-permute-start | bytes 442376 | tf_op jit(solution)/shard_map/ppermute | solution.py:358
  226.3 32.8 %copy-start.1 = (f32[4,288,128]{2,1,0:T(8,128)}, f32[4,288,128]{2,1,0:T(8,128)S(1)}, u32[]{:S(2)}) copy-start(f32[4,288,128]{2,1,0:T(8,128)S(1)} %pad_maximum_fusion.a_ref) | copy-start | bytes 1769476
  226.3 29.3 %collective-permute-start.13 = (f32[4,288,128]{2,1,0:T(8,128)S(1)}, f32[4,288,128]{2,1,0:T(8,128)S(1)}, u32[]{:S(2)}, u32[]{:S(2)}) collective-permute-start(f32[4,288,128]{2,1,0:T(8,128)S(1)} %pad_maximum_fusion.a_ref), channel_id=1, source_target_pairs={{0,96},{16,112},{32,0},{48,16},{64,32},{80,48},{96,64},{112,80},{1... | collective-permute-start | bytes 1769480 | tf_op jit(solution)/shard_map/ppermute | solution.py:362
  230.2 25.4 %collective-permute-start.14 = (f32[4,288,128]{2,1,0:T(8,128)S(1)}, f32[4,288,128]{2,1,0:T(8,128)S(1)}, u32[]{:S(2)}, u32[]{:S(2)}) collective-permute-start(f32[4,288,128]{2,1,0:T(8,128)S(1)} %pad_maximum_fusion.a_ref), channel_id=1, source_target_pairs={{0,64},{16,80},{32,96},{48,112},{64,0},{80,16},{96,32},{112,48},{1... | collective-permute-start | bytes 1769480 | tf_op jit(solution)/shard_map/ppermute | solution.py:362
  230.2 28.8 %collective-permute-start.15 = (f32[4,288,128]{2,1,0:T(8,128)S(1)}, f32[4,288,128]{2,1,0:T(8,128)S(1)}, u32[]{:S(2)}, u32[]{:S(2)}) collective-permute-start(f32[4,288,128]{2,1,0:T(8,128)S(1)} %pad_maximum_fusion.a_ref), channel_id=1, source_target_pairs={{0,32},{16,48},{32,64},{48,80},{64,96},{80,112},{96,0},{112,16},{1... | collective-permute-start | bytes 1769480 | tf_op jit(solution)/shard_map/ppermute | solution.py:362
  266.5 1.4 collective-permute-start.16
  (8 other events, 12.7 us)

commit v2 on v1

--- a/solution.py
+++ b/solution.py
@@ -20,6 +20,14 @@
 F32 = jnp.float32
 BF16 = jnp.bfloat16
 PARAMS = pltpu.CompilerParams(vmem_limit_bytes=56 * 2**20)
+
+
+def cost(microseconds):
+    return pl.CostEstimate(
+        flops=int(microseconds * 1.15e9), bytes_accessed=int(microseconds * 3.69e6), transcendentals=0
+    )
+
+
 VMEM = pl.BlockSpec(memory_space=pltpu.VMEM)
 SMEM = pl.BlockSpec(memory_space=pltpu.SMEM)
 ANY = pl.BlockSpec(memory_space=pl.ANY)
@@ -84,6 +92,7 @@
         out_specs=pl.BlockSpec((CAP, HALF), lambda i: (0, 0)),
         out_shape=shape_of((CAP, HALF), BF16),
         compiler_params=PARAMS,
+        cost_estimate=cost(4.3),
         name="pack_first",
     )(leave, rows)
 
@@ -106,6 +115,7 @@
         out_specs=[VMEM, VMEM],
         out_shape=[shape_of((24, ROWS), F32), shape_of((2, ROWS, LANES), F32)],
         compiler_params=PARAMS,
+        cost_estimate=cost(3.2),
         name="slots",
     )(leave, owner)
 
@@ -141,6 +151,7 @@
         out_specs=[whole((ROWS, HALF)), whole((CAP, HALF))],
         out_shape=[shape_of((ROWS, HALF), BF16), shape_of((CAP, HALF), BF16)],
         compiler_params=PARAMS,
+        cost_estimate=cost(20.0 if half == 0 else 5.3),
         name="swap",
     )(row, col, rows, arrived)
 
@@ -171,6 +182,7 @@
         out_shape=shape_of((N_BLK * CAPP, HALF), BF16),
         scratch_shapes=[pltpu.VMEM((ROWS, HALF), BF16)],
         compiler_params=PARAMS,
+        cost_estimate=cost(9.8),
         name="leaf_pack",
     )(row, col, rows, arrived)
 
@@ -210,6 +222,7 @@
         out_shape=[shape_of((4, CHUNK, LANES), F32)] * 2,
         scratch_shapes=[pltpu.VMEM((D, ROWS), BF16)] * 2,
         compiler_params=PARAMS,
+        cost_estimate=cost(8.6),
         name="gram",
     )(flip, leave, rows)
 
@@ -277,6 +290,7 @@
         out_shape=shape_of((8, D), F32),
         scratch_shapes=[pltpu.VMEM((len(BLOCKS) * LANES, LANES), F32), pltpu.VMEM((D, D), F32)],
         compiler_params=PARAMS,
+        cost_estimate=cost(6.6),
         name="power",
     )(place, members, start, *parts)
 
@@ -318,6 +332,7 @@
         out_specs=VMEM,
         out_shape=shape_of((2, ROWS), F32),
         compiler_params=PARAMS,
+        cost_estimate=cost(5.2),
         name="scores",
     )(core, mine, other, rows, left, right)
 
@@ -330,26 +345,32 @@
     out_ref[...] = part_ref[...]
 
 
-def join(left, right):
-    count = left.shape[0]
-    block = pl.BlockSpec((512, HALF), lambda i: (i, 0))
-    held = pl.pallas_call(
+JOIN = 512
+
+
+def join_first(left):
+    return pl.pallas_call(
         join_first_kernel,
-        grid=(count // 512,),
-        in_specs=[block],
-        out_specs=pl.BlockSpec((512, HALF), lambda i: (i, 0)),
-        out_shape=shape_of((count, D), BF16),
-        compiler_params=PARAMS,
+        grid=(N_BLK * CAPP // JOIN,),
+        in_specs=[pl.BlockSpec((JOIN, HALF), lambda i: (i, 0))],
+        out_specs=pl.BlockSpec((JOIN, HALF), lambda i: (i, 0)),
+        out_shape=shape_of((N_BLK * CAPP, D), BF16),
+        compiler_params=PARAMS,
+        cost_estimate=cost(5.2),
         name="join_first",
     )(left)
+
+
+def join_second(right, held):
     return pl.pallas_call(
         join_second_kernel,
-        grid=(count // 512,),
-        in_specs=[block, ANY],
-        out_specs=pl.BlockSpec((512, HALF), lambda i: (i, 1)),
-        out_shape=shape_of((count, D), BF16),
+        grid=(N_BLK * CAPP // JOIN,),
+        in_specs=[pl.BlockSpec((JOIN, HALF), lambda i: (i, 0)), ANY],
+        out_specs=pl.BlockSpec((JOIN, HALF), lambda i: (i, 1)),
+        out_shape=shape_of((N_BLK * CAPP, D), BF16),
         input_output_aliases={1: 0},
         compiler_params=PARAMS,
+        cost_estimate=cost(5.2),
         name="join_second",
     )(right, held)
 
@@ -360,6 +381,15 @@
 
 def along_z(value, k):
     return lax.ppermute(value, "cube", [(i, (i // 2 + k) % 4 * 2 + i % 2) for i in range(N_CUBE)])
+
+
+def along_x(value, k):
+    pairs = []
+    for i in range(N_CUBE * N_BLK):
+        cube, blk = i // N_BLK, i % N_BLK
+        x = (blk // 2 % 2 * 2 + cube % 2 + k) % 4
+        pairs.append((i, (cube // 2 * 2 + x % 2) * N_BLK + blk // 4 * 4 + x // 2 * 2 + blk % 2))
+    return lax.ppermute(value, ("cube", "blk"), pairs)
 
 
 def across(value, axis, bit):
@@ -377,50 +407,66 @@
 
     packed_l = pack_first(leave, rows, 0)
     arrived_l = across(packed_l, "cube", 1)
-    packed_r = pack_first(leave, rows, 1)
+    leave_b = after(leave, packed_l)
+    packed_r = pack_first(leave_b, rows, 1)
+    row, col = slots(leave_b, owner.reshape(1, ROWS))
 
     flip = jnp.bitwise_xor(x_lo, core).astype(jnp.int32).reshape(1)
-    keep, send = gram(flip, leave, rows)
+    leave_c, packed_r, row = lax.optimization_barrier((leave, packed_r, row))
+    keep, send = gram(flip, leave_c, rows)
     got = across(send, "blk", 1)
-    row, col = slots(leave, owner.reshape(1, ROWS))
+
+    packed_r, arrived_l, keep = lax.optimization_barrier((packed_r, arrived_l, keep))
+    arrived_r = across(packed_r, "cube", 1)
+    next_l, packed_l = swap(row, col, rows, arrived_l, 0)
+    arrived2_l = across(packed_l, "cube", 2)
+
+    got = after(got, packed_l)
 
     def part(k):
         at = (y + k) % 4
         return lax.dynamic_index_in_dim(keep, at, 0, False) + lax.dynamic_index_in_dim(got, at, 0, False)
 
-    parts = [part(k) for k in range(4)]
-    own = parts[0]
-    for k in (1, 2, 3):
-        own = own + along_y(parts[k], k)
+    parts = lax.optimization_barrier([part(k) for k in range(4)])
+    moved = [along_y(parts[k], k) for k in (1, 2, 3)]
+
+    next_r, packed_r = swap(row, col, rows, after(arrived_r, parts), 1)
+    arrived2_r = across(packed_r, "cube", 2)
+    leaf_l = leaf_pack(row, col, next_l, after(arrived2_l, packed_r))
+
+    moved, _, arrived2_r = lax.optimization_barrier((moved, leaf_l, arrived2_r))
+    out_l = lax.all_to_all(leaf_l, "blk", split_axis=0, concat_axis=0, tiled=True)
+    own = parts[0] + moved[0] + moved[1] + moved[2]
     quarters = own.reshape(4, PIECE, LANES)
-    own = lax.dynamic_index_in_dim(quarters, z, 0, False)
-    for k in (1, 2, 3):
-        own = own + along_z(lax.dynamic_index_in_dim(quarters, (z + k) % 4, 0, False), k)
-    own = own + across(own, "cube", 1)
-    own = own + across(own, "blk", 2)
+    parts = lax.optimization_barrier(
+        [lax.dynamic_index_in_dim(quarters, (z + k) % 4, 0, False) for k in range(4)]
+    )
+    moved = [along_z(parts[k], k) for k in (1, 2, 3)]
+
+    leaf_r = leaf_pack(row, col, next_r, after(arrived2_r, parts))
+
+    moved = after(moved, leaf_r)
+    own = parts[0] + moved[0] + moved[1] + moved[2]
     other = across(own, "blk", 1)
-    piece = jnp.where(core == 0, own + other, jnp.where(x_lo == 0, own, other))
-    stack = jnp.stack([piece] + [along_y(piece, -k) for k in (1, 2, 3)])
+    both = own + other
+    mine = jnp.where(core == 0, both, jnp.where(x_lo == 0, own, other))
+    theirs = jnp.where(core == 0, both, jnp.where(x_lo == 0, other, own))
+    mine, theirs, out_l = lax.optimization_barrier((mine, theirs, out_l))
+    piece = mine + along_x(mine, 2) + along_x(theirs, 1) + along_x(theirs, 3)
+    near = [along_y(piece, -k) for k in (1, 2, 3)]
+    near, leaf_r, out_l = lax.optimization_barrier((near, leaf_r, out_l))
+    out_r = lax.all_to_all(leaf_r, "blk", split_axis=0, concat_axis=0, tiled=True)
+    stack = jnp.stack([piece] + near)
     gathered = [stack] + [along_z(stack, -k) for k in (1, 2, 3)]
-
-    packed_r = after(packed_r, arrived_l)
-    arrived_r = across(packed_r, "cube", 1)
-    next_l, packed_l = swap(row, col, rows, arrived_l, 0)
-    arrived2_l = across(packed_l, "cube", 2)
-    next_r, packed_r = swap(row, col, rows, arrived_r, 1)
-    packed_r = after(packed_r, arrived2_l)
-    arrived2_r = across(packed_r, "cube", 2)
-    leaf_l = leaf_pack(row, col, next_l, arrived2_l)
-    out_l = lax.all_to_all(leaf_l, "blk", split_axis=0, concat_axis=0, tiled=True)
-    leaf_r = leaf_pack(row, col, next_r, arrived2_r)
-    out_r = lax.all_to_all(leaf_r, "blk", split_axis=0, concat_axis=0, tiled=True)
+    held = join_first(after(out_l, stack))
+    held, gathered = lax.optimization_barrier((held, gathered))
 
     place = jnp.stack([y, z]).astype(jnp.int32)
     members = jnp.where(core == 0, ROWS * N_BLK * N_CUBE, ROWS * N_BLK * N_CUBE // 2).astype(F32).reshape(1)
     mine = power(place, members, start_vec.reshape(1, D), gathered)
     theirs = across(mine, "blk", 1)
     scores = all_scores(core.astype(jnp.int32).reshape(1), mine, theirs, rows, next_l, next_r)
-    return scores, join(out_l, out_r)
+    return scores, join_second(out_r, held)
 
 
 def solution(mesh):

time: 286 us -> 190 us (0.66)
  waiting for transfers between devices: 155 us -> 59.9 us
    ppermute x9 -> x7, waiting for transfers between devices: 114 us -> 8.31 us  [across(): lax.ppermute(value, axis, [(i, i ^ bit) for i in range(lax.axis_size(axis...]
    all_to_all x1, waiting for transfers between devices: 0.01 us -> 16.8 us  [per_device(): lax.all_to_all(leaf_l, 'blk', split_axis=0, concat_axis=0, tiled=True)]
    ppermute x6, waiting for transfers between devices: 33 us -> 20.8 us  [along_z(): lax.ppermute(value, 'cube', [(i, (i // 2 + k) % 4 * 2 + i % 2) for i in r...]
    ppermute x0 -> x3, waiting for transfers between devices: none -> 6.08 us  [along_x(): return lax.ppermute(value, ('cube', 'blk'), pairs)]
    ppermute x0 -> x3, starting transfers between devices: none -> 4.84 us  [along_x(): return lax.ppermute(value, ('cube', 'blk'), pairs)]
    ppermute x9 -> x7, starting transfers between devices: 8.21 us -> 5.7 us  [across(): lax.ppermute(value, axis, [(i, i ^ bit) for i in range(lax.axis_size(axis...]
    unnamed x18 -> x24, local copies, waits for them, and re-layouts: 5.81 us -> 4.03 us
  transfers between devices with their start and end apart: 23 -> 24, of which waited for: 15 -> 13; matrix products, arithmetic and copies ran while one was open for 2% -> 4% of each run, Pallas kernels for 17% -> 34%
where the time goes in v2:
time: 190 us; the launch traced here: 188 us
  Pallas kernels  73.3 us (39%)
  waiting for transfers between devices  59.9 us (32%)
  starting transfers between devices  43.1 us (23%)
  other arithmetic  6.57 us (3%)
  local copies, waits for them, and re-layouts  4.08 us (2%)
    ppermute x6, waiting for transfers between devices, along_z(): lax.ppermute(value, 'cube', [(i, (i // 2 + k) % 4 * 2 + i % 2) for i in r...  20.8 us
    pallas_call x2, Pallas kernels, leaf_pack(): pl.pallas_call(leaf_kernel, grid=(1,), in_specs=[whole((24, ROWS)), pl.Bl...  19.6 us
    all_to_all x1, waiting for transfers between devices, per_device(): lax.all_to_all(leaf_l, 'blk', split_axis=0, concat_axis=0, tiled=True)  16.8 us
    ppermute x6, starting transfers between devices, along_z(): lax.ppermute(value, 'cube', [(i, (i // 2 + k) % 4 * 2 + i % 2) for i in r...  11.3 us
    pallas_call x2, Pallas kernels, swap(): pl.pallas_call(swap_kernel, grid=(1,), in_specs=[whole((24, ROWS)), whole...  11 us
    pallas_call x2, Pallas kernels, pack_first(): pl.pallas_call(pack_first_kernel, grid=(1,), in_specs=[pl.BlockSpec((2, R...  8.7 us
    pallas_call x1, Pallas kernels, gram(): pl.pallas_call(gram_kernel, in_specs=[SMEM, VMEM, VMEM], out_specs=[VMEM,...  8.48 us
    ppermute x6, starting transfers between devices, along_y(): lax.ppermute(value, 'blk', [(i, (i // 4 + k) % 4 * 4 + i % 4) for i in ra...  8.36 us
  transfers between devices with their start and end apart: 24, of which 13 were waited for; matrix products, arithmetic and copies ran while one was open for 4% of the time, Pallas kernels for 34%

profile of v2, /device:TPU:6, one launch (start us, length us, event | category | flops | bytes accessed | tf_op | source)
XLA Modules:
  0.0 187.7 jit_solution(9545364669782739911)
XLA Ops:
  0.6 4.4 %pack_first.2 = bf16[768,512]{1,0:T(8,128)(2,1)} custom-call(s32[2,1536]{1,0:T(2,128)} %leave_ref.4, bf16[1536,1024]{1,0:T(8,128)(2,1)} %rows_ref.11), custom_call_target="tpu_custom_call" | custom-call | flops 4944999936 | bytes 15867000 | tf_op jit(solution)/shard_map/pack_first/pallas_call | solution.py:88
  5.8 4.3 %pack_first.3 = bf16[768,512]{1,0:T(8,128)(2,1)} custom-call(s32[2,1536]{1,0:T(2,128)} %leave_ref.4, bf16[1536,1024]{1,0:T(8,128)(2,1)} %rows_ref.11), custom_call_target="tpu_custom_call" | custom-call | flops 4944999936 | bytes 15867000 | tf_op jit(solution)/shard_map/pack_first/pallas_call | solution.py:88
  10.2 3.2 %slots.1 = (f32[24,1536]{1,0:T(8,128)}, f32[2,1536,128]{2,1,0:T(8,128)}) custom-call(s32[2,1536]{1,0:T(2,128)} %leave_ref.4, s32[1,1536]{1,0:T(1,128)} %bitcast.40), custom_call_target="tpu_custom_call" | custom-call | flops 3680000000 | bytes 11808000 | tf_op jit(solution)/shard_map/slots/pallas_call | solution.py:112
  13.4 8.5 %gram.1 = (f32[4,1152,128]{2,1,0:T(8,128)}, f32[4,1152,128]{2,1,0:T(8,128)}) custom-call(s32[1]{0:T(128)} %bitcast.6.flip_ref, s32[2,1536]{1,0:T(2,128)} %leave_ref.4, bf16[1536,1024]{1,0:T(8,128)(2,1)} %rows_ref.11), custom_call_target="tpu_custom_call" | custom-call | flops 9889999872 | bytes 31734000 | tf_op jit(solution)/shard_map/gram/pallas_call | solution.py:218
  21.8 2.6 %collective-permute-done.arrived_ref = bf16[768,512]{1,0:T(8,128)(2,1)S(1)} collective-permute-done((bf16[768,512]{1,0:T(8,128)(2,1)}, bf16[768,512]{1,0:T(8,128)(2,1)S(1)}, u32[]{:S(2)}, u32[]{:S(2)}) %collective-permute-start) | collective-permute-done | bytes 786464 | tf_op jit(solution)/shard_map/ppermute | solution.py:396
  25.4 5.6 %swap.2 = (bf16[1536,512]{1,0:T(8,128)(2,1)}, bf16[768,512]{1,0:T(8,128)(2,1)}) custom-call(f32[24,1536]{1,0:T(8,128)} %get-tuple-element.57.row_ref, f32[2,1536,128]{2,1,0:T(8,128)} %get-tuple-element.58.col_ref, bf16[1536,1024]{1,0:T(8,128)(2,1)} %rows_ref.11, bf16[768,512]{1,0:T(8,128)(2,1)} %copy-done.5), custom_call_target="tpu_custom_call" | custom-call | flops 23000000512 | bytes 73800000 | tf_op jit(solution)/shard_map/swap/pallas_call | solution.py:142
  36.0 2.9 %collective-permute-start.3 = (f32[1152,128]{1,0:T(8,128)}, f32[1152,128]{1,0:T(8,128)}, u32[]{:S(2)}, u32[]{:S(2)}) collective-permute-start(f32[1152,128]{1,0:T(8,128)} %get-tuple-element.64), channel_id=1, source_target_pairs={{0,8},{1,9},{2,10},{3,11},{4,12},{5,13},{6,14},{7,15},{8,0},{9,1},... | collective-permute-start | bytes 1769480 | tf_op jit(solution)/shard_map/ppermute | solution.py:379
  40.2 2.9 %collective-permute-done.6.arrived_ref = bf16[768,512]{1,0:T(8,128)(2,1)S(1)} collective-permute-done((bf16[768,512]{1,0:T(8,128)(2,1)}, bf16[768,512]{1,0:T(8,128)(2,1)S(1)}, u32[]{:S(2)}, u32[]{:S(2)}) %collective-permute-start.6) | collective-permute-done | bytes 786464 | tf_op jit(solution)/shard_map/ppermute | solution.py:396
  44.0 5.4 %swap.3 = (bf16[1536,512]{1,0:T(8,128)(2,1)}, bf16[768,512]{1,0:T(8,128)(2,1)}) custom-call(f32[24,1536]{1,0:T(8,128)} %get-tuple-element.57.row_ref, f32[2,1536,128]{2,1,0:T(8,128)} %get-tuple-element.58.col_ref, bf16[1536,1024]{1,0:T(8,128)(2,1)} %rows_ref.11, bf16[768,512]{1,0:T(8,128)(2,1)} %copy-done.7), custom_call_target="tpu_custom_call" | custom-call | flops 6095000064 | bytes 19557000 | tf_op jit(solution)/shard_map/swap/pallas_call | solution.py:142
  52.2 9.8 %leaf_pack.2 = bf16[3072,512]{1,0:T(8,128)(2,1)} custom-call(f32[24,1536]{1,0:T(8,128)} %get-tuple-element.57.row_ref, f32[2,1536,128]{2,1,0:T(8,128)} %get-tuple-element.58.col_ref, bf16[1536,512]{1,0:T(8,128)(2,1)} %get-tuple-element.66.rows_ref.left_ref, bf16[768,512]{1,0:T(8,128)(2,1)} %copy-done.6), custom_call_target="tpu_custom_call" | custom-call | flops 11269999616 | bytes 36162000 | tf_op jit(solution)/shard_map/leaf_pack/pallas_call | solution.py:172
  62.1 7.5 %all-to-all-start = ((bf16[16,192,512]{2,1,0:T(8,128)(2,1)}), bf16[16,192,512]{2,1,0:T(8,128)(2,1)S(1)}, u32[]{:S(2)}, u32[]{:S(2)}) async-start(bf16[16,192,512]{2,1,0:T(8,128)(2,1)} %bitcast.33), calls=%async_computation | async-start | bytes 6291456 | tf_op jit(solution)/shard_map/all_to_all | solution.py:438
  71.6 3.8 %collective-permute-start.9 = (f32[288,128]{1,0:T(8,128)S(1)}, f32[288,128]{1,0:T(8,128)S(1)}, u32[]{:S(2)}, u32[]{:S(2)}) collective-permute-start(f32[288,128]{1,0:T(8,128)S(1)} %get-tuple-element.76), channel_id=1, source_target_pairs={{0,64},{16,80},{32,96},{48,112},{64,0},{80,16},{96,32},{112,48},{1... | collective-permute-start | bytes 442376 | tf_op jit(solution)/shard_map/ppermute | solution.py:383
  77.6 9.8 %leaf_pack.3 = bf16[3072,512]{1,0:T(8,128)(2,1)} custom-call(f32[24,1536]{1,0:T(8,128)} %get-tuple-element.57.row_ref, f32[2,1536,128]{2,1,0:T(8,128)} %get-tuple-element.58.col_ref, bf16[1536,512]{1,0:T(8,128)(2,1)} %get-tuple-element.78.rows_ref.right_ref, bf16[768,512]{1,0:T(8,128)(2,1)} %collective-permute-done.7.arrived_ref), custom_call_target="tpu_custom_call" | custom-call | flops 11269999616 | bytes 36162000 | tf_op jit(solution)/shard_map/leaf_pack/pallas_call | solution.py:172
  90.6 16.8 %all-to-all-done = bf16[16,192,512]{2,1,0:T(8,128)(2,1)S(1)} async-done(((bf16[16,192,512]{2,1,0:T(8,128)(2,1)}), bf16[16,192,512]{2,1,0:T(8,128)(2,1)S(1)}, u32[]{:S(2)}, u32[]{:S(2)}) %all-to-all-start) | async-done | bytes 3145760 | tf_op jit(solution)/shard_map/all_to_all | solution.py:438
  112.2 2.9 %collective-permute-done.14 = f32[288,128]{1,0:T(8,128)S(1)} collective-permute-done((f32[288,128]{1,0:T(8,128)}, f32[288,128]{1,0:T(8,128)S(1)}, u32[]{:S(2)}, u32[]{:S(2)}) %collective-permute-start.14) | collective-permute-done | bytes 147488 | tf_op jit(solution)/shard_map/ppermute | solution.py:392
  120.9 4.1 %collective-permute-done.15 = f32[288,128]{1,0:T(8,128)S(1)} collective-permute-done((f32[288,128]{1,0:T(8,128)S(1)}, f32[288,128]{1,0:T(8,128)S(1)}, u32[]{:S(2)}, u32[]{:S(2)}) %collective-permute-start.15) | collective-permute-done | bytes 147488 | tf_op jit(solution)/shard_map/ppermute | solution.py:379
  129.4 5.4 %all-to-all-start.1 = ((bf16[16,192,512]{2,1,0:T(8,128)(2,1)}), bf16[16,192,512]{2,1,0:T(8,128)(2,1)}, u32[]{:S(2)}, u32[]{:S(2)}) async-start(bf16[16,192,512]{2,1,0:T(8,128)(2,1)} %bitcast.34), calls=%async_computation.1 | async-start | bytes 6291456 | tf_op jit(solution)/shard_map/all_to_all | solution.py:458
  135.9 2.6 %collective-permute-start.18 = (f32[4,288,128]{2,1,0:T(8,128)S(1)}, f32[4,288,128]{2,1,0:T(8,128)S(1)}, u32[]{:S(2)}, u32[]{:S(2)}) collective-permute-start(f32[4,288,128]{2,1,0:T(8,128)S(1)} %pad_maximum_fusion.a_ref), channel_id=1, source_target_pairs={{0,96},{16,112},{32,0},{48,16},{64,32},{80,48},{96,64},{112,80},{1... | collective-permute-start | bytes 1769480 | tf_op jit(solution)/shard_map/ppermute | solution.py:383
  141.6 5.3 %join_first.1.held_ref = bf16[3072,1024]{1,0:T(8,128)(2,1)} custom-call(bf16[3072,512]{1,0:T(8,128)(2,1)} %bitcast.32), custom_call_target="tpu_custom_call" | custom-call | flops 5980000256 | bytes 19188000 | tf_op jit(solution)/shard_map/join_first/pallas_call | solution.py:352
  146.8 17.2 %collective-permute-done.18.b_ref = f32[4,288,128]{2,1,0:T(8,128)S(1)} collective-permute-done((f32[4,288,128]{2,1,0:T(8,128)S(1)}, f32[4,288,128]{2,1,0:T(8,128)S(1)}, u32[]{:S(2)}, u32[]{:S(2)}) %collective-permute-start.18) | collective-permute-done | bytes 589856 | tf_op jit(solution)/shard_map/ppermute | solution.py:383
  164.0 3.7 %collective-permute-done.20.d_ref = f32[4,288,128]{2,1,0:T(8,128)S(1)} collective-permute-done((f32[4,288,128]{2,1,0:T(8,128)S(1)}, f32[4,288,128]{2,1,0:T(8,128)S(1)}, u32[]{:S(2)}, u32[]{:S(2)}) %collective-permute-start.20) | collective-permute-done | bytes 589856 | tf_op jit(solution)/shard_map/ppermute | solution.py:383
  168.6 6.6 %power.1.mine_ref = f32[8,1024]{1,0:T(8,128)} custom-call(s32[2]{0:T(128)} %pad_add_fusion.place_ref, f32[1]{0:T(128)} %bitcast.3.members_ref, f32[1,1024]{1,0:T(1,128)} %bitcast.41, f32[4,288,128]{2,1,0:T(8,128)} %copy-done.2, f32[4,288,128]{2,1,0:T(8,128)} %copy-done.8, f32[4,288,128]{2,1,0:T(8,128)} %copy-done.9, f32[4,288,128]{2,1,0:T(8,128)} %copy-done.10), custom_call_target="tpu_custom_call" | custom-call | flops 7590000128 | bytes 24354000 | tf_op jit(solution)/shard_map/power/pallas_call | solution.py:286
  177.2 5.2 %scores.1 = f32[2,1536]{1,0:T(2,128)} custom-call(s32[1]{0:T(128)} %bitcast.core_ref, f32[8,1024]{1,0:T(8,128)} %power.1.mine_ref, f32[8,1024]{1,0:T(8,128)} %copy-done.11, bf16[1536,1024]{1,0:T(8,128)(2,1)} %rows_ref.11, bf16[1536,512]{1,0:T(8,128)(2,1)} %get-tuple-element.66.rows_ref.left_ref, bf16[1536,512]{1,0:T(8,128)(2,1)} %get-tuple-element.78.rows_ref.right_ref), custom_call_target="tpu_custom_call" | custom-call | flops 5980000256 | bytes 19188000 | tf_op jit(solution)/shard_map/scores/pallas_call | solution.py:329
  182.4 5.3 %join_second.1 = bf16[3072,1024]{1,0:T(8,128)(2,1)} custom-call(bf16[3072,512]{1,0:T(8,128)(2,1)} %bitcast.23.part_ref, bf16[3072,1024]{1,0:T(8,128)(2,1)} %join_first.1.held_ref), custom_call_target="tpu_custom_call", output_to_operand_aliasing={{}: (1, {})} | custom-call | flops 5980000256 | bytes 19188000 | tf_op jit(solution)/shard_map/join_second/pallas_call | solution.py:365
  (68 shorter events, 41.4 us)
Async XLA Ops:
  5.0 19.5 %collective-permute-start = (bf16[768,512]{1,0:T(8,128)(2,1)}, bf16[768,512]{1,0:T(8,128)(2,1)S(1)}, u32[]{:S(2)}, u32[]{:S(2)}) collective-permute-start(bf16[768,512]{1,0:T(8,128)(2,1)} %pack_first.2), channel_id=1, source_target_pairs={{0,16},{16,0},{32,48},{48,32},{64,80},{80,64},{96,112},{112,96},{1... | collective-permute-start | bytes 2359304 | tf_op jit(solution)/shard_map/ppermute | solution.py:396
  21.8 11.0 %collective-permute-start.1 = (f32[4,1152,128]{2,1,0:T(8,128)}, f32[4,1152,128]{2,1,0:T(8,128)S(1)}, u32[]{:S(2)}, u32[]{:S(2)}) collective-permute-start(f32[4,1152,128]{2,1,0:T(8,128)} %get-tuple-element.56), channel_id=1, source_target_pairs={{0,1},{1,0},{2,3},{3,2},{4,5},{5,4},{6,7},{7,6},{8,9},{9,8},{10,11... | collective-permute-start | bytes 7077896 | tf_op jit(solution)/shard_map/ppermute | solution.py:396
  24.5 18.6 %collective-permute-start.6 = (bf16[768,512]{1,0:T(8,128)(2,1)}, bf16[768,512]{1,0:T(8,128)(2,1)S(1)}, u32[]{:S(2)}, u32[]{:S(2)}) collective-permute-start(bf16[768,512]{1,0:T(8,128)(2,1)} %pack_first.3), channel_id=1, source_target_pairs={{0,16},{16,0},{32,48},{48,32},{64,80},{80,64},{96,112},{112,96},{1... | collective-permute-start | bytes 2359304 | tf_op jit(solution)/shard_map/ppermute | solution.py:396
  31.0 20.3 %collective-permute-start.5 = (bf16[768,512]{1,0:T(8,128)(2,1)}, bf16[768,512]{1,0:T(8,128)(2,1)S(1)}, u32[]{:S(2)}, u32[]{:S(2)}) collective-permute-start(bf16[768,512]{1,0:T(8,128)(2,1)} %get-tuple-element.60), channel_id=1, source_target_pairs={{0,32},{16,48},{32,0},{48,16},{64,96},{80,112},{96,64},{112,80},{1... | collective-permute-start | bytes 2359304 | tf_op jit(solution)/shard_map/ppermute | solution.py:396
  34.4 35.1 %collective-permute-start.2 = (f32[1152,128]{1,0:T(8,128)}, f32[1152,128]{1,0:T(8,128)}, u32[]{:S(2)}, u32[]{:S(2)}) collective-permute-start(f32[1152,128]{1,0:T(8,128)} %get-tuple-element.63), channel_id=1, source_target_pairs={{0,4},{1,5},{2,6},{3,7},{4,8},{5,9},{6,10},{7,11},{8,12},{9,13},{1... | collective-permute-start | bytes 1769480 | tf_op jit(solution)/shard_map/ppermute | solution.py:379
  36.0 33.5 %collective-permute-start.3 = (f32[1152,128]{1,0:T(8,128)}, f32[1152,128]{1,0:T(8,128)}, u32[]{:S(2)}, u32[]{:S(2)}) collective-permute-start(f32[1152,128]{1,0:T(8,128)} %get-tuple-element.64), channel_id=1, source_target_pairs={{0,8},{1,9},{2,10},{3,11},{4,12},{5,13},{6,14},{7,15},{8,0},{9,1},... | collective-permute-start | bytes 1769480 | tf_op jit(solution)/shard_map/ppermute | solution.py:379
  38.9 30.7 %collective-permute-start.4 = (f32[1152,128]{1,0:T(8,128)}, f32[1152,128]{1,0:T(8,128)}, u32[]{:S(2)}, u32[]{:S(2)}) collective-permute-start(f32[1152,128]{1,0:T(8,128)} %get-tuple-element.65), channel_id=1, source_target_pairs={{0,12},{1,13},{2,14},{3,15},{4,0},{5,1},{6,2},{7,3},{8,4},{9,5},{1... | collective-permute-start | bytes 1769480 | tf_op jit(solution)/shard_map/ppermute | solution.py:379
  49.4 20.2 %collective-permute-start.7 = (bf16[768,512]{1,0:T(8,128)(2,1)}, bf16[768,512]{1,0:T(8,128)(2,1)}, u32[]{:S(2)}, u32[]{:S(2)}) collective-permute-start(bf16[768,512]{1,0:T(8,128)(2,1)} %get-tuple-element.69), channel_id=1, source_target_pairs={{0,32},{16,48},{32,0},{48,16},{64,96},{80,112},{96,64},{112,80},{1... | collective-permute-start | bytes 2359304 | tf_op jit(solution)/shard_map/ppermute | solution.py:396
  62.1 45.3 %all-to-all-start = ((bf16[16,192,512]{2,1,0:T(8,128)(2,1)}), bf16[16,192,512]{2,1,0:T(8,128)(2,1)S(1)}, u32[]{:S(2)}, u32[]{:S(2)}) async-start(bf16[16,192,512]{2,1,0:T(8,128)(2,1)} %bitcast.33), calls=%async_computation | async-start | bytes 6291456 | tf_op jit(solution)/shard_map/all_to_all | solution.py:438
  71.3 16.1 %collective-permute-start.8 = (f32[288,128]{1,0:T(8,128)S(1)}, f32[288,128]{1,0:T(8,128)S(1)}, u32[]{:S(2)}, u32[]{:S(2)}) collective-permute-start(f32[288,128]{1,0:T(8,128)S(1)} %get-tuple-element.75), channel_id=1, source_target_pairs={{0,32},{16,48},{32,64},{48,80},{64,96},{80,112},{96,0},{112,16},{1... | collective-permute-start | bytes 442376 | tf_op jit(solution)/shard_map/ppermute | solution.py:383
  71.6 15.8 %collective-permute-start.9 = (f32[288,128]{1,0:T(8,128)S(1)}, f32[288,128]{1,0:T(8,128)S(1)}, u32[]{:S(2)}, u32[]{:S(2)}) collective-permute-start(f32[288,128]{1,0:T(8,128)S(1)} %get-tuple-element.76), channel_id=1, source_target_pairs={{0,64},{16,80},{32,96},{48,112},{64,0},{80,16},{96,32},{112,48},{1... | collective-permute-start | bytes 442376 | tf_op jit(solution)/shard_map/ppermute | solution.py:383
  75.4 12.0 %collective-permute-start.10 = (f32[288,128]{1,0:T(8,128)S(1)}, f32[288,128]{1,0:T(8,128)S(1)}, u32[]{:S(2)}, u32[]{:S(2)}) collective-permute-start(f32[288,128]{1,0:T(8,128)S(1)} %get-tuple-element.77), channel_id=1, source_target_pairs={{0,96},{16,112},{32,0},{48,16},{64,32},{80,48},{96,64},{112,80},{1... | collective-permute-start | bytes 442376 | tf_op jit(solution)/shard_map/ppermute | solution.py:383
  87.4 1.6 collective-permute-start.11
  107.4 7.7 %collective-permute-start.14 = (f32[288,128]{1,0:T(8,128)}, f32[288,128]{1,0:T(8,128)S(1)}, u32[]{:S(2)}, u32[]{:S(2)}) collective-permute-start(f32[288,128]{1,0:T(8,128)} %get-tuple-element.85), channel_id=1, source_target_pairs={{0,18},{1,19},{2,16},{3,17},{4,22},{5,23},{6,20},{7,21},{8,26},{9,... | collective-permute-start | bytes 442376 | tf_op jit(solution)/shard_map/ppermute | solution.py:392
  108.2 9.0 %collective-permute-start.13 = (f32[288,128]{1,0:T(8,128)}, f32[288,128]{1,0:T(8,128)S(1)}, u32[]{:S(2)}, u32[]{:S(2)}) collective-permute-start(f32[288,128]{1,0:T(8,128)} %get-tuple-element.85), channel_id=1, source_target_pairs={{0,16},{1,17},{2,18},{3,19},{4,20},{5,21},{6,22},{7,23},{8,24},{9,... | collective-permute-start | bytes 442376 | tf_op jit(solution)/shard_map/ppermute | solution.py:392
  110.6 7.7 %collective-permute-start.12 = (f32[288,128]{1,0:T(8,128)S(1)}, f32[288,128]{1,0:T(8,128)S(1)}, u32[]{:S(2)}, u32[]{:S(2)}) collective-permute-start(f32[288,128]{1,0:T(8,128)S(1)} %get-tuple-element.84), channel_id=1, source_target_pairs={{0,2},{1,3},{2,0},{3,1},{4,6},{5,7},{6,4},{7,5},{8,10},{9,11},{10,... | collective-permute-start | bytes 442376 | tf_op jit(solution)/shard_map/ppermute | solution.py:392
  118.4 6.6 %collective-permute-start.15 = (f32[288,128]{1,0:T(8,128)S(1)}, f32[288,128]{1,0:T(8,128)S(1)}, u32[]{:S(2)}, u32[]{:S(2)}) collective-permute-start(f32[288,128]{1,0:T(8,128)S(1)} %add_add_fusion.1), channel_id=1, source_target_pairs={{0,12},{1,13},{2,14},{3,15},{4,0},{5,1},{6,2},{7,3},{8,4},{9,5},{1... | collective-permute-start | bytes 442376 | tf_op jit(solution)/shard_map/ppermute | solution.py:379
  119.9 7.3 %collective-permute-start.16 = (f32[288,128]{1,0:T(8,128)S(1)}, f32[288,128]{1,0:T(8,128)S(1)}, u32[]{:S(2)}, u32[]{:S(2)}) collective-permute-start(f32[288,128]{1,0:T(8,128)S(1)} %add_add_fusion.1), channel_id=1, source_target_pairs={{0,8},{1,9},{2,10},{3,11},{4,12},{5,13},{6,14},{7,15},{8,0},{9,1},... | collective-permute-start | bytes 442376 | tf_op jit(solution)/shard_map/ppermute | solution.py:379
  120.8 8.0 %collective-permute-start.17 = (f32[288,128]{1,0:T(8,128)S(1)}, f32[288,128]{1,0:T(8,128)S(1)}, u32[]{:S(2)}, u32[]{:S(2)}) collective-permute-start(f32[288,128]{1,0:T(8,128)S(1)} %add_add_fusion.1), channel_id=1, source_target_pairs={{0,4},{1,5},{2,6},{3,7},{4,8},{5,9},{6,10},{7,11},{8,12},{9,13},{1... | collective-permute-start | bytes 442376 | tf_op jit(solution)/shard_map/ppermute | solution.py:379
  129.4 53.0 %all-to-all-start.1 = ((bf16[16,192,512]{2,1,0:T(8,128)(2,1)}), bf16[16,192,512]{2,1,0:T(8,128)(2,1)}, u32[]{:S(2)}, u32[]{:S(2)}) async-start(bf16[16,192,512]{2,1,0:T(8,128)(2,1)} %bitcast.34), calls=%async_computation.1 | async-start | bytes 6291456 | tf_op jit(solution)/shard_map/all_to_all | solution.py:458
  135.9 28.2 %collective-permute-start.18 = (f32[4,288,128]{2,1,0:T(8,128)S(1)}, f32[4,288,128]{2,1,0:T(8,128)S(1)}, u32[]{:S(2)}, u32[]{:S(2)}) collective-permute-start(f32[4,288,128]{2,1,0:T(8,128)S(1)} %pad_maximum_fusion.a_ref), channel_id=1, source_target_pairs={{0,96},{16,112},{32,0},{48,16},{64,32},{80,48},{96,64},{112,80},{1... | collective-permute-start | bytes 1769480 | tf_op jit(solution)/shard_map/ppermute | solution.py:383
  138.4 25.6 %collective-permute-start.19 = (f32[4,288,128]{2,1,0:T(8,128)S(1)}, f32[4,288,128]{2,1,0:T(8,128)S(1)}, u32[]{:S(2)}, u32[]{:S(2)}) collective-permute-start(f32[4,288,128]{2,1,0:T(8,128)S(1)} %pad_maximum_fusion.a_ref), channel_id=1, source_target_pairs={{0,64},{16,80},{32,96},{48,112},{64,0},{80,16},{96,32},{112,48},{1... | collective-permute-start | bytes 1769480 | tf_op jit(solution)/shard_map/ppermute | solution.py:383
  139.6 28.1 %collective-permute-start.20 = (f32[4,288,128]{2,1,0:T(8,128)S(1)}, f32[4,288,128]{2,1,0:T(8,128)S(1)}, u32[]{:S(2)}, u32[]{:S(2)}) collective-permute-start(f32[4,288,128]{2,1,0:T(8,128)S(1)} %pad_maximum_fusion.a_ref), channel_id=1, source_target_pairs={{0,32},{16,48},{32,64},{48,80},{64,96},{80,112},{96,0},{112,16},{1... | collective-permute-start | bytes 1769480 | tf_op jit(solution)/shard_map/ppermute | solution.py:383
  175.2 1.4 collective-permute-start.21
  (12 other events, 54.3 us)

commit v3 on v2

--- a/solution.py
+++ b/solution.py
@@ -317,24 +317,27 @@
     return total[0:1, :] + total[1:2, :] + total[2:3, :]
 
 
-def scores_kernel(core_ref, mine_ref, other_ref, rows_ref, left_ref, right_ref, out_ref):
-    first = core_ref[0] == 0
-    top = jnp.where(first, mine_ref[...], other_ref[...])
-    low = jnp.where(first, other_ref[...], mine_ref[...])
+def scores_kernel(flags_ref, own_ref, core_ref, z_ref, both_ref, rows_ref, left_ref, right_ref, out_ref):
+    worker = flags_ref[0] == flags_ref[1]
+    same = jnp.where(worker, own_ref[...], core_ref[...])
+    unlike = jnp.where(worker, both_ref[...], z_ref[...])
+    even = flags_ref[1] == 0
+    top = jnp.where(even, same, unlike)
+    low = jnp.where(even, unlike, same)
     out_ref[0:1, :] = project(top[0:1, :], [rows_ref[...]]) - top[1:2, 0:1]
     out_ref[1:2, :] = project(low[0:1, :], [left_ref[...], right_ref[...]]) - low[1:2, 0:1]
 
 
-def all_scores(core, mine, other, rows, left, right):
+def all_scores(flags, found, rows, left, right):
     return pl.pallas_call(
         scores_kernel,
-        in_specs=[SMEM] + [VMEM] * 5,
+        in_specs=[SMEM] + [VMEM] * 7,
         out_specs=VMEM,
         out_shape=shape_of((2, ROWS), F32),
         compiler_params=PARAMS,
         cost_estimate=cost(5.2),
         name="scores",
-    )(core, mine, other, rows, left, right)
+    )(flags, *found, rows, left, right)
 
 
 def join_first_kernel(part_ref, out_ref):
@@ -345,7 +348,7 @@
     out_ref[...] = part_ref[...]
 
 
-JOIN = 512
+JOIN = 1024
 
 
 def join_first(left):
@@ -394,6 +397,23 @@
 
 def across(value, axis, bit):
     return lax.ppermute(value, axis, [(i, i ^ bit) for i in range(lax.axis_size(axis))])
+
+
+def device(z, x_lo, y, x_hi, core):
+    return (z * 2 + x_lo) * N_BLK + y * 4 + x_hi * 2 + core
+
+
+PLACES = [(z, x_lo, y, x_hi, c) for z in range(4) for x_lo in (0, 1) for y in range(4) for x_hi in (0, 1) for c in (0, 1)]
+
+
+def to_worker(value, k):
+    pairs = [(device((p[0] + k) % 4, *p[1:]), device(*p)) for p in PLACES if p[0] % 2 == p[4]]
+    return lax.ppermute(value, ("cube", "blk"), pairs)
+
+
+def from_worker(value, dz, dc):
+    pairs = [(device(*p), device(p[0] ^ dz, *p[1:4], p[4] ^ dc)) for p in PLACES if p[0] % 2 == p[4]]
+    return lax.ppermute(value, ("cube", "blk"), pairs)
 
 
 def after(value, earlier):
@@ -451,21 +471,21 @@
     both = own + other
     mine = jnp.where(core == 0, both, jnp.where(x_lo == 0, own, other))
     theirs = jnp.where(core == 0, both, jnp.where(x_lo == 0, other, own))
-    mine, theirs, out_l = lax.optimization_barrier((mine, theirs, out_l))
     piece = mine + along_x(mine, 2) + along_x(theirs, 1) + along_x(theirs, 3)
-    near = [along_y(piece, -k) for k in (1, 2, 3)]
-    near, leaf_r, out_l = lax.optimization_barrier((near, leaf_r, out_l))
+    near = [along_y(piece, -k) for k in (2, 1, 3)]
+    leaf_r, near, out_l = lax.optimization_barrier((leaf_r, near, out_l))
     out_r = lax.all_to_all(leaf_r, "blk", split_axis=0, concat_axis=0, tiled=True)
-    stack = jnp.stack([piece] + near)
-    gathered = [stack] + [along_z(stack, -k) for k in (1, 2, 3)]
+    stack = jnp.stack([piece, near[1], near[0], near[2]])
+    gathered = [stack] + [to_worker(stack, k) for k in (1, 2, 3)]
     held = join_first(after(out_l, stack))
     held, gathered = lax.optimization_barrier((held, gathered))
 
     place = jnp.stack([y, z]).astype(jnp.int32)
     members = jnp.where(core == 0, ROWS * N_BLK * N_CUBE, ROWS * N_BLK * N_CUBE // 2).astype(F32).reshape(1)
-    mine = power(place, members, start_vec.reshape(1, D), gathered)
-    theirs = across(mine, "blk", 1)
-    scores = all_scores(core.astype(jnp.int32).reshape(1), mine, theirs, rows, next_l, next_r)
+    found = power(place, members, start_vec.reshape(1, D), gathered)
+    found = [found] + [from_worker(found, dz, dc) for dz, dc in ((0, 1), (1, 0), (1, 1))]
+    flags = jnp.stack([core, z % 2]).astype(jnp.int32)
+    scores = all_scores(flags, found, rows, next_l, next_r)
     return scores, join_second(out_r, held)
 
 

time: 190 us -> 182 us (0.958)
  waiting for transfers between devices: 59.9 us -> 44.4 us
  starting transfers between devices: 43.1 us -> 53.3 us
    ppermute x6 -> x3, waiting for transfers between devices: 20.8 us -> 0.01 us  [along_z(): lax.ppermute(value, 'cube', [(i, (i // 2 + k) % 4 * 2 + i % 2) for i in r...]
    all_to_all x1, waiting for transfers between devices: 16.8 us -> 0.01 us  [per_device(): lax.all_to_all(leaf_l, 'blk', split_axis=0, concat_axis=0, tiled=True)]
    ppermute x3, waiting for transfers between devices: 6.08 us -> 20.3 us  [along_x(): return lax.ppermute(value, ('cube', 'blk'), pairs)]
    ppermute x0 -> x6, starting transfers between devices: none -> 12.9 us  [the longest x3 8.35 us: to_worker(): return lax.ppermute(value, ('cube', 'blk'), pairs)]
    ppermute x0 -> x6, waiting for transfers between devices: none -> 12.2 us  [the longest x3 9.44 us: to_worker(): return lax.ppermute(value, ('cube', 'blk'), pairs)]
    ppermute x6 -> x3, starting transfers between devices: 11.3 us -> 6.28 us  [along_z(): lax.ppermute(value, 'cube', [(i, (i // 2 + k) % 4 * 2 + i % 2) for i in r...]
    ppermute x6, waiting for transfers between devices: 7.87 us -> 5 us  [along_y(): lax.ppermute(value, 'blk', [(i, (i // 4 + k) % 4 * 4 + i % 4) for i in ra...]
    ppermute x6, starting transfers between devices: 8.36 us -> 10.7 us  [along_y(): lax.ppermute(value, 'blk', [(i, (i // 4 + k) % 4 * 4 + i % 4) for i in ra...]
  transfers between devices with their start and end apart: 24 -> 26, of which waited for: 13 -> 13; matrix products, arithmetic and copies ran while one was open for 4% -> 3% of each run, Pallas kernels for 34% -> 35%
where the time goes in v3:
time: 182 us; the launch traced here: 181 us
  Pallas kernels  71.6 us (39%)
  starting transfers between devices  53.3 us (29%)
  waiting for transfers between devices  44.4 us (24%)
  local copies, waits for them, and re-layouts  5.78 us (3%)
  other arithmetic  5.56 us (3%)
    ppermute x3, waiting for transfers between devices, along_x(): return lax.ppermute(value, ('cube', 'blk'), pairs)  20.3 us
    pallas_call x2, Pallas kernels, leaf_pack(): pl.pallas_call(leaf_kernel, grid=(1,), in_specs=[whole((24, ROWS)), pl.Bl...  19.6 us
    pallas_call x2, Pallas kernels, swap(): pl.pallas_call(swap_kernel, grid=(1,), in_specs=[whole((24, ROWS)), whole...  11 us
    ppermute x6, starting transfers between devices, along_y(): lax.ppermute(value, 'blk', [(i, (i // 4 + k) % 4 * 4 + i % 4) for i in ra...  10.7 us
    ppermute x3, waiting for transfers between devices, to_worker(): return lax.ppermute(value, ('cube', 'blk'), pairs)  9.44 us
    pallas_call x2, Pallas kernels, pack_first(): pl.pallas_call(pack_first_kernel, grid=(1,), in_specs=[pl.BlockSpec((2, R...  8.69 us
    pallas_call x1, Pallas kernels, gram(): pl.pallas_call(gram_kernel, in_specs=[SMEM, VMEM, VMEM], out_specs=[VMEM,...  8.49 us
    ppermute x3, starting transfers between devices, to_worker(): return lax.ppermute(value, ('cube', 'blk'), pairs)  8.35 us
  transfers between devices with their start and end apart: 26, of which 13 were waited for; matrix products, arithmetic and copies ran while one was open for 3% of the time, Pallas kernels for 35%

profile of v3, /device:TPU:6, one launch (start us, length us, event | category | flops | bytes accessed | tf_op | source)
XLA Modules:
  0.0 181.4 jit_solution(5962302832006093083)
XLA Ops:
  0.6 4.4 %pack_first.2 = bf16[768,512]{1,0:T(8,128)(2,1)} custom-call(s32[2,1536]{1,0:T(2,128)} %leave_ref.4, bf16[1536,1024]{1,0:T(8,128)(2,1)} %rows_ref.11), custom_call_target="tpu_custom_call" | custom-call | flops 4944999936 | bytes 15867000 | tf_op jit(solution)/shard_map/pack_first/pallas_call | solution.py:88
  5.8 4.3 %pack_first.3 = bf16[768,512]{1,0:T(8,128)(2,1)} custom-call(s32[2,1536]{1,0:T(2,128)} %leave_ref.4, bf16[1536,1024]{1,0:T(8,128)(2,1)} %rows_ref.11), custom_call_target="tpu_custom_call" | custom-call | flops 4944999936 | bytes 15867000 | tf_op jit(solution)/shard_map/pack_first/pallas_call | solution.py:88
  10.1 3.2 %slots.1 = (f32[24,1536]{1,0:T(8,128)}, f32[2,1536,128]{2,1,0:T(8,128)}) custom-call(s32[2,1536]{1,0:T(2,128)} %leave_ref.4, s32[1,1536]{1,0:T(1,128)} %bitcast.40), custom_call_target="tpu_custom_call" | custom-call | flops 3680000000 | bytes 11808000 | tf_op jit(solution)/shard_map/slots/pallas_call | solution.py:112
  13.3 8.5 %gram.1 = (f32[4,1152,128]{2,1,0:T(8,128)}, f32[4,1152,128]{2,1,0:T(8,128)}) custom-call(s32[1]{0:T(128)} %bitcast.7.flip_ref, s32[2,1536]{1,0:T(2,128)} %leave_ref.4, bf16[1536,1024]{1,0:T(8,128)(2,1)} %rows_ref.11), custom_call_target="tpu_custom_call" | custom-call | flops 9889999872 | bytes 31734000 | tf_op jit(solution)/shard_map/gram/pallas_call | solution.py:218
  25.4 5.6 %swap.2 = (bf16[1536,512]{1,0:T(8,128)(2,1)}, bf16[768,512]{1,0:T(8,128)(2,1)}) custom-call(f32[24,1536]{1,0:T(8,128)} %get-tuple-element.49.row_ref, f32[2,1536,128]{2,1,0:T(8,128)} %get-tuple-element.50.col_ref, bf16[1536,1024]{1,0:T(8,128)(2,1)} %rows_ref.11, bf16[768,512]{1,0:T(8,128)(2,1)} %copy-done.4), custom_call_target="tpu_custom_call" | custom-call | flops 23000000512 | bytes 73800000 | tf_op jit(solution)/shard_map/swap/pallas_call | solution.py:142
  36.0 2.9 %collective-permute-start.4 = (f32[1152,128]{1,0:T(8,128)}, f32[1152,128]{1,0:T(8,128)}, u32[]{:S(2)}, u32[]{:S(2)}) collective-permute-start(f32[1152,128]{1,0:T(8,128)} %get-tuple-element.62), channel_id=1, source_target_pairs={{0,8},{1,9},{2,10},{3,11},{4,12},{5,13},{6,14},{7,15},{8,0},{9,1},... | collective-permute-start | bytes 1769480 | tf_op jit(solution)/shard_map/ppermute | solution.py:382
  40.3 2.9 %collective-permute-done.1.arrived_ref = bf16[768,512]{1,0:T(8,128)(2,1)S(1)} collective-permute-done((bf16[768,512]{1,0:T(8,128)(2,1)}, bf16[768,512]{1,0:T(8,128)(2,1)S(1)}, u32[]{:S(2)}, u32[]{:S(2)}) %collective-permute-start.1) | collective-permute-done | bytes 786464 | tf_op jit(solution)/shard_map/ppermute | solution.py:399
  44.0 5.4 %swap.3 = (bf16[1536,512]{1,0:T(8,128)(2,1)}, bf16[768,512]{1,0:T(8,128)(2,1)}) custom-call(f32[24,1536]{1,0:T(8,128)} %get-tuple-element.49.row_ref, f32[2,1536,128]{2,1,0:T(8,128)} %get-tuple-element.50.col_ref, bf16[1536,1024]{1,0:T(8,128)(2,1)} %rows_ref.11, bf16[768,512]{1,0:T(8,128)(2,1)} %copy-done.6), custom_call_target="tpu_custom_call" | custom-call | flops 6095000064 | bytes 19557000 | tf_op jit(solution)/shard_map/swap/pallas_call | solution.py:142
  52.3 9.8 %leaf_pack.2 = bf16[3072,512]{1,0:T(8,128)(2,1)} custom-call(f32[24,1536]{1,0:T(8,128)} %get-tuple-element.49.row_ref, f32[2,1536,128]{2,1,0:T(8,128)} %get-tuple-element.50.col_ref, bf16[1536,512]{1,0:T(8,128)(2,1)} %get-tuple-element.66.rows_ref.left_ref, bf16[768,512]{1,0:T(8,128)(2,1)} %copy-done.5), custom_call_target="tpu_custom_call" | custom-call | flops 11269999616 | bytes 36162000 | tf_op jit(solution)/shard_map/leaf_pack/pallas_call | solution.py:172
  62.1 7.5 %all-to-all-start = ((bf16[16,192,512]{2,1,0:T(8,128)(2,1)}), bf16[16,192,512]{2,1,0:T(8,128)(2,1)S(1)}, u32[]{:S(2)}, u32[]{:S(2)}) async-start(bf16[16,192,512]{2,1,0:T(8,128)(2,1)} %bitcast.34), calls=%async_computation | async-start | bytes 6291456 | tf_op jit(solution)/shard_map/all_to_all | solution.py:458
  71.6 3.8 %collective-permute-start.9 = (f32[288,128]{1,0:T(8,128)S(1)}, f32[288,128]{1,0:T(8,128)S(1)}, u32[]{:S(2)}, u32[]{:S(2)}) collective-permute-start(f32[288,128]{1,0:T(8,128)S(1)} %get-tuple-element.75), channel_id=1, source_target_pairs={{0,64},{16,80},{32,96},{48,112},{64,0},{80,16},{96,32},{112,48},{1... | collective-permute-start | bytes 442376 | tf_op jit(solution)/shard_map/ppermute | solution.py:386
  77.6 9.8 %leaf_pack.3 = bf16[3072,512]{1,0:T(8,128)(2,1)} custom-call(f32[24,1536]{1,0:T(8,128)} %get-tuple-element.49.row_ref, f32[2,1536,128]{2,1,0:T(8,128)} %get-tuple-element.50.col_ref, bf16[1536,512]{1,0:T(8,128)(2,1)} %get-tuple-element.65.rows_ref.right_ref, bf16[768,512]{1,0:T(8,128)(2,1)} %collective-permute-done.7.arrived_ref), custom_call_target="tpu_custom_call" | custom-call | flops 11269999616 | bytes 36162000 | tf_op jit(solution)/shard_map/leaf_pack/pallas_call | solution.py:172
  92.2 17.0 %collective-permute-done.14 = f32[288,128]{1,0:T(8,128)S(1)} collective-permute-done((f32[288,128]{1,0:T(8,128)S(1)}, f32[288,128]{1,0:T(8,128)S(1)}, u32[]{:S(2)}, u32[]{:S(2)}) %collective-permute-start.14) | collective-permute-done | bytes 147488 | tf_op jit(solution)/shard_map/ppermute | solution.py:395
  112.5 2.8 %collective-permute-start.15 = (f32[288,128]{1,0:T(8,128)S(1)}, f32[288,128]{1,0:T(8,128)S(1)}, u32[]{:S(2)}, u32[]{:S(2)}) collective-permute-start(f32[288,128]{1,0:T(8,128)S(1)} %add_add_fusion.1), channel_id=1, source_target_pairs={{0,8},{1,9},{2,10},{3,11},{4,12},{5,13},{6,14},{7,15},{8,0},{9,1},... | collective-permute-start | bytes 442376 | tf_op jit(solution)/shard_map/ppermute | solution.py:382
  117.4 3.4 %collective-permute-done.15 = f32[288,128]{1,0:T(8,128)S(1)} collective-permute-done((f32[288,128]{1,0:T(8,128)S(1)}, f32[288,128]{1,0:T(8,128)S(1)}, u32[]{:S(2)}, u32[]{:S(2)}) %collective-permute-start.15) | collective-permute-done | bytes 147488 | tf_op jit(solution)/shard_map/ppermute | solution.py:382
  124.8 7.1 %all-to-all-start.1 = ((bf16[16,192,512]{2,1,0:T(8,128)(2,1)}), bf16[16,192,512]{2,1,0:T(8,128)(2,1)}, u32[]{:S(2)}, u32[]{:S(2)}) async-start(bf16[16,192,512]{2,1,0:T(8,128)(2,1)} %bitcast.35), calls=%async_computation.1 | async-start | bytes 6291456 | tf_op jit(solution)/shard_map/all_to_all | solution.py:477
  134.2 5.5 %collective-permute-start.19 = (f32[4,288,128]{2,1,0:T(8,128)S(1)}, f32[4,288,128]{2,1,0:T(8,128)S(1)}, u32[]{:S(2)}, u32[]{:S(2)}) collective-permute-start(f32[4,288,128]{2,1,0:T(8,128)S(1)} %pad_maximum_fusion.a_ref), channel_id=1, source_target_pairs={{64,0},{66,2},{68,4},{70,6},{72,8},{74,10},{76,12},{78,14},{80,16}... | collective-permute-start | bytes 1769480 | tf_op jit(solution)/shard_map/ppermute | solution.py:411
  141.8 4.4 %join_first.1.held_ref = bf16[3072,1024]{1,0:T(8,128)(2,1)} custom-call(bf16[3072,512]{1,0:T(8,128)(2,1)} %bitcast.33), custom_call_target="tpu_custom_call" | custom-call | flops 5980000256 | bytes 19188000 | tf_op jit(solution)/shard_map/join_first/pallas_call | solution.py:355
  146.2 2.8 %collective-permute-done.18.b_ref = f32[4,288,128]{2,1,0:T(8,128)S(1)} collective-permute-done((f32[4,288,128]{2,1,0:T(8,128)S(1)}, f32[4,288,128]{2,1,0:T(8,128)S(1)}, u32[]{:S(2)}, u32[]{:S(2)}) %collective-permute-start.18) | collective-permute-done | bytes 589856 | tf_op jit(solution)/shard_map/ppermute | solution.py:411
  149.1 3.8 %collective-permute-done.19.c_ref = f32[4,288,128]{2,1,0:T(8,128)S(1)} collective-permute-done((f32[4,288,128]{2,1,0:T(8,128)S(1)}, f32[4,288,128]{2,1,0:T(8,128)S(1)}, u32[]{:S(2)}, u32[]{:S(2)}) %collective-permute-start.19) | collective-permute-done | bytes 589856 | tf_op jit(solution)/shard_map/ppermute | solution.py:411
  152.8 2.8 %collective-permute-done.20.d_ref = f32[4,288,128]{2,1,0:T(8,128)S(1)} collective-permute-done((f32[4,288,128]{2,1,0:T(8,128)S(1)}, f32[4,288,128]{2,1,0:T(8,128)S(1)}, u32[]{:S(2)}, u32[]{:S(2)}) %collective-permute-start.20) | collective-permute-done | bytes 589856 | tf_op jit(solution)/shard_map/ppermute | solution.py:411
  156.5 6.6 %power.1.own_ref = f32[8,1024]{1,0:T(8,128)} custom-call(s32[2]{0:T(128)} %pad_add_fusion.1.place_ref, f32[1]{0:T(128)} %bitcast.4.members_ref, f32[1,1024]{1,0:T(1,128)} %bitcast.41, f32[4,288,128]{2,1,0:T(8,128)} %copy-done.2, f32[4,288,128]{2,1,0:T(8,128)} %copy-done.7, f32[4,288,128]{2,1,0:T(8,128)} %copy-done.8, f32[4,288,128]{2,1,0:T(8,128)} %copy-done.9), custom_call_target="tpu_custom_call" | custom-call | flops 7590000128 | bytes 24354000 | tf_op jit(solution)/shard_map/power/pallas_call | solution.py:286
  171.8 5.3 %scores.1 = f32[2,1536]{1,0:T(2,128)} custom-call(s32[2]{0:T(128)} %pad_add_fusion.flags_ref, f32[8,1024]{1,0:T(8,128)} %power.1.own_ref, f32[8,1024]{1,0:T(8,128)} %copy-done.10, f32[8,1024]{1,0:T(8,128)} %copy-done.11, f32[8,1024]{1,0:T(8,128)} %copy-done.12, bf16[1536,1024]{1,0:T(8,128)(2,1)} %rows_ref.11, ...), custom_call_target="tpu_custom_call" | custom-call | flops 5980000256 | bytes 19188000 | tf_op jit(solution)/shard_map/scores/pallas_call | solution.py:332
  177.1 4.4 %join_second.1 = bf16[3072,1024]{1,0:T(8,128)(2,1)} custom-call(bf16[3072,512]{1,0:T(8,128)(2,1)} %bitcast.24.part_ref, bf16[3072,1024]{1,0:T(8,128)(2,1)} %join_first.1.held_ref), custom_call_target="tpu_custom_call", output_to_operand_aliasing={{}: (1, {})} | custom-call | flops 5980000256 | bytes 19188000 | tf_op jit(solution)/shard_map/join_second/pallas_call | solution.py:368
  (75 shorter events, 46.7 us)
Async XLA Ops:
  5.0 19.5 %collective-permute-start = (bf16[768,512]{1,0:T(8,128)(2,1)}, bf16[768,512]{1,0:T(8,128)(2,1)S(1)}, u32[]{:S(2)}, u32[]{:S(2)}) collective-permute-start(bf16[768,512]{1,0:T(8,128)(2,1)} %pack_first.2), channel_id=1, source_target_pairs={{0,16},{16,0},{32,48},{48,32},{64,80},{80,64},{96,112},{112,96},{1... | collective-permute-start | bytes 2359304 | tf_op jit(solution)/shard_map/ppermute | solution.py:399
  21.8 11.1 %collective-permute-start.2 = (f32[4,1152,128]{2,1,0:T(8,128)}, f32[4,1152,128]{2,1,0:T(8,128)S(1)}, u32[]{:S(2)}, u32[]{:S(2)}) collective-permute-start(f32[4,1152,128]{2,1,0:T(8,128)} %get-tuple-element.56), channel_id=1, source_target_pairs={{0,1},{1,0},{2,3},{3,2},{4,5},{5,4},{6,7},{7,6},{8,9},{9,8},{10,11... | collective-permute-start | bytes 7077896 | tf_op jit(solution)/shard_map/ppermute | solution.py:399
  24.5 18.6 %collective-permute-start.1 = (bf16[768,512]{1,0:T(8,128)(2,1)}, bf16[768,512]{1,0:T(8,128)(2,1)S(1)}, u32[]{:S(2)}, u32[]{:S(2)}) collective-permute-start(bf16[768,512]{1,0:T(8,128)(2,1)} %pack_first.3), channel_id=1, source_target_pairs={{0,16},{16,0},{32,48},{48,32},{64,80},{80,64},{96,112},{112,96},{1... | collective-permute-start | bytes 2359304 | tf_op jit(solution)/shard_map/ppermute | solution.py:399
  31.0 20.3 %collective-permute-start.6 = (bf16[768,512]{1,0:T(8,128)(2,1)}, bf16[768,512]{1,0:T(8,128)(2,1)S(1)}, u32[]{:S(2)}, u32[]{:S(2)}) collective-permute-start(bf16[768,512]{1,0:T(8,128)(2,1)} %get-tuple-element.58), channel_id=1, source_target_pairs={{0,32},{16,48},{32,0},{48,16},{64,96},{80,112},{96,64},{112,80},{1... | collective-permute-start | bytes 2359304 | tf_op jit(solution)/shard_map/ppermute | solution.py:399
  34.4 35.1 %collective-permute-start.3 = (f32[1152,128]{1,0:T(8,128)}, f32[1152,128]{1,0:T(8,128)}, u32[]{:S(2)}, u32[]{:S(2)}) collective-permute-start(f32[1152,128]{1,0:T(8,128)} %get-tuple-element.61), channel_id=1, source_target_pairs={{0,4},{1,5},{2,6},{3,7},{4,8},{5,9},{6,10},{7,11},{8,12},{9,13},{1... | collective-permute-start | bytes 1769480 | tf_op jit(solution)/shard_map/ppermute | solution.py:382
  36.0 33.5 %collective-permute-start.4 = (f32[1152,128]{1,0:T(8,128)}, f32[1152,128]{1,0:T(8,128)}, u32[]{:S(2)}, u32[]{:S(2)}) collective-permute-start(f32[1152,128]{1,0:T(8,128)} %get-tuple-element.62), channel_id=1, source_target_pairs={{0,8},{1,9},{2,10},{3,11},{4,12},{5,13},{6,14},{7,15},{8,0},{9,1},... | collective-permute-start | bytes 1769480 | tf_op jit(solution)/shard_map/ppermute | solution.py:382
  38.9 30.6 %collective-permute-start.5 = (f32[1152,128]{1,0:T(8,128)}, f32[1152,128]{1,0:T(8,128)}, u32[]{:S(2)}, u32[]{:S(2)}) collective-permute-start(f32[1152,128]{1,0:T(8,128)} %get-tuple-element.63), channel_id=1, source_target_pairs={{0,12},{1,13},{2,14},{3,15},{4,0},{5,1},{6,2},{7,3},{8,4},{9,5},{1... | collective-permute-start | bytes 1769480 | tf_op jit(solution)/shard_map/ppermute | solution.py:382
  49.4 20.2 %collective-permute-start.7 = (bf16[768,512]{1,0:T(8,128)(2,1)}, bf16[768,512]{1,0:T(8,128)(2,1)}, u32[]{:S(2)}, u32[]{:S(2)}) collective-permute-start(bf16[768,512]{1,0:T(8,128)(2,1)} %get-tuple-element.67), channel_id=1, source_target_pairs={{0,32},{16,48},{32,0},{48,16},{64,96},{80,112},{96,64},{112,80},{1... | collective-permute-start | bytes 2359304 | tf_op jit(solution)/shard_map/ppermute | solution.py:399
  62.1 61.0 %all-to-all-start = ((bf16[16,192,512]{2,1,0:T(8,128)(2,1)}), bf16[16,192,512]{2,1,0:T(8,128)(2,1)S(1)}, u32[]{:S(2)}, u32[]{:S(2)}) async-start(bf16[16,192,512]{2,1,0:T(8,128)(2,1)} %bitcast.34), calls=%async_computation | async-start | bytes 6291456 | tf_op jit(solution)/shard_map/all_to_all | solution.py:458
  71.3 16.1 %collective-permute-start.8 = (f32[288,128]{1,0:T(8,128)S(1)}, f32[288,128]{1,0:T(8,128)S(1)}, u32[]{:S(2)}, u32[]{:S(2)}) collective-permute-start(f32[288,128]{1,0:T(8,128)S(1)} %get-tuple-element.74), channel_id=1, source_target_pairs={{0,32},{16,48},{32,64},{48,80},{64,96},{80,112},{96,0},{112,16},{1... | collective-permute-start | bytes 442376 | tf_op jit(solution)/shard_map/ppermute | solution.py:386
  71.6 15.8 %collective-permute-start.9 = (f32[288,128]{1,0:T(8,128)S(1)}, f32[288,128]{1,0:T(8,128)S(1)}, u32[]{:S(2)}, u32[]{:S(2)}) collective-permute-start(f32[288,128]{1,0:T(8,128)S(1)} %get-tuple-element.75), channel_id=1, source_target_pairs={{0,64},{16,80},{32,96},{48,112},{64,0},{80,16},{96,32},{112,48},{1... | collective-permute-start | bytes 442376 | tf_op jit(solution)/shard_map/ppermute | solution.py:386
  75.4 12.0 %collective-permute-start.10 = (f32[288,128]{1,0:T(8,128)S(1)}, f32[288,128]{1,0:T(8,128)S(1)}, u32[]{:S(2)}, u32[]{:S(2)}) collective-permute-start(f32[288,128]{1,0:T(8,128)S(1)} %get-tuple-element.76), channel_id=1, source_target_pairs={{0,96},{16,112},{32,0},{48,16},{64,32},{80,48},{96,64},{112,80},{1... | collective-permute-start | bytes 442376 | tf_op jit(solution)/shard_map/ppermute | solution.py:386
  88.9 20.4 %collective-permute-start.14 = (f32[288,128]{1,0:T(8,128)S(1)}, f32[288,128]{1,0:T(8,128)S(1)}, u32[]{:S(2)}, u32[]{:S(2)}) collective-permute-start(f32[288,128]{1,0:T(8,128)S(1)} %get-tuple-element.101), channel_id=1, source_target_pairs={{0,18},{1,19},{2,16},{3,17},{4,22},{5,23},{6,20},{7,21},{8,26},{9,... | collective-permute-start | bytes 442376 | tf_op jit(solution)/shard_map/ppermute | solution.py:395
  89.8 20.2 %collective-permute-start.13 = (f32[288,128]{1,0:T(8,128)S(1)}, f32[288,128]{1,0:T(8,128)S(1)}, u32[]{:S(2)}, u32[]{:S(2)}) collective-permute-start(f32[288,128]{1,0:T(8,128)S(1)} %get-tuple-element.101), channel_id=1, source_target_pairs={{0,16},{1,17},{2,18},{3,19},{4,20},{5,21},{6,22},{7,23},{8,24},{9,... | collective-permute-start | bytes 442376 | tf_op jit(solution)/shard_map/ppermute | solution.py:395
  92.2 20.3 %collective-permute-start.12 = (f32[288,128]{1,0:T(8,128)S(1)}, f32[288,128]{1,0:T(8,128)S(1)}, u32[]{:S(2)}, u32[]{:S(2)}) collective-permute-start(f32[288,128]{1,0:T(8,128)S(1)} %get-tuple-element.100), channel_id=1, source_target_pairs={{0,2},{1,3},{2,0},{3,1},{4,6},{5,7},{6,4},{7,5},{8,10},{9,11},{10,... | collective-permute-start | bytes 442376 | tf_op jit(solution)/shard_map/ppermute | solution.py:395
  112.5 8.3 %collective-permute-start.15 = (f32[288,128]{1,0:T(8,128)S(1)}, f32[288,128]{1,0:T(8,128)S(1)}, u32[]{:S(2)}, u32[]{:S(2)}) collective-permute-start(f32[288,128]{1,0:T(8,128)S(1)} %add_add_fusion.1), channel_id=1, source_target_pairs={{0,8},{1,9},{2,10},{3,11},{4,12},{5,13},{6,14},{7,15},{8,0},{9,1},... | collective-permute-start | bytes 442376 | tf_op jit(solution)/shard_map/ppermute | solution.py:382
  115.4 6.5 %collective-permute-start.16 = (f32[288,128]{1,0:T(8,128)S(1)}, f32[288,128]{1,0:T(8,128)S(1)}, u32[]{:S(2)}, u32[]{:S(2)}) collective-permute-start(f32[288,128]{1,0:T(8,128)S(1)} %add_add_fusion.1), channel_id=1, source_target_pairs={{0,12},{1,13},{2,14},{3,15},{4,0},{5,1},{6,2},{7,3},{8,4},{9,5},{1... | collective-permute-start | bytes 442376 | tf_op jit(solution)/shard_map/ppermute | solution.py:382
  115.7 7.4 %collective-permute-start.17 = (f32[288,128]{1,0:T(8,128)S(1)}, f32[288,128]{1,0:T(8,128)}, u32[]{:S(2)}, u32[]{:S(2)}) collective-permute-start(f32[288,128]{1,0:T(8,128)S(1)} %add_add_fusion.1), channel_id=1, source_target_pairs={{0,4},{1,5},{2,6},{3,7},{4,8},{5,9},{6,10},{7,11},{8,12},{9,13},{1... | collective-permute-start | bytes 442376 | tf_op jit(solution)/shard_map/ppermute | solution.py:382
  124.8 52.3 %all-to-all-start.1 = ((bf16[16,192,512]{2,1,0:T(8,128)(2,1)}), bf16[16,192,512]{2,1,0:T(8,128)(2,1)}, u32[]{:S(2)}, u32[]{:S(2)}) async-start(bf16[16,192,512]{2,1,0:T(8,128)(2,1)} %bitcast.35), calls=%async_computation.1 | async-start | bytes 6291456 | tf_op jit(solution)/shard_map/all_to_all | solution.py:477
  132.9 16.2 %collective-permute-start.18 = (f32[4,288,128]{2,1,0:T(8,128)S(1)}, f32[4,288,128]{2,1,0:T(8,128)S(1)}, u32[]{:S(2)}, u32[]{:S(2)}) collective-permute-start(f32[4,288,128]{2,1,0:T(8,128)S(1)} %pad_maximum_fusion.a_ref), channel_id=1, source_target_pairs={{32,0},{34,2},{36,4},{38,6},{40,8},{42,10},{44,12},{46,14},{48,16}... | collective-permute-start | bytes 1769480 | tf_op jit(solution)/shard_map/ppermute | solution.py:411
  134.2 18.6 %collective-permute-start.19 = (f32[4,288,128]{2,1,0:T(8,128)S(1)}, f32[4,288,128]{2,1,0:T(8,128)S(1)}, u32[]{:S(2)}, u32[]{:S(2)}) collective-permute-start(f32[4,288,128]{2,1,0:T(8,128)S(1)} %pad_maximum_fusion.a_ref), channel_id=1, source_target_pairs={{64,0},{66,2},{68,4},{70,6},{72,8},{74,10},{76,12},{78,14},{80,16}... | collective-permute-start | bytes 1769480 | tf_op jit(solution)/shard_map/ppermute | solution.py:411
  139.7 15.9 %collective-permute-start.20 = (f32[4,288,128]{2,1,0:T(8,128)S(1)}, f32[4,288,128]{2,1,0:T(8,128)S(1)}, u32[]{:S(2)}, u32[]{:S(2)}) collective-permute-start(f32[4,288,128]{2,1,0:T(8,128)S(1)} %pad_maximum_fusion.a_ref), channel_id=1, source_target_pairs={{96,0},{98,2},{100,4},{102,6},{104,8},{106,10},{108,12},{110,14},{... | collective-permute-start | bytes 1769480 | tf_op jit(solution)/shard_map/ppermute | solution.py:411
  163.2 5.2 %collective-permute-start.21 = (f32[8,1024]{1,0:T(8,128)}, f32[8,1024]{1,0:T(8,128)S(1)}, u32[]{:S(2)}, u32[]{:S(2)}) collective-permute-start(f32[8,1024]{1,0:T(8,128)} %power.1.own_ref), channel_id=1, source_target_pairs={{0,1},{2,3},{4,5},{6,7},{8,9},{10,11},{12,13},{14,15},{16,17},{18,... | collective-permute-start | bytes 98312 | tf_op jit(solution)/shard_map/ppermute | solution.py:416
  165.7 5.4 %collective-permute-start.23 = (f32[8,1024]{1,0:T(8,128)}, f32[8,1024]{1,0:T(8,128)S(1)}, u32[]{:S(2)}, u32[]{:S(2)}) collective-permute-start(f32[8,1024]{1,0:T(8,128)} %power.1.own_ref), channel_id=1, source_target_pairs={{0,33},{2,35},{4,37},{6,39},{8,41},{10,43},{12,45},{14,47},{16,49}... | collective-permute-start | bytes 98312 | tf_op jit(solution)/shard_map/ppermute | solution.py:416
  (15 other events, 47.8 us)

commit v4 on v3

--- a/solution.py
+++ b/solution.py
@@ -19,7 +19,10 @@
 PIECE = CHUNK // 4
 F32 = jnp.float32
 BF16 = jnp.bfloat16
-PARAMS = pltpu.CompilerParams(vmem_limit_bytes=56 * 2**20)
+
+
+def params(mebibytes):
+    return pltpu.CompilerParams(vmem_limit_bytes=mebibytes * 2**20)
 
 
 def cost(microseconds):
@@ -91,17 +94,15 @@
         in_specs=[pl.BlockSpec((2, ROWS), lambda i: (0, 0)), pl.BlockSpec((ROWS, HALF), lambda i: (0, half))],
         out_specs=pl.BlockSpec((CAP, HALF), lambda i: (0, 0)),
         out_shape=shape_of((CAP, HALF), BF16),
-        compiler_params=PARAMS,
+        compiler_params=params(8),
         cost_estimate=cost(4.3),
         name="pack_first",
-    )(leave, rows)
-
-
-def slots_kernel(leave_ref, owner_ref, row_ref, col_ref):
+    )(leave, in_hbm(rows))
+
+
+def slots_kernel(leave_ref, owner_ref, row_ref):
     for level in range(2):
-        row = slot_row(leave_ref, level)
-        row_ref[level * 8 : (level + 1) * 8, :] = row
-        store_column(row, col_ref.at[level])
+        row_ref[level * 8 : (level + 1) * 8, :] = slot_row(leave_ref, level)
     owner = jnp.broadcast_to(owner_ref[...], (N_BLK, ROWS))
     named = jnp.where(owner == iota((N_BLK, ROWS), 0), 1.0, 0.0)
     place = named * (running_count(named) - 1.0 + (iota((N_BLK, ROWS), 0) * CAPP).astype(F32))
@@ -112,12 +113,16 @@
     return pl.pallas_call(
         slots_kernel,
         in_specs=[VMEM, VMEM],
-        out_specs=[VMEM, VMEM],
-        out_shape=[shape_of((24, ROWS), F32), shape_of((2, ROWS, LANES), F32)],
-        compiler_params=PARAMS,
+        out_specs=VMEM,
+        out_shape=shape_of((24, ROWS), F32),
+        compiler_params=params(6),
         cost_estimate=cost(3.2),
         name="slots",
     )(leave, owner)
+
+
+def in_hbm(value):
+    return pltpu.with_memory_space_constraint(value, pltpu.HBM)
 
 
 def placed(col, arrived, stay):
@@ -126,65 +131,66 @@
     return jnp.where(leaves, moved.astype(F32), stay.astype(F32)).astype(BF16)
 
 
-def swap_kernel(row_ref, col_ref, rows_ref, arrived_ref, next_ref, packed_ref):
+def whole(shape):
+    return pl.BlockSpec(shape, lambda i: (0,) * len(shape))
+
+
+def swap_kernel(row_ref, rows_ref, arrived_ref, next_ref, packed_ref, col_ref):
+    store_column(row_ref[0:8, :], col_ref)
     arrived = arrived_ref[...]
     for t in range(ROWS // 256):
         here = slice(t * 256, (t + 1) * 256)
-        next_ref[here, :] = placed(col_ref[0, here, :], arrived, rows_ref[here, :])
+        next_ref[here, :] = placed(col_ref[here, :], arrived, rows_ref[here, :])
     row = row_ref[8:16, :]
     for t in range(CAP // 256):
         hot = picker(row, t * 256, 256)
         packed_ref[t * 256 : (t + 1) * 256, :] = jnp.dot(hot, next_ref[...], preferred_element_type=F32).astype(BF16)
 
 
-def swap(row, col, rows, arrived, half):
-    whole = lambda shape: pl.BlockSpec(shape, lambda i: (0,) * len(shape))
+def swap(row, rows, arrived, half):
     return pl.pallas_call(
         swap_kernel,
         grid=(1,),
-        in_specs=[
-            whole((24, ROWS)),
-            whole((1, ROWS, LANES)),
-            pl.BlockSpec((ROWS, HALF), lambda i: (0, half)),
-            whole((CAP, HALF)),
-        ],
+        in_specs=[whole((24, ROWS)), pl.BlockSpec((ROWS, HALF), lambda i: (0, half)), whole((CAP, HALF))],
         out_specs=[whole((ROWS, HALF)), whole((CAP, HALF))],
         out_shape=[shape_of((ROWS, HALF), BF16), shape_of((CAP, HALF), BF16)],
-        compiler_params=PARAMS,
+        scratch_shapes=[pltpu.VMEM((ROWS, LANES), F32)],
+        compiler_params=params(12),
         cost_estimate=cost(20.0 if half == 0 else 5.3),
         name="swap",
-    )(row, col, rows, arrived)
-
-
-def leaf_kernel(row_ref, col_ref, rows_ref, arrived_ref, out_ref, last_ref):
-    arrived = arrived_ref[...]
-    for t in range(ROWS // 256):
-        here = slice(t * 256, (t + 1) * 256)
-        last_ref[here, :] = placed(col_ref[0, here, :], arrived, rows_ref[here, :])
-    row = row_ref[16:24, :]
-    for t in range(N_BLK * CAPP // 256):
+    )(row, in_hbm(rows), arrived)
+
+
+SLOTS = 768
+
+
+def leaf_kernel(row_ref, rows_ref, arrived_ref, out_ref, last_ref, col_ref):
+    @pl.when(pl.program_id(0) == 0)
+    def _():
+        store_column(row_ref[8:16, :], col_ref)
+        arrived = arrived_ref[...]
+        for t in range(ROWS // 256):
+            here = slice(t * 256, (t + 1) * 256)
+            last_ref[here, :] = placed(col_ref[here, :], arrived, rows_ref[here, :])
+
+    row = row_ref[16:24, :] - (pl.program_id(0) * SLOTS).astype(F32)
+    for t in range(SLOTS // 256):
         hot = picker(row, t * 256, 256)
         out_ref[t * 256 : (t + 1) * 256, :] = jnp.dot(hot, last_ref[...], preferred_element_type=F32).astype(BF16)
 
 
-def leaf_pack(row, col, rows, arrived):
-    whole = lambda shape: pl.BlockSpec(shape, lambda i: (0,) * len(shape))
+def leaf_pack(row, rows, arrived):
     return pl.pallas_call(
         leaf_kernel,
-        grid=(1,),
-        in_specs=[
-            whole((24, ROWS)),
-            pl.BlockSpec((1, ROWS, LANES), lambda i: (1, 0, 0)),
-            whole((ROWS, HALF)),
-            whole((CAP, HALF)),
-        ],
-        out_specs=whole((N_BLK * CAPP, HALF)),
-        out_shape=shape_of((N_BLK * CAPP, HALF), BF16),
-        scratch_shapes=[pltpu.VMEM((ROWS, HALF), BF16)],
-        compiler_params=PARAMS,
+        grid=(N_BLK * CAPP // SLOTS,),
+        in_specs=[whole((24, ROWS)), whole((ROWS, HALF)), whole((CAP, HALF))],
+        out_specs=pl.BlockSpec((SLOTS, HALF), lambda i: (i, 0)),
+        out_shape=pltpu.HBM((N_BLK * CAPP, HALF), BF16),
+        scratch_shapes=[pltpu.VMEM((ROWS, HALF), BF16), pltpu.VMEM((ROWS, LANES), F32)],
+        compiler_params=params(16),
         cost_estimate=cost(9.8),
         name="leaf_pack",
-    )(row, col, rows, arrived)
+    )(row, rows, arrived)
 
 
 def gram_kernel(flip_ref, leave_ref, rows_ref, keep_ref, send_ref, turned_ref, masked_ref):
@@ -221,7 +227,7 @@
         out_specs=[VMEM, VMEM],
         out_shape=[shape_of((4, CHUNK, LANES), F32)] * 2,
         scratch_shapes=[pltpu.VMEM((D, ROWS), BF16)] * 2,
-        compiler_params=PARAMS,
+        compiler_params=params(22),
         cost_estimate=cost(8.6),
         name="gram",
     )(flip, leave, rows)
@@ -289,7 +295,7 @@
         out_specs=VMEM,
         out_shape=shape_of((8, D), F32),
         scratch_shapes=[pltpu.VMEM((len(BLOCKS) * LANES, LANES), F32), pltpu.VMEM((D, D), F32)],
-        compiler_params=PARAMS,
+        compiler_params=params(12),
         cost_estimate=cost(6.6),
         name="power",
     )(place, members, start, *parts)
@@ -334,7 +340,7 @@
         in_specs=[SMEM] + [VMEM] * 7,
         out_specs=VMEM,
         out_shape=shape_of((2, ROWS), F32),
-        compiler_params=PARAMS,
+        compiler_params=params(8),
         cost_estimate=cost(5.2),
         name="scores",
     )(flags, *found, rows, left, right)
@@ -358,7 +364,7 @@
         in_specs=[pl.BlockSpec((JOIN, HALF), lambda i: (i, 0))],
         out_specs=pl.BlockSpec((JOIN, HALF), lambda i: (i, 0)),
         out_shape=shape_of((N_BLK * CAPP, D), BF16),
-        compiler_params=PARAMS,
+        compiler_params=params(10),
         cost_estimate=cost(5.2),
         name="join_first",
     )(left)
@@ -372,7 +378,7 @@
         out_specs=pl.BlockSpec((JOIN, HALF), lambda i: (i, 1)),
         out_shape=shape_of((N_BLK * CAPP, D), BF16),
         input_output_aliases={1: 0},
-        compiler_params=PARAMS,
+        compiler_params=params(10),
         cost_estimate=cost(5.2),
         name="join_second",
     )(right, held)
@@ -429,7 +435,7 @@
     arrived_l = across(packed_l, "cube", 1)
     leave_b = after(leave, packed_l)
     packed_r = pack_first(leave_b, rows, 1)
-    row, col = slots(leave_b, owner.reshape(1, ROWS))
+    row = slots(leave_b, owner.reshape(1, ROWS))
 
     flip = jnp.bitwise_xor(x_lo, core).astype(jnp.int32).reshape(1)
     leave_c, packed_r, row = lax.optimization_barrier((leave, packed_r, row))
@@ -438,7 +444,7 @@
 
     packed_r, arrived_l, keep = lax.optimization_barrier((packed_r, arrived_l, keep))
     arrived_r = across(packed_r, "cube", 1)
-    next_l, packed_l = swap(row, col, rows, arrived_l, 0)
+    next_l, packed_l = swap(row, rows, arrived_l, 0)
     arrived2_l = across(packed_l, "cube", 2)
 
     got = after(got, packed_l)
@@ -450,9 +456,9 @@
     parts = lax.optimization_barrier([part(k) for k in range(4)])
     moved = [along_y(parts[k], k) for k in (1, 2, 3)]
 
-    next_r, packed_r = swap(row, col, rows, after(arrived_r, parts), 1)
+    next_r, packed_r = swap(row, rows, after(arrived_r, parts), 1)
     arrived2_r = across(packed_r, "cube", 2)
-    leaf_l = leaf_pack(row, col, next_l, after(arrived2_l, packed_r))
+    leaf_l = leaf_pack(row, next_l, after(arrived2_l, packed_r))
 
     moved, _, arrived2_r = lax.optimization_barrier((moved, leaf_l, arrived2_r))
     out_l = lax.all_to_all(leaf_l, "blk", split_axis=0, concat_axis=0, tiled=True)
@@ -463,7 +469,7 @@
     )
     moved = [along_z(parts[k], k) for k in (1, 2, 3)]
 
-    leaf_r = leaf_pack(row, col, next_r, after(arrived2_r, parts))
+    leaf_r = leaf_pack(row, next_r, after(arrived2_r, parts))
 
     moved = after(moved, leaf_r)
     own = parts[0] + moved[0] + moved[1] + moved[2]

time: 182 us -> 175 us (0.962)
  Pallas kernels: 71.6 us -> 56.9 us
  waiting for transfers between devices: 44.4 us -> 50.4 us
    pallas_call x5, Pallas kernels: 33.8 us -> 27.1 us  [the longest x2 17 us: leaf_pack(): pl.pallas_call(leaf_kernel, grid=(N_BLK * CAPP // SLOTS,), in_specs=[whol...]
    ppermute x3, waiting for transfers between devices: 9.44 us -> 12.6 us  [to_worker(): return lax.ppermute(value, ('cube', 'blk'), pairs)]
    ppermute x6, waiting for transfers between devices: 6.86 us -> 9.58 us  [across(): lax.ppermute(value, axis, [(i, i ^ bit) for i in range(lax.axis_size(axis...]
    pallas_call x1, Pallas kernels: 5.25 us -> 2.89 us  [all_scores(): pl.pallas_call(scores_kernel, in_specs=[SMEM] + [VMEM] * 7, out_specs=VME...]
    pallas_call x1, Pallas kernels: 4.38 us -> 2.08 us  [join_first(): pl.pallas_call(join_first_kernel, grid=(N_BLK * CAPP // JOIN,), in_specs=...]
    pallas_call x1, Pallas kernels: 8.49 us -> 6.55 us  [gram(): pl.pallas_call(gram_kernel, in_specs=[SMEM, VMEM, VMEM], out_specs=[VMEM,...]
  transfers between devices with their start and end apart: 26 -> 26, of which waited for: 13 -> 14; matrix products, arithmetic and copies ran while one was open for 3% -> 4% of each run, Pallas kernels for 35% -> 28%
where the time goes in v4:
time: 175 us; the launch traced here: 174 us
  Pallas kernels  56.9 us (33%)
  starting transfers between devices  53.6 us (31%)
  waiting for transfers between devices  50.4 us (29%)
  other arithmetic  6.94 us (4%)
  local copies, waits for them, and re-layouts  5.4 us (3%)
    ppermute x3, waiting for transfers between devices, along_x(): return lax.ppermute(value, ('cube', 'blk'), pairs)  20 us
    pallas_call x2, Pallas kernels, leaf_pack(): pl.pallas_call(leaf_kernel, grid=(N_BLK * CAPP // SLOTS,), in_specs=[whol...  17 us
    ppermute x3, waiting for transfers between devices, to_worker(): return lax.ppermute(value, ('cube', 'blk'), pairs)  12.6 us
    ppermute x6, starting transfers between devices, along_y(): lax.ppermute(value, 'blk', [(i, (i // 4 + k) % 4 * 4 + i % 4) for i in ra...  10.7 us
    ppermute x6, waiting for transfers between devices, across(): lax.ppermute(value, axis, [(i, i ^ bit) for i in range(lax.axis_size(axis...  9.58 us
    pallas_call x2, Pallas kernels, swap(): pl.pallas_call(swap_kernel, grid=(1,), in_specs=[whole((24, ROWS)), pl.Bl...  9.08 us
    ppermute x3, starting transfers between devices, to_worker(): return lax.ppermute(value, ('cube', 'blk'), pairs)  8.29 us
    pallas_call x2, Pallas kernels, pack_first(): pl.pallas_call(pack_first_kernel, grid=(1,), in_specs=[pl.BlockSpec((2, R...  7.74 us
  transfers between devices with their start and end apart: 26, of which 14 were waited for; matrix products, arithmetic and copies ran while one was open for 4% of the time, Pallas kernels for 28%

profile of v4, /device:TPU:6, one launch (start us, length us, event | category | flops | bytes accessed | tf_op | source)
XLA Modules:
  0.0 174.2 jit_solution(9491368087242874)
XLA Ops:
  1.3 4.3 %pack_first.2 = bf16[768,512]{1,0:T(8,128)(2,1)} custom-call(s32[2,1536]{1,0:T(2,128)S(1)} %copy-done.3, bf16[1536,1024]{1,0:T(8,128)(2,1)} %rows_ref.11), custom_call_target="tpu_custom_call" | custom-call | flops 4944999936 | bytes 15867000 | tf_op jit(solution)/shard_map/pack_first/pallas_call | solution.py:91
  6.5 3.4 %pack_first.3 = bf16[768,512]{1,0:T(8,128)(2,1)S(1)} custom-call(s32[2,1536]{1,0:T(2,128)S(1)} %copy-done.4, bf16[1536,1024]{1,0:T(8,128)(2,1)} %rows_ref.11), custom_call_target="tpu_custom_call" | custom-call | flops 4944999936 | bytes 15867000 | tf_op jit(solution)/shard_map/pack_first/pallas_call | solution.py:91
  13.8 6.6 %gram.1 = (f32[4,1152,128]{2,1,0:T(8,128)S(1)}, f32[4,1152,128]{2,1,0:T(8,128)}) custom-call(s32[1]{0:T(128)} %bitcast.7.flip_ref, s32[2,1536]{1,0:T(2,128)S(1)} %copy-done.4, bf16[1536,1024]{1,0:T(8,128)(2,1)S(1)} %copy-done), custom_call_target="tpu_custom_call" | custom-call | flops 9889999872 | bytes 31734000 | tf_op jit(solution)/shard_map/gram/pallas_call | solution.py:224
  20.4 4.8 %collective-permute-done.arrived_ref = bf16[768,512]{1,0:T(8,128)(2,1)S(1)} collective-permute-done((bf16[768,512]{1,0:T(8,128)(2,1)}, bf16[768,512]{1,0:T(8,128)(2,1)S(1)}, u32[]{:S(2)}, u32[]{:S(2)}) %collective-permute-start) | collective-permute-done | bytes 786464 | tf_op jit(solution)/shard_map/ppermute | solution.py:405
  26.0 4.1 %swap.2 = (bf16[1536,512]{1,0:T(8,128)(2,1)S(1)}, bf16[768,512]{1,0:T(8,128)(2,1)S(1)}) custom-call(f32[24,1536]{1,0:T(8,128)S(1)} %slots.1.row_ref, bf16[1536,1024]{1,0:T(8,128)(2,1)} %rows_ref.11, bf16[768,512]{1,0:T(8,128)(2,1)S(1)} %collective-permute-done.arrived_ref), custom_call_target="tpu_custom_call" | custom-call | flops 23000000512 | bytes 73800000 | tf_op jit(solution)/shard_map/swap/pallas_call | solution.py:151
  32.1 3.1 %add_bitcast_fusion = (f32[1152,128]{1,0:T(8,128)}, f32[1152,128]{1,0:T(8,128)}, f32[1152,128]{1,0:T(8,128)}, f32[1152,128]{1,0:T(8,128)}) fusion(f32[4,1152,128]{2,1,0:T(8,128)} %collective-permute-done.2, s32[]{:T(128)S(6)} %select_n.123, f32[4,1152,128]{2,1,0:T(8,128)S(1)} %get-tuple-element.51, s32[]{:T(128)S(6)} %select_n.121, s32[]{:T(128)S(6)} %select_n.119, ...), kind=kLoop, calls=%fused_computation.2 | loop fusion | flops 589824 | bytes 7077904 | tf_op jit(solution)/shard_map/add | solution.py:454
  36.8 2.9 %collective-permute-start.4 = (f32[1152,128]{1,0:T(8,128)}, f32[1152,128]{1,0:T(8,128)}, u32[]{:S(2)}, u32[]{:S(2)}) collective-permute-start(f32[1152,128]{1,0:T(8,128)} %get-tuple-element.58), channel_id=1, source_target_pairs={{0,8},{1,9},{2,10},{3,11},{4,12},{5,13},{6,14},{7,15},{8,0},{9,1},... | collective-permute-start | bytes 1769480 | tf_op jit(solution)/shard_map/ppermute | solution.py:388
  43.8 5.0 %swap.3 = (bf16[1536,512]{1,0:T(8,128)(2,1)S(1)}, bf16[768,512]{1,0:T(8,128)(2,1)}) custom-call(f32[24,1536]{1,0:T(8,128)S(1)} %slots.1.row_ref, bf16[1536,1024]{1,0:T(8,128)(2,1)} %rows_ref.11, bf16[768,512]{1,0:T(8,128)(2,1)S(1)} %collective-permute-done.1.arrived_ref), custom_call_target="tpu_custom_call" | custom-call | flops 6095000064 | bytes 19557000 | tf_op jit(solution)/shard_map/swap/pallas_call | solution.py:151
  51.9 7.9 %leaf_pack.2 = bf16[3072,512]{1,0:T(8,128)(2,1)} custom-call(f32[24,1536]{1,0:T(8,128)S(1)} %slots.1.row_ref, bf16[1536,512]{1,0:T(8,128)(2,1)S(1)} %get-tuple-element.62.rows_ref.left_ref, bf16[768,512]{1,0:T(8,128)(2,1)S(1)} %collective-permute-done.6.arrived_ref), custom_call_target="tpu_custom_call" | custom-call | flops 11269999616 | bytes 36162000 | tf_op jit(solution)/shard_map/leaf_pack/pallas_call | solution.py:183
  59.9 7.5 %all-to-all-start = ((bf16[16,192,512]{2,1,0:T(8,128)(2,1)}), bf16[16,192,512]{2,1,0:T(8,128)(2,1)S(1)}, u32[]{:S(2)}, u32[]{:S(2)}) async-start(bf16[16,192,512]{2,1,0:T(8,128)(2,1)} %bitcast.36), calls=%async_computation | async-start | bytes 6291456 | tf_op jit(solution)/shard_map/all_to_all | solution.py:464
  71.7 3.6 %collective-permute-start.9 = (f32[288,128]{1,0:T(8,128)S(1)}, f32[288,128]{1,0:T(8,128)S(1)}, u32[]{:S(2)}, u32[]{:S(2)}) collective-permute-start(f32[288,128]{1,0:T(8,128)S(1)} %get-tuple-element.71), channel_id=1, source_target_pairs={{0,64},{16,80},{32,96},{48,112},{64,0},{80,16},{96,32},{112,48},{1... | collective-permute-start | bytes 442376 | tf_op jit(solution)/shard_map/ppermute | solution.py:392
  76.3 9.0 %leaf_pack.3 = bf16[3072,512]{1,0:T(8,128)(2,1)} custom-call(f32[24,1536]{1,0:T(8,128)S(1)} %slots.1.row_ref, bf16[1536,512]{1,0:T(8,128)(2,1)S(1)} %copy-done.10, bf16[768,512]{1,0:T(8,128)(2,1)} %collective-permute-done.7.arrived_ref), custom_call_target="tpu_custom_call" | custom-call | flops 11269999616 | bytes 36162000 | tf_op jit(solution)/shard_map/leaf_pack/pallas_call | solution.py:183
  90.3 16.8 %collective-permute-done.14 = f32[288,128]{1,0:T(8,128)S(1)} collective-permute-done((f32[288,128]{1,0:T(8,128)S(1)}, f32[288,128]{1,0:T(8,128)S(1)}, u32[]{:S(2)}, u32[]{:S(2)}) %collective-permute-start.14) | collective-permute-done | bytes 147488 | tf_op jit(solution)/shard_map/ppermute | solution.py:401
  110.4 2.8 %collective-permute-start.15 = (f32[288,128]{1,0:T(8,128)S(1)}, f32[288,128]{1,0:T(8,128)S(1)}, u32[]{:S(2)}, u32[]{:S(2)}) collective-permute-start(f32[288,128]{1,0:T(8,128)S(1)} %add_add_fusion.1), channel_id=1, source_target_pairs={{0,8},{1,9},{2,10},{3,11},{4,12},{5,13},{6,14},{7,15},{8,0},{9,1},... | collective-permute-start | bytes 442376 | tf_op jit(solution)/shard_map/ppermute | solution.py:388
  115.2 3.5 %collective-permute-done.15 = f32[288,128]{1,0:T(8,128)S(1)} collective-permute-done((f32[288,128]{1,0:T(8,128)S(1)}, f32[288,128]{1,0:T(8,128)S(1)}, u32[]{:S(2)}, u32[]{:S(2)}) %collective-permute-start.15) | collective-permute-done | bytes 147488 | tf_op jit(solution)/shard_map/ppermute | solution.py:388
  120.9 7.1 %all-to-all-start.1 = ((bf16[16,192,512]{2,1,0:T(8,128)(2,1)}), bf16[16,192,512]{2,1,0:T(8,128)(2,1)}, u32[]{:S(2)}, u32[]{:S(2)}) async-start(bf16[16,192,512]{2,1,0:T(8,128)(2,1)} %bitcast.37), calls=%async_computation.1 | async-start | bytes 6291456 | tf_op jit(solution)/shard_map/all_to_all | solution.py:483
  131.1 5.5 %collective-permute-start.19 = (f32[4,288,128]{2,1,0:T(8,128)}, f32[4,288,128]{2,1,0:T(8,128)}, u32[]{:S(2)}, u32[]{:S(2)}) collective-permute-start(f32[4,288,128]{2,1,0:T(8,128)} %pad_maximum_fusion.a_ref), channel_id=1, source_target_pairs={{64,0},{66,2},{68,4},{70,6},{72,8},{74,10},{76,12},{78,14},{80,16}... | collective-permute-start | bytes 1769480 | tf_op jit(solution)/shard_map/ppermute | solution.py:417
  140.3 6.0 %collective-permute-done.18.b_ref = f32[4,288,128]{2,1,0:T(8,128)} collective-permute-done((f32[4,288,128]{2,1,0:T(8,128)}, f32[4,288,128]{2,1,0:T(8,128)}, u32[]{:S(2)}, u32[]{:S(2)}) %collective-permute-start.18) | collective-permute-done | bytes 589856 | tf_op jit(solution)/shard_map/ppermute | solution.py:417
  146.3 3.8 %collective-permute-done.19.c_ref = f32[4,288,128]{2,1,0:T(8,128)} collective-permute-done((f32[4,288,128]{2,1,0:T(8,128)}, f32[4,288,128]{2,1,0:T(8,128)}, u32[]{:S(2)}, u32[]{:S(2)}) %collective-permute-start.19) | collective-permute-done | bytes 589856 | tf_op jit(solution)/shard_map/ppermute | solution.py:417
  150.1 2.8 %collective-permute-done.20.d_ref = f32[4,288,128]{2,1,0:T(8,128)} collective-permute-done((f32[4,288,128]{2,1,0:T(8,128)}, f32[4,288,128]{2,1,0:T(8,128)}, u32[]{:S(2)}, u32[]{:S(2)}) %collective-permute-start.20) | collective-permute-done | bytes 589856 | tf_op jit(solution)/shard_map/ppermute | solution.py:417
  152.9 6.1 %power.1.own_ref = f32[8,1024]{1,0:T(8,128)S(1)} custom-call(s32[2]{0:T(128)S(1)} %pad_add_fusion.1.place_ref, f32[1]{0:T(128)} %bitcast.4.members_ref, f32[1,1024]{1,0:T(1,128)S(1)} %bitcast.35, f32[4,288,128]{2,1,0:T(8,128)} %pad_maximum_fusion.a_ref, f32[4,288,128]{2,1,0:T(8,128)} %collective-permute-done.18.b_ref, ...), custom_call_target="tpu_custom_call" | custom-call | flops 7590000128 | bytes 24354000 | tf_op jit(solution)/shard_map/power/pallas_call | solution.py:292
  163.7 3.2 %collective-permute-done.23.both_ref = f32[8,1024]{1,0:T(8,128)S(1)} collective-permute-done((f32[8,1024]{1,0:T(8,128)S(1)}, f32[8,1024]{1,0:T(8,128)S(1)}, u32[]{:S(2)}, u32[]{:S(2)}) %collective-permute-start.23) | collective-permute-done | bytes 32800 | tf_op jit(solution)/shard_map/ppermute | solution.py:422
  166.9 2.9 %scores.1 = f32[2,1536]{1,0:T(2,128)} custom-call(s32[2]{0:T(128)S(1)} %pad_add_fusion.flags_ref, f32[8,1024]{1,0:T(8,128)S(1)} %power.1.own_ref, f32[8,1024]{1,0:T(8,128)S(1)} %collective-permute-done.21.core_ref, f32[8,1024]{1,0:T(8,128)S(1)} %collective-permute-done.22.z_ref, f32[8,1024]{1,0:T(8,128)S(1)} %collective-permute-done.23.both_ref, ...), custom_call_target="tpu_custom_call" | custom-call | flops 5980000256 | bytes 19188000 | tf_op jit(solution)/shard_map/scores/pallas_call | solution.py:338
  169.8 4.4 %join_second.1 = bf16[3072,1024]{1,0:T(8,128)(2,1)} custom-call(bf16[3072,512]{1,0:T(8,128)(2,1)} %bitcast.24.part_ref, bf16[3072,1024]{1,0:T(8,128)(2,1)} %join_first.1.held_ref), custom_call_target="tpu_custom_call", output_to_operand_aliasing={{}: (1, {})} | custom-call | flops 5980000256 | bytes 19188000 | tf_op jit(solution)/shard_map/join_second/pallas_call | solution.py:374
  (75 shorter events, 46.3 us)
Async XLA Ops:
  5.7 19.5 %collective-permute-start = (bf16[768,512]{1,0:T(8,128)(2,1)}, bf16[768,512]{1,0:T(8,128)(2,1)S(1)}, u32[]{:S(2)}, u32[]{:S(2)}) collective-permute-start(bf16[768,512]{1,0:T(8,128)(2,1)} %pack_first.2), channel_id=1, source_target_pairs={{0,16},{16,0},{32,48},{48,32},{64,80},{80,64},{96,112},{112,96},{1... | collective-permute-start | bytes 2359304 | tf_op jit(solution)/shard_map/ppermute | solution.py:405
  20.4 11.7 %collective-permute-start.2 = (f32[4,1152,128]{2,1,0:T(8,128)}, f32[4,1152,128]{2,1,0:T(8,128)}, u32[]{:S(2)}, u32[]{:S(2)}) collective-permute-start(f32[4,1152,128]{2,1,0:T(8,128)} %get-tuple-element.52), channel_id=1, source_target_pairs={{0,1},{1,0},{2,3},{3,2},{4,5},{5,4},{6,7},{7,6},{8,9},{9,8},{10,11... | collective-permute-start | bytes 7077896 | tf_op jit(solution)/shard_map/ppermute | solution.py:405
  25.1 18.6 %collective-permute-start.1 = (bf16[768,512]{1,0:T(8,128)(2,1)}, bf16[768,512]{1,0:T(8,128)(2,1)S(1)}, u32[]{:S(2)}, u32[]{:S(2)}) collective-permute-start(bf16[768,512]{1,0:T(8,128)(2,1)} %copy-done.2), channel_id=1, source_target_pairs={{0,16},{16,0},{32,48},{48,32},{64,80},{80,64},{96,112},{112,96},{1... | collective-permute-start | bytes 2359304 | tf_op jit(solution)/shard_map/ppermute | solution.py:405
  30.1 21.9 %collective-permute-start.6 = (bf16[768,512]{1,0:T(8,128)(2,1)S(1)}, bf16[768,512]{1,0:T(8,128)(2,1)S(1)}, u32[]{:S(2)}, u32[]{:S(2)}) collective-permute-start(bf16[768,512]{1,0:T(8,128)(2,1)S(1)} %get-tuple-element.54), channel_id=1, source_target_pairs={{0,32},{16,48},{32,0},{48,16},{64,96},{80,112},{96,64},{112,80},{1... | collective-permute-start | bytes 2359304 | tf_op jit(solution)/shard_map/ppermute | solution.py:405
  35.2 32.1 %collective-permute-start.3 = (f32[1152,128]{1,0:T(8,128)}, f32[1152,128]{1,0:T(8,128)}, u32[]{:S(2)}, u32[]{:S(2)}) collective-permute-start(f32[1152,128]{1,0:T(8,128)} %get-tuple-element.57), channel_id=1, source_target_pairs={{0,4},{1,5},{2,6},{3,7},{4,8},{5,9},{6,10},{7,11},{8,12},{9,13},{1... | collective-permute-start | bytes 1769480 | tf_op jit(solution)/shard_map/ppermute | solution.py:388
  36.8 30.6 %collective-permute-start.4 = (f32[1152,128]{1,0:T(8,128)}, f32[1152,128]{1,0:T(8,128)}, u32[]{:S(2)}, u32[]{:S(2)}) collective-permute-start(f32[1152,128]{1,0:T(8,128)} %get-tuple-element.58), channel_id=1, source_target_pairs={{0,8},{1,9},{2,10},{3,11},{4,12},{5,13},{6,14},{7,15},{8,0},{9,1},... | collective-permute-start | bytes 1769480 | tf_op jit(solution)/shard_map/ppermute | solution.py:388
  39.7 27.7 %collective-permute-start.5 = (f32[1152,128]{1,0:T(8,128)}, f32[1152,128]{1,0:T(8,128)}, u32[]{:S(2)}, u32[]{:S(2)}) collective-permute-start(f32[1152,128]{1,0:T(8,128)} %get-tuple-element.59), channel_id=1, source_target_pairs={{0,12},{1,13},{2,14},{3,15},{4,0},{5,1},{6,2},{7,3},{8,4},{9,5},{1... | collective-permute-start | bytes 1769480 | tf_op jit(solution)/shard_map/ppermute | solution.py:388
  50.0 18.1 %collective-permute-start.7 = (bf16[768,512]{1,0:T(8,128)(2,1)}, bf16[768,512]{1,0:T(8,128)(2,1)}, u32[]{:S(2)}, u32[]{:S(2)}) collective-permute-start(bf16[768,512]{1,0:T(8,128)(2,1)} %get-tuple-element.63), channel_id=1, source_target_pairs={{0,32},{16,48},{32,0},{48,16},{64,96},{80,112},{96,64},{112,80},{1... | collective-permute-start | bytes 2359304 | tf_op jit(solution)/shard_map/ppermute | solution.py:405
  59.9 61.0 %all-to-all-start = ((bf16[16,192,512]{2,1,0:T(8,128)(2,1)}), bf16[16,192,512]{2,1,0:T(8,128)(2,1)S(1)}, u32[]{:S(2)}, u32[]{:S(2)}) async-start(bf16[16,192,512]{2,1,0:T(8,128)(2,1)} %bitcast.36), calls=%async_computation | async-start | bytes 6291456 | tf_op jit(solution)/shard_map/all_to_all | solution.py:464
  69.8 15.5 %collective-permute-start.8 = (f32[288,128]{1,0:T(8,128)S(1)}, f32[288,128]{1,0:T(8,128)S(1)}, u32[]{:S(2)}, u32[]{:S(2)}) collective-permute-start(f32[288,128]{1,0:T(8,128)S(1)} %get-tuple-element.70), channel_id=1, source_target_pairs={{0,32},{16,48},{32,64},{48,80},{64,96},{80,112},{96,0},{112,16},{1... | collective-permute-start | bytes 442376 | tf_op jit(solution)/shard_map/ppermute | solution.py:392
  71.7 13.6 %collective-permute-start.9 = (f32[288,128]{1,0:T(8,128)S(1)}, f32[288,128]{1,0:T(8,128)S(1)}, u32[]{:S(2)}, u32[]{:S(2)}) collective-permute-start(f32[288,128]{1,0:T(8,128)S(1)} %get-tuple-element.71), channel_id=1, source_target_pairs={{0,64},{16,80},{32,96},{48,112},{64,0},{80,16},{96,32},{112,48},{1... | collective-permute-start | bytes 442376 | tf_op jit(solution)/shard_map/ppermute | solution.py:392
  75.2 10.1 %collective-permute-start.10 = (f32[288,128]{1,0:T(8,128)S(1)}, f32[288,128]{1,0:T(8,128)S(1)}, u32[]{:S(2)}, u32[]{:S(2)}) collective-permute-start(f32[288,128]{1,0:T(8,128)S(1)} %get-tuple-element.72), channel_id=1, source_target_pairs={{0,96},{16,112},{32,0},{48,16},{64,32},{80,48},{96,64},{112,80},{1... | collective-permute-start | bytes 442376 | tf_op jit(solution)/shard_map/ppermute | solution.py:392
  86.8 20.3 %collective-permute-start.14 = (f32[288,128]{1,0:T(8,128)S(1)}, f32[288,128]{1,0:T(8,128)S(1)}, u32[]{:S(2)}, u32[]{:S(2)}) collective-permute-start(f32[288,128]{1,0:T(8,128)S(1)} %get-tuple-element.97), channel_id=1, source_target_pairs={{0,18},{1,19},{2,16},{3,17},{4,22},{5,23},{6,20},{7,21},{8,26},{9,... | collective-permute-start | bytes 442376 | tf_op jit(solution)/shard_map/ppermute | solution.py:401
  87.7 20.1 %collective-permute-start.13 = (f32[288,128]{1,0:T(8,128)S(1)}, f32[288,128]{1,0:T(8,128)S(1)}, u32[]{:S(2)}, u32[]{:S(2)}) collective-permute-start(f32[288,128]{1,0:T(8,128)S(1)} %get-tuple-element.97), channel_id=1, source_target_pairs={{0,16},{1,17},{2,18},{3,19},{4,20},{5,21},{6,22},{7,23},{8,24},{9,... | collective-permute-start | bytes 442376 | tf_op jit(solution)/shard_map/ppermute | solution.py:401
  90.1 20.2 %collective-permute-start.12 = (f32[288,128]{1,0:T(8,128)S(1)}, f32[288,128]{1,0:T(8,128)S(1)}, u32[]{:S(2)}, u32[]{:S(2)}) collective-permute-start(f32[288,128]{1,0:T(8,128)S(1)} %get-tuple-element.96), channel_id=1, source_target_pairs={{0,2},{1,3},{2,0},{3,1},{4,6},{5,7},{6,4},{7,5},{8,10},{9,11},{10,... | collective-permute-start | bytes 442376 | tf_op jit(solution)/shard_map/ppermute | solution.py:401
  110.4 8.3 %collective-permute-start.15 = (f32[288,128]{1,0:T(8,128)S(1)}, f32[288,128]{1,0:T(8,128)S(1)}, u32[]{:S(2)}, u32[]{:S(2)}) collective-permute-start(f32[288,128]{1,0:T(8,128)S(1)} %add_add_fusion.1), channel_id=1, source_target_pairs={{0,8},{1,9},{2,10},{3,11},{4,12},{5,13},{6,14},{7,15},{8,0},{9,1},... | collective-permute-start | bytes 442376 | tf_op jit(solution)/shard_map/ppermute | solution.py:388
  113.2 6.5 %collective-permute-start.16 = (f32[288,128]{1,0:T(8,128)S(1)}, f32[288,128]{1,0:T(8,128)S(1)}, u32[]{:S(2)}, u32[]{:S(2)}) collective-permute-start(f32[288,128]{1,0:T(8,128)S(1)} %add_add_fusion.1), channel_id=1, source_target_pairs={{0,12},{1,13},{2,14},{3,15},{4,0},{5,1},{6,2},{7,3},{8,4},{9,5},{1... | collective-permute-start | bytes 442376 | tf_op jit(solution)/shard_map/ppermute | solution.py:388
  113.5 7.4 %collective-permute-start.17 = (f32[288,128]{1,0:T(8,128)S(1)}, f32[288,128]{1,0:T(8,128)}, u32[]{:S(2)}, u32[]{:S(2)}) collective-permute-start(f32[288,128]{1,0:T(8,128)S(1)} %add_add_fusion.1), channel_id=1, source_target_pairs={{0,4},{1,5},{2,6},{3,7},{4,8},{5,9},{6,10},{7,11},{8,12},{9,13},{1... | collective-permute-start | bytes 442376 | tf_op jit(solution)/shard_map/ppermute | solution.py:388
  120.9 48.9 %all-to-all-start.1 = ((bf16[16,192,512]{2,1,0:T(8,128)(2,1)}), bf16[16,192,512]{2,1,0:T(8,128)(2,1)}, u32[]{:S(2)}, u32[]{:S(2)}) async-start(bf16[16,192,512]{2,1,0:T(8,128)(2,1)} %bitcast.37), calls=%async_computation.1 | async-start | bytes 6291456 | tf_op jit(solution)/shard_map/all_to_all | solution.py:483
  129.8 16.5 %collective-permute-start.18 = (f32[4,288,128]{2,1,0:T(8,128)}, f32[4,288,128]{2,1,0:T(8,128)}, u32[]{:S(2)}, u32[]{:S(2)}) collective-permute-start(f32[4,288,128]{2,1,0:T(8,128)} %pad_maximum_fusion.a_ref), channel_id=1, source_target_pairs={{32,0},{34,2},{36,4},{38,6},{40,8},{42,10},{44,12},{46,14},{48,16}... | collective-permute-start | bytes 1769480 | tf_op jit(solution)/shard_map/ppermute | solution.py:417
  131.1 19.0 %collective-permute-start.19 = (f32[4,288,128]{2,1,0:T(8,128)}, f32[4,288,128]{2,1,0:T(8,128)}, u32[]{:S(2)}, u32[]{:S(2)}) collective-permute-start(f32[4,288,128]{2,1,0:T(8,128)} %pad_maximum_fusion.a_ref), channel_id=1, source_target_pairs={{64,0},{66,2},{68,4},{70,6},{72,8},{74,10},{76,12},{78,14},{80,16}... | collective-permute-start | bytes 1769480 | tf_op jit(solution)/shard_map/ppermute | solution.py:417
  136.6 16.3 %collective-permute-start.20 = (f32[4,288,128]{2,1,0:T(8,128)}, f32[4,288,128]{2,1,0:T(8,128)}, u32[]{:S(2)}, u32[]{:S(2)}) collective-permute-start(f32[4,288,128]{2,1,0:T(8,128)} %pad_maximum_fusion.a_ref), channel_id=1, source_target_pairs={{96,0},{98,2},{100,4},{102,6},{104,8},{106,10},{108,12},{110,14},{... | collective-permute-start | bytes 1769480 | tf_op jit(solution)/shard_map/ppermute | solution.py:417
  159.1 4.6 %collective-permute-start.21 = (f32[8,1024]{1,0:T(8,128)S(1)}, f32[8,1024]{1,0:T(8,128)S(1)}, u32[]{:S(2)}, u32[]{:S(2)}) collective-permute-start(f32[8,1024]{1,0:T(8,128)S(1)} %power.1.own_ref), channel_id=1, source_target_pairs={{0,1},{2,3},{4,5},{6,7},{8,9},{10,11},{12,13},{14,15},{16,17},{18,... | collective-permute-start | bytes 98312 | tf_op jit(solution)/shard_map/ppermute | solution.py:422
  161.7 5.2 %collective-permute-start.23 = (f32[8,1024]{1,0:T(8,128)S(1)}, f32[8,1024]{1,0:T(8,128)S(1)}, u32[]{:S(2)}, u32[]{:S(2)}) collective-permute-start(f32[8,1024]{1,0:T(8,128)S(1)} %power.1.own_ref), channel_id=1, source_target_pairs={{0,33},{2,35},{4,37},{6,39},{8,41},{10,43},{12,45},{14,47},{16,49}... | collective-permute-start | bytes 98312 | tf_op jit(solution)/shard_map/ppermute | solution.py:422
  (15 other events, 107.0 us)

commit v5 on v4

--- a/solution.py
+++ b/solution.py
@@ -365,7 +365,7 @@
         out_specs=pl.BlockSpec((JOIN, HALF), lambda i: (i, 0)),
         out_shape=shape_of((N_BLK * CAPP, D), BF16),
         compiler_params=params(10),
-        cost_estimate=cost(5.2),
+        cost_estimate=cost(8.0),
         name="join_first",
     )(left)
 
@@ -479,12 +479,12 @@
     theirs = jnp.where(core == 0, both, jnp.where(x_lo == 0, other, own))
     piece = mine + along_x(mine, 2) + along_x(theirs, 1) + along_x(theirs, 3)
     near = [along_y(piece, -k) for k in (2, 1, 3)]
-    leaf_r, near, out_l = lax.optimization_barrier((leaf_r, near, out_l))
+    leaf_r, _, out_l = lax.optimization_barrier((leaf_r, piece, out_l))
     out_r = lax.all_to_all(leaf_r, "blk", split_axis=0, concat_axis=0, tiled=True)
+    held = join_first(after(out_l, leaf_r))
+    held, near = lax.optimization_barrier((held, near))
     stack = jnp.stack([piece, near[1], near[0], near[2]])
     gathered = [stack] + [to_worker(stack, k) for k in (1, 2, 3)]
-    held = join_first(after(out_l, stack))
-    held, gathered = lax.optimization_barrier((held, gathered))
 
     place = jnp.stack([y, z]).astype(jnp.int32)
     members = jnp.where(core == 0, ROWS * N_BLK * N_CUBE, ROWS * N_BLK * N_CUBE // 2).astype(F32).reshape(1)

time: 175 us -> 169 us (0.966)
  waiting for transfers between devices: 50.4 us -> 46.2 us
    ppermute x6, waiting for transfers between devices: 5.03 us -> 0.02 us  [along_y(): lax.ppermute(value, 'blk', [(i, (i // 4 + k) % 4 * 4 + i % 4) for i in ra...]
    unnamed x26 -> x24, local copies, waits for them, and re-layouts: 5.35 us -> 4.66 us
  transfers between devices with their start and end apart: 26 -> 26, of which waited for: 14 -> 11; matrix products, arithmetic and copies ran while one was open for 4% -> 4% of each run, Pallas kernels for 28% -> 28%
where the time goes in v5:
time: 169 us; the launch traced here: 168 us
  Pallas kernels  55.8 us (33%)
  starting transfers between devices  53.6 us (32%)
  waiting for transfers between devices  46.2 us (27%)
  other arithmetic  7.05 us (4%)
  local copies, waits for them, and re-layouts  4.72 us (3%)
    ppermute x3, waiting for transfers between devices, along_x(): return lax.ppermute(value, ('cube', 'blk'), pairs)  19 us
    pallas_call x2, Pallas kernels, leaf_pack(): pl.pallas_call(leaf_kernel, grid=(N_BLK * CAPP // SLOTS,), in_specs=[whol...  17 us
    ppermute x3, waiting for transfers between devices, to_worker(): return lax.ppermute(value, ('cube', 'blk'), pairs)  14.3 us
    ppermute x6, starting transfers between devices, along_y(): lax.ppermute(value, 'blk', [(i, (i // 4 + k) % 4 * 4 + i % 4) for i in ra...  10.7 us
    ppermute x6, waiting for transfers between devices, across(): lax.ppermute(value, axis, [(i, i ^ bit) for i in range(lax.axis_size(axis...  9.75 us
    pallas_call x2, Pallas kernels, swap(): pl.pallas_call(swap_kernel, grid=(1,), in_specs=[whole((24, ROWS)), pl.Bl...  9.17 us
    ppermute x3, starting transfers between devices, to_worker(): return lax.ppermute(value, ('cube', 'blk'), pairs)  8.27 us
    pallas_call x2, Pallas kernels, pack_first(): pl.pallas_call(pack_first_kernel, grid=(1,), in_specs=[pl.BlockSpec((2, R...  7.74 us
  transfers between devices with their start and end apart: 26, of which 11 were waited for; matrix products, arithmetic and copies ran while one was open for 4% of the time, Pallas kernels for 28%

profile of v5, /device:TPU:6, one launch (start us, length us, event | category | flops | bytes accessed | tf_op | source)
XLA Modules:
  0.0 168.3 jit_solution(4052653732157028876)
XLA Ops:
  1.3 4.3 %pack_first.2 = bf16[768,512]{1,0:T(8,128)(2,1)} custom-call(s32[2,1536]{1,0:T(2,128)S(1)} %copy-done.3, bf16[1536,1024]{1,0:T(8,128)(2,1)} %rows_ref.11), custom_call_target="tpu_custom_call" | custom-call | flops 4944999936 | bytes 15867000 | tf_op jit(solution)/shard_map/pack_first/pallas_call | solution.py:91
  6.5 3.4 %pack_first.3 = bf16[768,512]{1,0:T(8,128)(2,1)S(1)} custom-call(s32[2,1536]{1,0:T(2,128)S(1)} %copy-done.4, bf16[1536,1024]{1,0:T(8,128)(2,1)} %rows_ref.11), custom_call_target="tpu_custom_call" | custom-call | flops 4944999936 | bytes 15867000 | tf_op jit(solution)/shard_map/pack_first/pallas_call | solution.py:91
  13.8 6.6 %gram.1 = (f32[4,1152,128]{2,1,0:T(8,128)S(1)}, f32[4,1152,128]{2,1,0:T(8,128)}) custom-call(s32[1]{0:T(128)} %bitcast.7.flip_ref, s32[2,1536]{1,0:T(2,128)S(1)} %copy-done.4, bf16[1536,1024]{1,0:T(8,128)(2,1)S(1)} %copy-done), custom_call_target="tpu_custom_call" | custom-call | flops 9889999872 | bytes 31734000 | tf_op jit(solution)/shard_map/gram/pallas_call | solution.py:224
  20.4 4.8 %collective-permute-done.arrived_ref = bf16[768,512]{1,0:T(8,128)(2,1)S(1)} collective-permute-done((bf16[768,512]{1,0:T(8,128)(2,1)}, bf16[768,512]{1,0:T(8,128)(2,1)S(1)}, u32[]{:S(2)}, u32[]{:S(2)}) %collective-permute-start) | collective-permute-done | bytes 786464 | tf_op jit(solution)/shard_map/ppermute | solution.py:405
  26.0 4.1 %swap.2 = (bf16[1536,512]{1,0:T(8,128)(2,1)S(1)}, bf16[768,512]{1,0:T(8,128)(2,1)S(1)}) custom-call(f32[24,1536]{1,0:T(8,128)S(1)} %slots.1.row_ref, bf16[1536,1024]{1,0:T(8,128)(2,1)} %rows_ref.11, bf16[768,512]{1,0:T(8,128)(2,1)S(1)} %collective-permute-done.arrived_ref), custom_call_target="tpu_custom_call" | custom-call | flops 23000000512 | bytes 73800000 | tf_op jit(solution)/shard_map/swap/pallas_call | solution.py:151
  32.1 3.1 %add_bitcast_fusion = (f32[1152,128]{1,0:T(8,128)}, f32[1152,128]{1,0:T(8,128)}, f32[1152,128]{1,0:T(8,128)}, f32[1152,128]{1,0:T(8,128)}) fusion(f32[4,1152,128]{2,1,0:T(8,128)} %collective-permute-done.1, s32[]{:T(128)S(6)} %select_n.124, f32[4,1152,128]{2,1,0:T(8,128)S(1)} %get-tuple-element.45, s32[]{:T(128)S(6)} %select_n.122, s32[]{:T(128)S(6)} %select_n.120, ...), kind=kLoop, calls=%fused_computation.2 | loop fusion | flops 589824 | bytes 7077904 | tf_op jit(solution)/shard_map/add | solution.py:454
  36.7 2.9 %collective-permute-start.3 = (f32[1152,128]{1,0:T(8,128)}, f32[1152,128]{1,0:T(8,128)}, u32[]{:S(2)}, u32[]{:S(2)}) collective-permute-start(f32[1152,128]{1,0:T(8,128)} %get-tuple-element.53), channel_id=1, source_target_pairs={{0,8},{1,9},{2,10},{3,11},{4,12},{5,13},{6,14},{7,15},{8,0},{9,1},... | collective-permute-start | bytes 1769480 | tf_op jit(solution)/shard_map/ppermute | solution.py:388
  41.0 2.8 %collective-permute-done.6.arrived_ref = bf16[768,512]{1,0:T(8,128)(2,1)S(1)} collective-permute-done((bf16[768,512]{1,0:T(8,128)(2,1)}, bf16[768,512]{1,0:T(8,128)(2,1)S(1)}, u32[]{:S(2)}, u32[]{:S(2)}) %collective-permute-start.6) | collective-permute-done | bytes 786464 | tf_op jit(solution)/shard_map/ppermute | solution.py:405
  43.8 5.1 %swap.3 = (bf16[1536,512]{1,0:T(8,128)(2,1)S(1)}, bf16[768,512]{1,0:T(8,128)(2,1)}) custom-call(f32[24,1536]{1,0:T(8,128)S(1)} %slots.1.row_ref, bf16[1536,1024]{1,0:T(8,128)(2,1)} %rows_ref.11, bf16[768,512]{1,0:T(8,128)(2,1)S(1)} %collective-permute-done.6.arrived_ref), custom_call_target="tpu_custom_call" | custom-call | flops 6095000064 | bytes 19557000 | tf_op jit(solution)/shard_map/swap/pallas_call | solution.py:151
  52.0 7.9 %leaf_pack.2 = bf16[3072,512]{1,0:T(8,128)(2,1)} custom-call(f32[24,1536]{1,0:T(8,128)S(1)} %slots.1.row_ref, bf16[1536,512]{1,0:T(8,128)(2,1)S(1)} %get-tuple-element.55.rows_ref.left_ref, bf16[768,512]{1,0:T(8,128)(2,1)S(1)} %collective-permute-done.5.arrived_ref), custom_call_target="tpu_custom_call" | custom-call | flops 11269999616 | bytes 36162000 | tf_op jit(solution)/shard_map/leaf_pack/pallas_call | solution.py:183
  59.9 7.5 %all-to-all-start = ((bf16[16,192,512]{2,1,0:T(8,128)(2,1)}), bf16[16,192,512]{2,1,0:T(8,128)(2,1)S(1)}, u32[]{:S(2)}, u32[]{:S(2)}) async-start(bf16[16,192,512]{2,1,0:T(8,128)(2,1)} %bitcast.36), calls=%async_computation | async-start | bytes 6291456 | tf_op jit(solution)/shard_map/all_to_all | solution.py:464
  71.7 3.6 %collective-permute-start.9 = (f32[288,128]{1,0:T(8,128)S(1)}, f32[288,128]{1,0:T(8,128)S(1)}, u32[]{:S(2)}, u32[]{:S(2)}) collective-permute-start(f32[288,128]{1,0:T(8,128)S(1)} %get-tuple-element.65), channel_id=1, source_target_pairs={{0,64},{16,80},{32,96},{48,112},{64,0},{80,16},{96,32},{112,48},{1... | collective-permute-start | bytes 442376 | tf_op jit(solution)/shard_map/ppermute | solution.py:392
  76.3 9.0 %leaf_pack.3 = bf16[3072,512]{1,0:T(8,128)(2,1)} custom-call(f32[24,1536]{1,0:T(8,128)S(1)} %slots.1.row_ref, bf16[1536,512]{1,0:T(8,128)(2,1)S(1)} %copy-done.10, bf16[768,512]{1,0:T(8,128)(2,1)} %collective-permute-done.7.arrived_ref), custom_call_target="tpu_custom_call" | custom-call | flops 11269999616 | bytes 36162000 | tf_op jit(solution)/shard_map/leaf_pack/pallas_call | solution.py:183
  91.4 15.7 %collective-permute-done.14 = f32[288,128]{1,0:T(8,128)S(1)} collective-permute-done((f32[288,128]{1,0:T(8,128)S(1)}, f32[288,128]{1,0:T(8,128)S(1)}, u32[]{:S(2)}, u32[]{:S(2)}) %collective-permute-start.14) | collective-permute-done | bytes 147488 | tf_op jit(solution)/shard_map/ppermute | solution.py:401
  110.4 2.8 %collective-permute-start.15 = (f32[288,128]{1,0:T(8,128)S(1)}, f32[288,128]{1,0:T(8,128)}, u32[]{:S(2)}, u32[]{:S(2)}) collective-permute-start(f32[288,128]{1,0:T(8,128)S(1)} %add_add_fusion.1), channel_id=1, source_target_pairs={{0,8},{1,9},{2,10},{3,11},{4,12},{5,13},{6,14},{7,15},{8,0},{9,1},... | collective-permute-start | bytes 442376 | tf_op jit(solution)/shard_map/ppermute | solution.py:388
  115.3 7.0 %all-to-all-start.1 = ((bf16[16,192,512]{2,1,0:T(8,128)(2,1)}), bf16[16,192,512]{2,1,0:T(8,128)(2,1)}, u32[]{:S(2)}, u32[]{:S(2)}) async-start(bf16[16,192,512]{2,1,0:T(8,128)(2,1)} %bitcast.37), calls=%async_computation.1 | async-start | bytes 6291456 | tf_op jit(solution)/shard_map/all_to_all | solution.py:483
  126.8 5.5 %collective-permute-start.19 = (f32[4,288,128]{2,1,0:T(8,128)S(1)}, f32[4,288,128]{2,1,0:T(8,128)S(1)}, u32[]{:S(2)}, u32[]{:S(2)}) collective-permute-start(f32[4,288,128]{2,1,0:T(8,128)S(1)} %pad_maximum_fusion.a_ref), channel_id=1, source_target_pairs={{64,0},{66,2},{68,4},{70,6},{72,8},{74,10},{76,12},{78,14},{80,16}... | collective-permute-start | bytes 1769480 | tf_op jit(solution)/shard_map/ppermute | solution.py:417
  133.9 7.8 %collective-permute-done.18.b_ref = f32[4,288,128]{2,1,0:T(8,128)S(1)} collective-permute-done((f32[4,288,128]{2,1,0:T(8,128)S(1)}, f32[4,288,128]{2,1,0:T(8,128)S(1)}, u32[]{:S(2)}, u32[]{:S(2)}) %collective-permute-start.18) | collective-permute-done | bytes 589856 | tf_op jit(solution)/shard_map/ppermute | solution.py:417
  141.7 3.7 %collective-permute-done.19.c_ref = f32[4,288,128]{2,1,0:T(8,128)S(1)} collective-permute-done((f32[4,288,128]{2,1,0:T(8,128)S(1)}, f32[4,288,128]{2,1,0:T(8,128)S(1)}, u32[]{:S(2)}, u32[]{:S(2)}) %collective-permute-start.19) | collective-permute-done | bytes 589856 | tf_op jit(solution)/shard_map/ppermute | solution.py:417
  145.4 2.8 %collective-permute-done.20.d_ref = f32[4,288,128]{2,1,0:T(8,128)S(1)} collective-permute-done((f32[4,288,128]{2,1,0:T(8,128)S(1)}, f32[4,288,128]{2,1,0:T(8,128)S(1)}, u32[]{:S(2)}, u32[]{:S(2)}) %collective-permute-start.20) | collective-permute-done | bytes 589856 | tf_op jit(solution)/shard_map/ppermute | solution.py:417
  148.3 4.9 %power.1.own_ref = f32[8,1024]{1,0:T(8,128)S(1)} custom-call(s32[2]{0:T(128)S(1)} %pad_add_fusion.1.place_ref, f32[1]{0:T(128)} %bitcast.4.members_ref, f32[1,1024]{1,0:T(1,128)S(1)} %bitcast.35, f32[4,288,128]{2,1,0:T(8,128)S(1)} %pad_maximum_fusion.a_ref, f32[4,288,128]{2,1,0:T(8,128)S(1)} %collective-permute-done.18.b_ref, ...), custom_call_target="tpu_custom_call" | custom-call | flops 7590000128 | bytes 24354000 | tf_op jit(solution)/shard_map/power/pallas_call | solution.py:292
  157.8 3.2 %collective-permute-done.23.both_ref = f32[8,1024]{1,0:T(8,128)S(1)} collective-permute-done((f32[8,1024]{1,0:T(8,128)S(1)}, f32[8,1024]{1,0:T(8,128)S(1)}, u32[]{:S(2)}, u32[]{:S(2)}) %collective-permute-start.23) | collective-permute-done | bytes 32800 | tf_op jit(solution)/shard_map/ppermute | solution.py:422
  161.0 2.9 %scores.1 = f32[2,1536]{1,0:T(2,128)} custom-call(s32[2]{0:T(128)S(1)} %pad_add_fusion.flags_ref, f32[8,1024]{1,0:T(8,128)S(1)} %power.1.own_ref, f32[8,1024]{1,0:T(8,128)S(1)} %collective-permute-done.21.core_ref, f32[8,1024]{1,0:T(8,128)S(1)} %collective-permute-done.22.z_ref, f32[8,1024]{1,0:T(8,128)S(1)} %collective-permute-done.23.both_ref, ...), custom_call_target="tpu_custom_call" | custom-call | flops 5980000256 | bytes 19188000 | tf_op jit(solution)/shard_map/scores/pallas_call | solution.py:338
  163.9 4.4 %join_second.1 = bf16[3072,1024]{1,0:T(8,128)(2,1)} custom-call(bf16[3072,512]{1,0:T(8,128)(2,1)} %bitcast.24.part_ref, bf16[3072,1024]{1,0:T(8,128)(2,1)} %join_first.1.held_ref), custom_call_target="tpu_custom_call", output_to_operand_aliasing={{}: (1, {})} | custom-call | flops 5980000256 | bytes 19188000 | tf_op jit(solution)/shard_map/join_second/pallas_call | solution.py:374
  (73 shorter events, 41.6 us)
Async XLA Ops:
  5.7 19.5 %collective-permute-start = (bf16[768,512]{1,0:T(8,128)(2,1)}, bf16[768,512]{1,0:T(8,128)(2,1)S(1)}, u32[]{:S(2)}, u32[]{:S(2)}) collective-permute-start(bf16[768,512]{1,0:T(8,128)(2,1)} %pack_first.2), channel_id=1, source_target_pairs={{0,16},{16,0},{32,48},{48,32},{64,80},{80,64},{96,112},{112,96},{1... | collective-permute-start | bytes 2359304 | tf_op jit(solution)/shard_map/ppermute | solution.py:405
  20.4 11.7 %collective-permute-start.1 = (f32[4,1152,128]{2,1,0:T(8,128)}, f32[4,1152,128]{2,1,0:T(8,128)}, u32[]{:S(2)}, u32[]{:S(2)}) collective-permute-start(f32[4,1152,128]{2,1,0:T(8,128)} %get-tuple-element.46), channel_id=1, source_target_pairs={{0,1},{1,0},{2,3},{3,2},{4,5},{5,4},{6,7},{7,6},{8,9},{9,8},{10,11... | collective-permute-start | bytes 7077896 | tf_op jit(solution)/shard_map/ppermute | solution.py:405
  25.2 18.6 %collective-permute-start.6 = (bf16[768,512]{1,0:T(8,128)(2,1)}, bf16[768,512]{1,0:T(8,128)(2,1)S(1)}, u32[]{:S(2)}, u32[]{:S(2)}) collective-permute-start(bf16[768,512]{1,0:T(8,128)(2,1)} %copy-done.2), channel_id=1, source_target_pairs={{0,16},{16,0},{32,48},{48,32},{64,80},{80,64},{96,112},{112,96},{1... | collective-permute-start | bytes 2359304 | tf_op jit(solution)/shard_map/ppermute | solution.py:405
  30.1 21.9 %collective-permute-start.5 = (bf16[768,512]{1,0:T(8,128)(2,1)S(1)}, bf16[768,512]{1,0:T(8,128)(2,1)S(1)}, u32[]{:S(2)}, u32[]{:S(2)}) collective-permute-start(bf16[768,512]{1,0:T(8,128)(2,1)S(1)} %get-tuple-element.49), channel_id=1, source_target_pairs={{0,32},{16,48},{32,0},{48,16},{64,96},{80,112},{96,64},{112,80},{1... | collective-permute-start | bytes 2359304 | tf_op jit(solution)/shard_map/ppermute | solution.py:405
  35.1 32.2 %collective-permute-start.2 = (f32[1152,128]{1,0:T(8,128)}, f32[1152,128]{1,0:T(8,128)}, u32[]{:S(2)}, u32[]{:S(2)}) collective-permute-start(f32[1152,128]{1,0:T(8,128)} %get-tuple-element.52), channel_id=1, source_target_pairs={{0,4},{1,5},{2,6},{3,7},{4,8},{5,9},{6,10},{7,11},{8,12},{9,13},{1... | collective-permute-start | bytes 1769480 | tf_op jit(solution)/shard_map/ppermute | solution.py:388
  36.7 30.7 %collective-permute-start.3 = (f32[1152,128]{1,0:T(8,128)}, f32[1152,128]{1,0:T(8,128)}, u32[]{:S(2)}, u32[]{:S(2)}) collective-permute-start(f32[1152,128]{1,0:T(8,128)} %get-tuple-element.53), channel_id=1, source_target_pairs={{0,8},{1,9},{2,10},{3,11},{4,12},{5,13},{6,14},{7,15},{8,0},{9,1},... | collective-permute-start | bytes 1769480 | tf_op jit(solution)/shard_map/ppermute | solution.py:388
  39.6 27.8 %collective-permute-start.4 = (f32[1152,128]{1,0:T(8,128)}, f32[1152,128]{1,0:T(8,128)}, u32[]{:S(2)}, u32[]{:S(2)}) collective-permute-start(f32[1152,128]{1,0:T(8,128)} %get-tuple-element.54), channel_id=1, source_target_pairs={{0,12},{1,13},{2,14},{3,15},{4,0},{5,1},{6,2},{7,3},{8,4},{9,5},{1... | collective-permute-start | bytes 1769480 | tf_op jit(solution)/shard_map/ppermute | solution.py:388
  50.0 18.1 %collective-permute-start.7 = (bf16[768,512]{1,0:T(8,128)(2,1)}, bf16[768,512]{1,0:T(8,128)(2,1)}, u32[]{:S(2)}, u32[]{:S(2)}) collective-permute-start(bf16[768,512]{1,0:T(8,128)(2,1)} %get-tuple-element.58), channel_id=1, source_target_pairs={{0,32},{16,48},{32,0},{48,16},{64,96},{80,112},{96,64},{112,80},{1... | collective-permute-start | bytes 2359304 | tf_op jit(solution)/shard_map/ppermute | solution.py:405
  59.9 55.4 %all-to-all-start = ((bf16[16,192,512]{2,1,0:T(8,128)(2,1)}), bf16[16,192,512]{2,1,0:T(8,128)(2,1)S(1)}, u32[]{:S(2)}, u32[]{:S(2)}) async-start(bf16[16,192,512]{2,1,0:T(8,128)(2,1)} %bitcast.36), calls=%async_computation | async-start | bytes 6291456 | tf_op jit(solution)/shard_map/all_to_all | solution.py:464
  69.9 15.5 %collective-permute-start.8 = (f32[288,128]{1,0:T(8,128)S(1)}, f32[288,128]{1,0:T(8,128)S(1)}, u32[]{:S(2)}, u32[]{:S(2)}) collective-permute-start(f32[288,128]{1,0:T(8,128)S(1)} %get-tuple-element.64), channel_id=1, source_target_pairs={{0,32},{16,48},{32,64},{48,80},{64,96},{80,112},{96,0},{112,16},{1... | collective-permute-start | bytes 442376 | tf_op jit(solution)/shard_map/ppermute | solution.py:392
  71.7 13.6 %collective-permute-start.9 = (f32[288,128]{1,0:T(8,128)S(1)}, f32[288,128]{1,0:T(8,128)S(1)}, u32[]{:S(2)}, u32[]{:S(2)}) collective-permute-start(f32[288,128]{1,0:T(8,128)S(1)} %get-tuple-element.65), channel_id=1, source_target_pairs={{0,64},{16,80},{32,96},{48,112},{64,0},{80,16},{96,32},{112,48},{1... | collective-permute-start | bytes 442376 | tf_op jit(solution)/shard_map/ppermute | solution.py:392
  75.3 10.1 %collective-permute-start.10 = (f32[288,128]{1,0:T(8,128)S(1)}, f32[288,128]{1,0:T(8,128)S(1)}, u32[]{:S(2)}, u32[]{:S(2)}) collective-permute-start(f32[288,128]{1,0:T(8,128)S(1)} %get-tuple-element.66), channel_id=1, source_target_pairs={{0,96},{16,112},{32,0},{48,16},{64,32},{80,48},{96,64},{112,80},{1... | collective-permute-start | bytes 442376 | tf_op jit(solution)/shard_map/ppermute | solution.py:392
  87.9 19.2 %collective-permute-start.14 = (f32[288,128]{1,0:T(8,128)S(1)}, f32[288,128]{1,0:T(8,128)S(1)}, u32[]{:S(2)}, u32[]{:S(2)}) collective-permute-start(f32[288,128]{1,0:T(8,128)S(1)} %get-tuple-element.89), channel_id=1, source_target_pairs={{0,18},{1,19},{2,16},{3,17},{4,22},{5,23},{6,20},{7,21},{8,26},{9,... | collective-permute-start | bytes 442376 | tf_op jit(solution)/shard_map/ppermute | solution.py:401
  88.8 19.0 %collective-permute-start.13 = (f32[288,128]{1,0:T(8,128)S(1)}, f32[288,128]{1,0:T(8,128)S(1)}, u32[]{:S(2)}, u32[]{:S(2)}) collective-permute-start(f32[288,128]{1,0:T(8,128)S(1)} %get-tuple-element.89), channel_id=1, source_target_pairs={{0,16},{1,17},{2,18},{3,19},{4,20},{5,21},{6,22},{7,23},{8,24},{9,... | collective-permute-start | bytes 442376 | tf_op jit(solution)/shard_map/ppermute | solution.py:401
  91.2 19.1 %collective-permute-start.12 = (f32[288,128]{1,0:T(8,128)S(1)}, f32[288,128]{1,0:T(8,128)S(1)}, u32[]{:S(2)}, u32[]{:S(2)}) collective-permute-start(f32[288,128]{1,0:T(8,128)S(1)} %get-tuple-element.88), channel_id=1, source_target_pairs={{0,2},{1,3},{2,0},{3,1},{4,6},{5,7},{6,4},{7,5},{8,10},{9,11},{10,... | collective-permute-start | bytes 442376 | tf_op jit(solution)/shard_map/ppermute | solution.py:401
  110.4 14.0 %collective-permute-start.15 = (f32[288,128]{1,0:T(8,128)S(1)}, f32[288,128]{1,0:T(8,128)}, u32[]{:S(2)}, u32[]{:S(2)}) collective-permute-start(f32[288,128]{1,0:T(8,128)S(1)} %add_add_fusion.1), channel_id=1, source_target_pairs={{0,8},{1,9},{2,10},{3,11},{4,12},{5,13},{6,14},{7,15},{8,0},{9,1},... | collective-permute-start | bytes 442376 | tf_op jit(solution)/shard_map/ppermute | solution.py:388
  113.2 11.2 %collective-permute-start.16 = (f32[288,128]{1,0:T(8,128)S(1)}, f32[288,128]{1,0:T(8,128)}, u32[]{:S(2)}, u32[]{:S(2)}) collective-permute-start(f32[288,128]{1,0:T(8,128)S(1)} %add_add_fusion.1), channel_id=1, source_target_pairs={{0,12},{1,13},{2,14},{3,15},{4,0},{5,1},{6,2},{7,3},{8,4},{9,5},{1... | collective-permute-start | bytes 442376 | tf_op jit(solution)/shard_map/ppermute | solution.py:388
  113.5 10.9 %collective-permute-start.17 = (f32[288,128]{1,0:T(8,128)S(1)}, f32[288,128]{1,0:T(8,128)}, u32[]{:S(2)}, u32[]{:S(2)}) collective-permute-start(f32[288,128]{1,0:T(8,128)S(1)} %add_add_fusion.1), channel_id=1, source_target_pairs={{0,4},{1,5},{2,6},{3,7},{4,8},{5,9},{6,10},{7,11},{8,12},{9,13},{1... | collective-permute-start | bytes 442376 | tf_op jit(solution)/shard_map/ppermute | solution.py:388
  115.3 48.7 %all-to-all-start.1 = ((bf16[16,192,512]{2,1,0:T(8,128)(2,1)}), bf16[16,192,512]{2,1,0:T(8,128)(2,1)}, u32[]{:S(2)}, u32[]{:S(2)}) async-start(bf16[16,192,512]{2,1,0:T(8,128)(2,1)} %bitcast.37), calls=%async_computation.1 | async-start | bytes 6291456 | tf_op jit(solution)/shard_map/all_to_all | solution.py:483
  125.5 16.2 %collective-permute-start.18 = (f32[4,288,128]{2,1,0:T(8,128)S(1)}, f32[4,288,128]{2,1,0:T(8,128)S(1)}, u32[]{:S(2)}, u32[]{:S(2)}) collective-permute-start(f32[4,288,128]{2,1,0:T(8,128)S(1)} %pad_maximum_fusion.a_ref), channel_id=1, source_target_pairs={{32,0},{34,2},{36,4},{38,6},{40,8},{42,10},{44,12},{46,14},{48,16}... | collective-permute-start | bytes 1769480 | tf_op jit(solution)/shard_map/ppermute | solution.py:417
  126.8 18.6 %collective-permute-start.19 = (f32[4,288,128]{2,1,0:T(8,128)S(1)}, f32[4,288,128]{2,1,0:T(8,128)S(1)}, u32[]{:S(2)}, u32[]{:S(2)}) collective-permute-start(f32[4,288,128]{2,1,0:T(8,128)S(1)} %pad_maximum_fusion.a_ref), channel_id=1, source_target_pairs={{64,0},{66,2},{68,4},{70,6},{72,8},{74,10},{76,12},{78,14},{80,16}... | collective-permute-start | bytes 1769480 | tf_op jit(solution)/shard_map/ppermute | solution.py:417
  132.3 15.9 %collective-permute-start.20 = (f32[4,288,128]{2,1,0:T(8,128)S(1)}, f32[4,288,128]{2,1,0:T(8,128)S(1)}, u32[]{:S(2)}, u32[]{:S(2)}) collective-permute-start(f32[4,288,128]{2,1,0:T(8,128)S(1)} %pad_maximum_fusion.a_ref), channel_id=1, source_target_pairs={{96,0},{98,2},{100,4},{102,6},{104,8},{106,10},{108,12},{110,14},{... | collective-permute-start | bytes 1769480 | tf_op jit(solution)/shard_map/ppermute | solution.py:417
  153.2 4.7 %collective-permute-start.21 = (f32[8,1024]{1,0:T(8,128)S(1)}, f32[8,1024]{1,0:T(8,128)S(1)}, u32[]{:S(2)}, u32[]{:S(2)}) collective-permute-start(f32[8,1024]{1,0:T(8,128)S(1)} %power.1.own_ref), channel_id=1, source_target_pairs={{0,1},{2,3},{4,5},{6,7},{8,9},{10,11},{12,13},{14,15},{16,17},{18,... | collective-permute-start | bytes 98312 | tf_op jit(solution)/shard_map/ppermute | solution.py:422
  155.8 5.2 %collective-permute-start.23 = (f32[8,1024]{1,0:T(8,128)S(1)}, f32[8,1024]{1,0:T(8,128)S(1)}, u32[]{:S(2)}, u32[]{:S(2)}) collective-permute-start(f32[8,1024]{1,0:T(8,128)S(1)} %power.1.own_ref), channel_id=1, source_target_pairs={{0,33},{2,35},{4,37},{6,39},{8,41},{10,43},{12,45},{14,47},{16,49}... | collective-permute-start | bytes 98312 | tf_op jit(solution)/shard_map/ppermute | solution.py:422
  (14 other events, 114.2 us)

commit v6 on v5

--- a/solution.py
+++ b/solution.py
@@ -350,11 +350,27 @@
     out_ref[...] = part_ref[...]
 
 
-def join_second_kernel(part_ref, held_ref, out_ref):
-    out_ref[...] = part_ref[...]
+def join_second_kernel(part_ref, held_ref, out_ref, buffer_ref, in_sem, out_sem):
+    copies = []
+    for i in range(PIECES):
+        here = pl.ds(i * (N_BLK * CAPP // PIECES), N_BLK * CAPP // PIECES)
+        copies.append(
+            (
+                pltpu.make_async_copy(part_ref.at[here], buffer_ref.at[here], in_sem.at[i]),
+                pltpu.make_async_copy(buffer_ref.at[here], out_ref.at[here, pl.ds(HALF, HALF)], out_sem.at[i]),
+            )
+        )
+    for arriving, _ in copies:
+        arriving.start()
+    for arriving, leaving in copies:
+        arriving.wait()
+        leaving.start()
+    for _, leaving in copies:
+        leaving.wait()
 
 
 JOIN = 1024
+PIECES = 8
 
 
 def join_first(left):
@@ -373,10 +389,14 @@
 def join_second(right, held):
     return pl.pallas_call(
         join_second_kernel,
-        grid=(N_BLK * CAPP // JOIN,),
-        in_specs=[pl.BlockSpec((JOIN, HALF), lambda i: (i, 0)), ANY],
-        out_specs=pl.BlockSpec((JOIN, HALF), lambda i: (i, 1)),
+        in_specs=[ANY, ANY],
+        out_specs=ANY,
         out_shape=shape_of((N_BLK * CAPP, D), BF16),
+        scratch_shapes=[
+            pltpu.VMEM((N_BLK * CAPP, HALF), BF16),
+            pltpu.SemaphoreType.DMA((PIECES,)),
+            pltpu.SemaphoreType.DMA((PIECES,)),
+        ],
         input_output_aliases={1: 0},
         compiler_params=params(10),
         cost_estimate=cost(5.2),

time: 169 us -> 168 us (level)
  no operation moved by 1% of the time
where the time goes in v6:
time: 168 us; the launch traced here: 167 us
  Pallas kernels  54.2 us (32%)
  starting transfers between devices  53.6 us (32%)
  waiting for transfers between devices  46.2 us (28%)
  other arithmetic  7.05 us (4%)
  local copies, waits for them, and re-layouts  4.72 us (3%)
    ppermute x3, waiting for transfers between devices, along_x(): return lax.ppermute(value, ('cube', 'blk'), pairs)  19 us
    pallas_call x2, Pallas kernels, leaf_pack(): pl.pallas_call(leaf_kernel, grid=(N_BLK * CAPP // SLOTS,), in_specs=[whol...  17 us
    ppermute x3, waiting for transfers between devices, to_worker(): return lax.ppermute(value, ('cube', 'blk'), pairs)  14.3 us
    ppermute x6, starting transfers between devices, along_y(): lax.ppermute(value, 'blk', [(i, (i // 4 + k) % 4 * 4 + i % 4) for i in ra...  10.7 us
    ppermute x6, waiting for transfers between devices, across(): lax.ppermute(value, axis, [(i, i ^ bit) for i in range(lax.axis_size(axis...  9.75 us
    pallas_call x2, Pallas kernels, swap(): pl.pallas_call(swap_kernel, grid=(1,), in_specs=[whole((24, ROWS)), pl.Bl...  9.17 us
    ppermute x3, starting transfers between devices, to_worker(): return lax.ppermute(value, ('cube', 'blk'), pairs)  8.27 us
    pallas_call x2, Pallas kernels, pack_first(): pl.pallas_call(pack_first_kernel, grid=(1,), in_specs=[pl.BlockSpec((2, R...  7.74 us
  transfers between devices with their start and end apart: 26, of which 11 were waited for; matrix products, arithmetic and copies ran while one was open for 4% of the time, Pallas kernels for 28%

profile of v6, /device:TPU:6, one launch (start us, length us, event | category | flops | bytes accessed | tf_op | source)
XLA Modules:
  0.0 166.9 jit_solution(5076883833582888624)
XLA Ops:
  1.3 4.3 %pack_first.2 = bf16[768,512]{1,0:T(8,128)(2,1)} custom-call(s32[2,1536]{1,0:T(2,128)S(1)} %copy-done.3, bf16[1536,1024]{1,0:T(8,128)(2,1)} %rows_ref.11), custom_call_target="tpu_custom_call" | custom-call | flops 4944999936 | bytes 15867000 | tf_op jit(solution)/shard_map/pack_first/pallas_call | solution.py:91
  6.5 3.4 %pack_first.3 = bf16[768,512]{1,0:T(8,128)(2,1)S(1)} custom-call(s32[2,1536]{1,0:T(2,128)S(1)} %copy-done.4, bf16[1536,1024]{1,0:T(8,128)(2,1)} %rows_ref.11), custom_call_target="tpu_custom_call" | custom-call | flops 4944999936 | bytes 15867000 | tf_op jit(solution)/shard_map/pack_first/pallas_call | solution.py:91
  13.8 6.6 %gram.1 = (f32[4,1152,128]{2,1,0:T(8,128)S(1)}, f32[4,1152,128]{2,1,0:T(8,128)}) custom-call(s32[1]{0:T(128)} %bitcast.7.flip_ref, s32[2,1536]{1,0:T(2,128)S(1)} %copy-done.4, bf16[1536,1024]{1,0:T(8,128)(2,1)S(1)} %copy-done), custom_call_target="tpu_custom_call" | custom-call | flops 9889999872 | bytes 31734000 | tf_op jit(solution)/shard_map/gram/pallas_call | solution.py:224
  20.4 4.8 %collective-permute-done.arrived_ref = bf16[768,512]{1,0:T(8,128)(2,1)S(1)} collective-permute-done((bf16[768,512]{1,0:T(8,128)(2,1)}, bf16[768,512]{1,0:T(8,128)(2,1)S(1)}, u32[]{:S(2)}, u32[]{:S(2)}) %collective-permute-start) | collective-permute-done | bytes 786464 | tf_op jit(solution)/shard_map/ppermute | solution.py:425
  26.0 4.1 %swap.2 = (bf16[1536,512]{1,0:T(8,128)(2,1)S(1)}, bf16[768,512]{1,0:T(8,128)(2,1)S(1)}) custom-call(f32[24,1536]{1,0:T(8,128)S(1)} %slots.1.row_ref, bf16[1536,1024]{1,0:T(8,128)(2,1)} %rows_ref.11, bf16[768,512]{1,0:T(8,128)(2,1)S(1)} %collective-permute-done.arrived_ref), custom_call_target="tpu_custom_call" | custom-call | flops 23000000512 | bytes 73800000 | tf_op jit(solution)/shard_map/swap/pallas_call | solution.py:151
  32.1 3.1 %add_bitcast_fusion = (f32[1152,128]{1,0:T(8,128)}, f32[1152,128]{1,0:T(8,128)}, f32[1152,128]{1,0:T(8,128)}, f32[1152,128]{1,0:T(8,128)}) fusion(f32[4,1152,128]{2,1,0:T(8,128)} %collective-permute-done.1, s32[]{:T(128)S(6)} %select_n.124, f32[4,1152,128]{2,1,0:T(8,128)S(1)} %get-tuple-element.45, s32[]{:T(128)S(6)} %select_n.122, s32[]{:T(128)S(6)} %select_n.120, ...), kind=kLoop, calls=%fused_computation.2 | loop fusion | flops 589824 | bytes 7077904 | tf_op jit(solution)/shard_map/add | solution.py:474
  36.7 2.9 %collective-permute-start.3 = (f32[1152,128]{1,0:T(8,128)}, f32[1152,128]{1,0:T(8,128)}, u32[]{:S(2)}, u32[]{:S(2)}) collective-permute-start(f32[1152,128]{1,0:T(8,128)} %get-tuple-element.53), channel_id=1, source_target_pairs={{0,8},{1,9},{2,10},{3,11},{4,12},{5,13},{6,14},{7,15},{8,0},{9,1},... | collective-permute-start | bytes 1769480 | tf_op jit(solution)/shard_map/ppermute | solution.py:408
  41.0 2.8 %collective-permute-done.6.arrived_ref = bf16[768,512]{1,0:T(8,128)(2,1)S(1)} collective-permute-done((bf16[768,512]{1,0:T(8,128)(2,1)}, bf16[768,512]{1,0:T(8,128)(2,1)S(1)}, u32[]{:S(2)}, u32[]{:S(2)}) %collective-permute-start.6) | collective-permute-done | bytes 786464 | tf_op jit(solution)/shard_map/ppermute | solution.py:425
  43.8 5.1 %swap.3 = (bf16[1536,512]{1,0:T(8,128)(2,1)S(1)}, bf16[768,512]{1,0:T(8,128)(2,1)}) custom-call(f32[24,1536]{1,0:T(8,128)S(1)} %slots.1.row_ref, bf16[1536,1024]{1,0:T(8,128)(2,1)} %rows_ref.11, bf16[768,512]{1,0:T(8,128)(2,1)S(1)} %collective-permute-done.6.arrived_ref), custom_call_target="tpu_custom_call" | custom-call | flops 6095000064 | bytes 19557000 | tf_op jit(solution)/shard_map/swap/pallas_call | solution.py:151
  52.0 7.9 %leaf_pack.2 = bf16[3072,512]{1,0:T(8,128)(2,1)} custom-call(f32[24,1536]{1,0:T(8,128)S(1)} %slots.1.row_ref, bf16[1536,512]{1,0:T(8,128)(2,1)S(1)} %get-tuple-element.55.rows_ref.left_ref, bf16[768,512]{1,0:T(8,128)(2,1)S(1)} %collective-permute-done.5.arrived_ref), custom_call_target="tpu_custom_call" | custom-call | flops 11269999616 | bytes 36162000 | tf_op jit(solution)/shard_map/leaf_pack/pallas_call | solution.py:183
  59.9 7.5 %all-to-all-start = ((bf16[16,192,512]{2,1,0:T(8,128)(2,1)}), bf16[16,192,512]{2,1,0:T(8,128)(2,1)S(1)}, u32[]{:S(2)}, u32[]{:S(2)}) async-start(bf16[16,192,512]{2,1,0:T(8,128)(2,1)} %bitcast.36), calls=%async_computation | async-start | bytes 6291456 | tf_op jit(solution)/shard_map/all_to_all | solution.py:484
  71.7 3.6 %collective-permute-start.9 = (f32[288,128]{1,0:T(8,128)S(1)}, f32[288,128]{1,0:T(8,128)S(1)}, u32[]{:S(2)}, u32[]{:S(2)}) collective-permute-start(f32[288,128]{1,0:T(8,128)S(1)} %get-tuple-element.65), channel_id=1, source_target_pairs={{0,64},{16,80},{32,96},{48,112},{64,0},{80,16},{96,32},{112,48},{1... | collective-permute-start | bytes 442376 | tf_op jit(solution)/shard_map/ppermute | solution.py:412
  76.3 9.0 %leaf_pack.3 = bf16[3072,512]{1,0:T(8,128)(2,1)} custom-call(f32[24,1536]{1,0:T(8,128)S(1)} %slots.1.row_ref, bf16[1536,512]{1,0:T(8,128)(2,1)S(1)} %copy-done.10, bf16[768,512]{1,0:T(8,128)(2,1)} %collective-permute-done.7.arrived_ref), custom_call_target="tpu_custom_call" | custom-call | flops 11269999616 | bytes 36162000 | tf_op jit(solution)/shard_map/leaf_pack/pallas_call | solution.py:183
  91.4 15.7 %collective-permute-done.14 = f32[288,128]{1,0:T(8,128)S(1)} collective-permute-done((f32[288,128]{1,0:T(8,128)S(1)}, f32[288,128]{1,0:T(8,128)S(1)}, u32[]{:S(2)}, u32[]{:S(2)}) %collective-permute-start.14) | collective-permute-done | bytes 147488 | tf_op jit(solution)/shard_map/ppermute | solution.py:421
  110.4 2.8 %collective-permute-start.15 = (f32[288,128]{1,0:T(8,128)S(1)}, f32[288,128]{1,0:T(8,128)}, u32[]{:S(2)}, u32[]{:S(2)}) collective-permute-start(f32[288,128]{1,0:T(8,128)S(1)} %add_add_fusion.1), channel_id=1, source_target_pairs={{0,8},{1,9},{2,10},{3,11},{4,12},{5,13},{6,14},{7,15},{8,0},{9,1},... | collective-permute-start | bytes 442376 | tf_op jit(solution)/shard_map/ppermute | solution.py:408
  115.3 7.0 %all-to-all-start.1 = ((bf16[16,192,512]{2,1,0:T(8,128)(2,1)}), bf16[16,192,512]{2,1,0:T(8,128)(2,1)}, u32[]{:S(2)}, u32[]{:S(2)}) async-start(bf16[16,192,512]{2,1,0:T(8,128)(2,1)} %bitcast.37), calls=%async_computation.1 | async-start | bytes 6291456 | tf_op jit(solution)/shard_map/all_to_all | solution.py:503
  126.8 5.5 %collective-permute-start.19 = (f32[4,288,128]{2,1,0:T(8,128)S(1)}, f32[4,288,128]{2,1,0:T(8,128)S(1)}, u32[]{:S(2)}, u32[]{:S(2)}) collective-permute-start(f32[4,288,128]{2,1,0:T(8,128)S(1)} %pad_maximum_fusion.a_ref), channel_id=1, source_target_pairs={{64,0},{66,2},{68,4},{70,6},{72,8},{74,10},{76,12},{78,14},{80,16}... | collective-permute-start | bytes 1769480 | tf_op jit(solution)/shard_map/ppermute | solution.py:437
  133.9 7.8 %collective-permute-done.18.b_ref = f32[4,288,128]{2,1,0:T(8,128)S(1)} collective-permute-done((f32[4,288,128]{2,1,0:T(8,128)S(1)}, f32[4,288,128]{2,1,0:T(8,128)S(1)}, u32[]{:S(2)}, u32[]{:S(2)}) %collective-permute-start.18) | collective-permute-done | bytes 589856 | tf_op jit(solution)/shard_map/ppermute | solution.py:437
  141.7 3.7 %collective-permute-done.19.c_ref = f32[4,288,128]{2,1,0:T(8,128)S(1)} collective-permute-done((f32[4,288,128]{2,1,0:T(8,128)S(1)}, f32[4,288,128]{2,1,0:T(8,128)S(1)}, u32[]{:S(2)}, u32[]{:S(2)}) %collective-permute-start.19) | collective-permute-done | bytes 589856 | tf_op jit(solution)/shard_map/ppermute | solution.py:437
  145.4 2.8 %collective-permute-done.20.d_ref = f32[4,288,128]{2,1,0:T(8,128)S(1)} collective-permute-done((f32[4,288,128]{2,1,0:T(8,128)S(1)}, f32[4,288,128]{2,1,0:T(8,128)S(1)}, u32[]{:S(2)}, u32[]{:S(2)}) %collective-permute-start.20) | collective-permute-done | bytes 589856 | tf_op jit(solution)/shard_map/ppermute | solution.py:437
  148.3 4.9 %power.1.own_ref = f32[8,1024]{1,0:T(8,128)S(1)} custom-call(s32[2]{0:T(128)S(1)} %pad_add_fusion.1.place_ref, f32[1]{0:T(128)} %bitcast.4.members_ref, f32[1,1024]{1,0:T(1,128)S(1)} %bitcast.35, f32[4,288,128]{2,1,0:T(8,128)S(1)} %pad_maximum_fusion.a_ref, f32[4,288,128]{2,1,0:T(8,128)S(1)} %collective-permute-done.18.b_ref, ...), custom_call_target="tpu_custom_call" | custom-call | flops 7590000128 | bytes 24354000 | tf_op jit(solution)/shard_map/power/pallas_call | solution.py:292
  157.8 3.2 %collective-permute-done.23.both_ref = f32[8,1024]{1,0:T(8,128)S(1)} collective-permute-done((f32[8,1024]{1,0:T(8,128)S(1)}, f32[8,1024]{1,0:T(8,128)S(1)}, u32[]{:S(2)}, u32[]{:S(2)}) %collective-permute-start.23) | collective-permute-done | bytes 32800 | tf_op jit(solution)/shard_map/ppermute | solution.py:442
  161.0 2.9 %scores.1 = f32[2,1536]{1,0:T(2,128)} custom-call(s32[2]{0:T(128)S(1)} %pad_add_fusion.flags_ref, f32[8,1024]{1,0:T(8,128)S(1)} %power.1.own_ref, f32[8,1024]{1,0:T(8,128)S(1)} %collective-permute-done.21.core_ref, f32[8,1024]{1,0:T(8,128)S(1)} %collective-permute-done.22.z_ref, f32[8,1024]{1,0:T(8,128)S(1)} %collective-permute-done.23.both_ref, ...), custom_call_target="tpu_custom_call" | custom-call | flops 5980000256 | bytes 19188000 | tf_op jit(solution)/shard_map/scores/pallas_call | solution.py:338
  163.9 2.8 %join_second.1 = bf16[3072,1024]{1,0:T(8,128)(2,1)} custom-call(bf16[3072,512]{1,0:T(8,128)(2,1)} %bitcast.24.part_ref, bf16[3072,1024]{1,0:T(8,128)(2,1)} %join_first.1.held_ref), custom_call_target="tpu_custom_call", output_to_operand_aliasing={{}: (1, {})} | custom-call | flops 5980000256 | bytes 19188000 | tf_op jit(solution)/shard_map/join_second/pallas_call | solution.py:390
  (73 shorter events, 41.6 us)
Async XLA Ops:
  5.7 19.5 %collective-permute-start = (bf16[768,512]{1,0:T(8,128)(2,1)}, bf16[768,512]{1,0:T(8,128)(2,1)S(1)}, u32[]{:S(2)}, u32[]{:S(2)}) collective-permute-start(bf16[768,512]{1,0:T(8,128)(2,1)} %pack_first.2), channel_id=1, source_target_pairs={{0,16},{16,0},{32,48},{48,32},{64,80},{80,64},{96,112},{112,96},{1... | collective-permute-start | bytes 2359304 | tf_op jit(solution)/shard_map/ppermute | solution.py:425
  20.4 11.7 %collective-permute-start.1 = (f32[4,1152,128]{2,1,0:T(8,128)}, f32[4,1152,128]{2,1,0:T(8,128)}, u32[]{:S(2)}, u32[]{:S(2)}) collective-permute-start(f32[4,1152,128]{2,1,0:T(8,128)} %get-tuple-element.46), channel_id=1, source_target_pairs={{0,1},{1,0},{2,3},{3,2},{4,5},{5,4},{6,7},{7,6},{8,9},{9,8},{10,11... | collective-permute-start | bytes 7077896 | tf_op jit(solution)/shard_map/ppermute | solution.py:425
  25.2 18.6 %collective-permute-start.6 = (bf16[768,512]{1,0:T(8,128)(2,1)}, bf16[768,512]{1,0:T(8,128)(2,1)S(1)}, u32[]{:S(2)}, u32[]{:S(2)}) collective-permute-start(bf16[768,512]{1,0:T(8,128)(2,1)} %copy-done.2), channel_id=1, source_target_pairs={{0,16},{16,0},{32,48},{48,32},{64,80},{80,64},{96,112},{112,96},{1... | collective-permute-start | bytes 2359304 | tf_op jit(solution)/shard_map/ppermute | solution.py:425
  30.1 21.9 %collective-permute-start.5 = (bf16[768,512]{1,0:T(8,128)(2,1)S(1)}, bf16[768,512]{1,0:T(8,128)(2,1)S(1)}, u32[]{:S(2)}, u32[]{:S(2)}) collective-permute-start(bf16[768,512]{1,0:T(8,128)(2,1)S(1)} %get-tuple-element.49), channel_id=1, source_target_pairs={{0,32},{16,48},{32,0},{48,16},{64,96},{80,112},{96,64},{112,80},{1... | collective-permute-start | bytes 2359304 | tf_op jit(solution)/shard_map/ppermute | solution.py:425
  35.1 32.2 %collective-permute-start.2 = (f32[1152,128]{1,0:T(8,128)}, f32[1152,128]{1,0:T(8,128)}, u32[]{:S(2)}, u32[]{:S(2)}) collective-permute-start(f32[1152,128]{1,0:T(8,128)} %get-tuple-element.52), channel_id=1, source_target_pairs={{0,4},{1,5},{2,6},{3,7},{4,8},{5,9},{6,10},{7,11},{8,12},{9,13},{1... | collective-permute-start | bytes 1769480 | tf_op jit(solution)/shard_map/ppermute | solution.py:408
  36.7 30.7 %collective-permute-start.3 = (f32[1152,128]{1,0:T(8,128)}, f32[1152,128]{1,0:T(8,128)}, u32[]{:S(2)}, u32[]{:S(2)}) collective-permute-start(f32[1152,128]{1,0:T(8,128)} %get-tuple-element.53), channel_id=1, source_target_pairs={{0,8},{1,9},{2,10},{3,11},{4,12},{5,13},{6,14},{7,15},{8,0},{9,1},... | collective-permute-start | bytes 1769480 | tf_op jit(solution)/shard_map/ppermute | solution.py:408
  39.6 27.8 %collective-permute-start.4 = (f32[1152,128]{1,0:T(8,128)}, f32[1152,128]{1,0:T(8,128)}, u32[]{:S(2)}, u32[]{:S(2)}) collective-permute-start(f32[1152,128]{1,0:T(8,128)} %get-tuple-element.54), channel_id=1, source_target_pairs={{0,12},{1,13},{2,14},{3,15},{4,0},{5,1},{6,2},{7,3},{8,4},{9,5},{1... | collective-permute-start | bytes 1769480 | tf_op jit(solution)/shard_map/ppermute | solution.py:408
  50.0 18.1 %collective-permute-start.7 = (bf16[768,512]{1,0:T(8,128)(2,1)}, bf16[768,512]{1,0:T(8,128)(2,1)}, u32[]{:S(2)}, u32[]{:S(2)}) collective-permute-start(bf16[768,512]{1,0:T(8,128)(2,1)} %get-tuple-element.58), channel_id=1, source_target_pairs={{0,32},{16,48},{32,0},{48,16},{64,96},{80,112},{96,64},{112,80},{1... | collective-permute-start | bytes 2359304 | tf_op jit(solution)/shard_map/ppermute | solution.py:425
  59.9 55.4 %all-to-all-start = ((bf16[16,192,512]{2,1,0:T(8,128)(2,1)}), bf16[16,192,512]{2,1,0:T(8,128)(2,1)S(1)}, u32[]{:S(2)}, u32[]{:S(2)}) async-start(bf16[16,192,512]{2,1,0:T(8,128)(2,1)} %bitcast.36), calls=%async_computation | async-start | bytes 6291456 | tf_op jit(solution)/shard_map/all_to_all | solution.py:484
  69.9 15.5 %collective-permute-start.8 = (f32[288,128]{1,0:T(8,128)S(1)}, f32[288,128]{1,0:T(8,128)S(1)}, u32[]{:S(2)}, u32[]{:S(2)}) collective-permute-start(f32[288,128]{1,0:T(8,128)S(1)} %get-tuple-element.64), channel_id=1, source_target_pairs={{0,32},{16,48},{32,64},{48,80},{64,96},{80,112},{96,0},{112,16},{1... | collective-permute-start | bytes 442376 | tf_op jit(solution)/shard_map/ppermute | solution.py:412
  71.7 13.6 %collective-permute-start.9 = (f32[288,128]{1,0:T(8,128)S(1)}, f32[288,128]{1,0:T(8,128)S(1)}, u32[]{:S(2)}, u32[]{:S(2)}) collective-permute-start(f32[288,128]{1,0:T(8,128)S(1)} %get-tuple-element.65), channel_id=1, source_target_pairs={{0,64},{16,80},{32,96},{48,112},{64,0},{80,16},{96,32},{112,48},{1... | collective-permute-start | bytes 442376 | tf_op jit(solution)/shard_map/ppermute | solution.py:412
  75.3 10.1 %collective-permute-start.10 = (f32[288,128]{1,0:T(8,128)S(1)}, f32[288,128]{1,0:T(8,128)S(1)}, u32[]{:S(2)}, u32[]{:S(2)}) collective-permute-start(f32[288,128]{1,0:T(8,128)S(1)} %get-tuple-element.66), channel_id=1, source_target_pairs={{0,96},{16,112},{32,0},{48,16},{64,32},{80,48},{96,64},{112,80},{1... | collective-permute-start | bytes 442376 | tf_op jit(solution)/shard_map/ppermute | solution.py:412
  87.9 19.2 %collective-permute-start.14 = (f32[288,128]{1,0:T(8,128)S(1)}, f32[288,128]{1,0:T(8,128)S(1)}, u32[]{:S(2)}, u32[]{:S(2)}) collective-permute-start(f32[288,128]{1,0:T(8,128)S(1)} %get-tuple-element.89), channel_id=1, source_target_pairs={{0,18},{1,19},{2,16},{3,17},{4,22},{5,23},{6,20},{7,21},{8,26},{9,... | collective-permute-start | bytes 442376 | tf_op jit(solution)/shard_map/ppermute | solution.py:421
  88.8 19.0 %collective-permute-start.13 = (f32[288,128]{1,0:T(8,128)S(1)}, f32[288,128]{1,0:T(8,128)S(1)}, u32[]{:S(2)}, u32[]{:S(2)}) collective-permute-start(f32[288,128]{1,0:T(8,128)S(1)} %get-tuple-element.89), channel_id=1, source_target_pairs={{0,16},{1,17},{2,18},{3,19},{4,20},{5,21},{6,22},{7,23},{8,24},{9,... | collective-permute-start | bytes 442376 | tf_op jit(solution)/shard_map/ppermute | solution.py:421
  91.2 19.1 %collective-permute-start.12 = (f32[288,128]{1,0:T(8,128)S(1)}, f32[288,128]{1,0:T(8,128)S(1)}, u32[]{:S(2)}, u32[]{:S(2)}) collective-permute-start(f32[288,128]{1,0:T(8,128)S(1)} %get-tuple-element.88), channel_id=1, source_target_pairs={{0,2},{1,3},{2,0},{3,1},{4,6},{5,7},{6,4},{7,5},{8,10},{9,11},{10,... | collective-permute-start | bytes 442376 | tf_op jit(solution)/shard_map/ppermute | solution.py:421
  110.4 14.0 %collective-permute-start.15 = (f32[288,128]{1,0:T(8,128)S(1)}, f32[288,128]{1,0:T(8,128)}, u32[]{:S(2)}, u32[]{:S(2)}) collective-permute-start(f32[288,128]{1,0:T(8,128)S(1)} %add_add_fusion.1), channel_id=1, source_target_pairs={{0,8},{1,9},{2,10},{3,11},{4,12},{5,13},{6,14},{7,15},{8,0},{9,1},... | collective-permute-start | bytes 442376 | tf_op jit(solution)/shard_map/ppermute | solution.py:408
  113.2 11.2 %collective-permute-start.16 = (f32[288,128]{1,0:T(8,128)S(1)}, f32[288,128]{1,0:T(8,128)}, u32[]{:S(2)}, u32[]{:S(2)}) collective-permute-start(f32[288,128]{1,0:T(8,128)S(1)} %add_add_fusion.1), channel_id=1, source_target_pairs={{0,12},{1,13},{2,14},{3,15},{4,0},{5,1},{6,2},{7,3},{8,4},{9,5},{1... | collective-permute-start | bytes 442376 | tf_op jit(solution)/shard_map/ppermute | solution.py:408
  113.5 10.9 %collective-permute-start.17 = (f32[288,128]{1,0:T(8,128)S(1)}, f32[288,128]{1,0:T(8,128)}, u32[]{:S(2)}, u32[]{:S(2)}) collective-permute-start(f32[288,128]{1,0:T(8,128)S(1)} %add_add_fusion.1), channel_id=1, source_target_pairs={{0,4},{1,5},{2,6},{3,7},{4,8},{5,9},{6,10},{7,11},{8,12},{9,13},{1... | collective-permute-start | bytes 442376 | tf_op jit(solution)/shard_map/ppermute | solution.py:408
  115.3 48.7 %all-to-all-start.1 = ((bf16[16,192,512]{2,1,0:T(8,128)(2,1)}), bf16[16,192,512]{2,1,0:T(8,128)(2,1)}, u32[]{:S(2)}, u32[]{:S(2)}) async-start(bf16[16,192,512]{2,1,0:T(8,128)(2,1)} %bitcast.37), calls=%async_computation.1 | async-start | bytes 6291456 | tf_op jit(solution)/shard_map/all_to_all | solution.py:503
  125.5 16.2 %collective-permute-start.18 = (f32[4,288,128]{2,1,0:T(8,128)S(1)}, f32[4,288,128]{2,1,0:T(8,128)S(1)}, u32[]{:S(2)}, u32[]{:S(2)}) collective-permute-start(f32[4,288,128]{2,1,0:T(8,128)S(1)} %pad_maximum_fusion.a_ref), channel_id=1, source_target_pairs={{32,0},{34,2},{36,4},{38,6},{40,8},{42,10},{44,12},{46,14},{48,16}... | collective-permute-start | bytes 1769480 | tf_op jit(solution)/shard_map/ppermute | solution.py:437
  126.8 18.6 %collective-permute-start.19 = (f32[4,288,128]{2,1,0:T(8,128)S(1)}, f32[4,288,128]{2,1,0:T(8,128)S(1)}, u32[]{:S(2)}, u32[]{:S(2)}) collective-permute-start(f32[4,288,128]{2,1,0:T(8,128)S(1)} %pad_maximum_fusion.a_ref), channel_id=1, source_target_pairs={{64,0},{66,2},{68,4},{70,6},{72,8},{74,10},{76,12},{78,14},{80,16}... | collective-permute-start | bytes 1769480 | tf_op jit(solution)/shard_map/ppermute | solution.py:437
  132.3 15.9 %collective-permute-start.20 = (f32[4,288,128]{2,1,0:T(8,128)S(1)}, f32[4,288,128]{2,1,0:T(8,128)S(1)}, u32[]{:S(2)}, u32[]{:S(2)}) collective-permute-start(f32[4,288,128]{2,1,0:T(8,128)S(1)} %pad_maximum_fusion.a_ref), channel_id=1, source_target_pairs={{96,0},{98,2},{100,4},{102,6},{104,8},{106,10},{108,12},{110,14},{... | collective-permute-start | bytes 1769480 | tf_op jit(solution)/shard_map/ppermute | solution.py:437
  153.2 4.7 %collective-permute-start.21 = (f32[8,1024]{1,0:T(8,128)S(1)}, f32[8,1024]{1,0:T(8,128)S(1)}, u32[]{:S(2)}, u32[]{:S(2)}) collective-permute-start(f32[8,1024]{1,0:T(8,128)S(1)} %power.1.own_ref), channel_id=1, source_target_pairs={{0,1},{2,3},{4,5},{6,7},{8,9},{10,11},{12,13},{14,15},{16,17},{18,... | collective-permute-start | bytes 98312 | tf_op jit(solution)/shard_map/ppermute | solution.py:442
  155.8 5.2 %collective-permute-start.23 = (f32[8,1024]{1,0:T(8,128)S(1)}, f32[8,1024]{1,0:T(8,128)S(1)}, u32[]{:S(2)}, u32[]{:S(2)}) collective-permute-start(f32[8,1024]{1,0:T(8,128)S(1)} %power.1.own_ref), channel_id=1, source_target_pairs={{0,33},{2,35},{4,37},{6,39},{8,41},{10,43},{12,45},{14,47},{16,49}... | collective-permute-start | bytes 98312 | tf_op jit(solution)/shard_map/ppermute | solution.py:442
  (14 other events, 114.2 us)

commit v7 on v6

--- a/solution.py
+++ b/solution.py
@@ -153,7 +153,7 @@
         grid=(1,),
         in_specs=[whole((24, ROWS)), pl.BlockSpec((ROWS, HALF), lambda i: (0, half)), whole((CAP, HALF))],
         out_specs=[whole((ROWS, HALF)), whole((CAP, HALF))],
-        out_shape=[shape_of((ROWS, HALF), BF16), shape_of((CAP, HALF), BF16)],
+        out_shape=[(shape_of if half == 0 else pltpu.HBM)((ROWS, HALF), BF16), shape_of((CAP, HALF), BF16)],
         scratch_shapes=[pltpu.VMEM((ROWS, LANES), F32)],
         compiler_params=params(12),
         cost_estimate=cost(20.0 if half == 0 else 5.3),

time: 168 us -> 167 us (level)
    unnamed x24 -> x22, local copies, waits for them, and re-layouts: 4.66 us -> 3.51 us
  transfers between devices with their start and end apart: 26 -> 26, of which waited for: 11 -> 11; matrix products, arithmetic and copies ran while one was open for 4% -> 4% of each run, Pallas kernels for 28% -> 29%
where the time goes in v7:
time: 167 us; the launch traced here: 166 us
  Pallas kernels  54.6 us (33%)
  starting transfers between devices  53.6 us (32%)
  waiting for transfers between devices  46.3 us (28%)
  other arithmetic  7.04 us (4%)
  local copies, waits for them, and re-layouts  3.56 us (2%)
    ppermute x3, waiting for transfers between devices, along_x(): return lax.ppermute(value, ('cube', 'blk'), pairs)  18.9 us
    pallas_call x2, Pallas kernels, leaf_pack(): pl.pallas_call(leaf_kernel, grid=(N_BLK * CAPP // SLOTS,), in_specs=[whol...  17 us
    ppermute x3, waiting for transfers between devices, to_worker(): return lax.ppermute(value, ('cube', 'blk'), pairs)  14.3 us
    ppermute x6, starting transfers between devices, along_y(): lax.ppermute(value, 'blk', [(i, (i // 4 + k) % 4 * 4 + i % 4) for i in ra...  10.7 us
    ppermute x6, waiting for transfers between devices, across(): lax.ppermute(value, axis, [(i, i ^ bit) for i in range(lax.axis_size(axis...  9.77 us
    pallas_call x2, Pallas kernels, swap(): pl.pallas_call(swap_kernel, grid=(1,), in_specs=[whole((24, ROWS)), pl.Bl...  9.51 us
    ppermute x3, starting transfers between devices, to_worker(): return lax.ppermute(value, ('cube', 'blk'), pairs)  8.29 us
    pallas_call x2, Pallas kernels, pack_first(): pl.pallas_call(pack_first_kernel, grid=(1,), in_specs=[pl.BlockSpec((2, R...  7.75 us
  transfers between devices with their start and end apart: 26, of which 11 were waited for; matrix products, arithmetic and copies ran while one was open for 4% of the time, Pallas kernels for 29%

profile of v7, /device:TPU:6, one launch (start us, length us, event | category | flops | bytes accessed | tf_op | source)
XLA Modules:
  0.0 166.1 jit_solution(1346404308862597226)
XLA Ops:
  1.3 4.3 %pack_first.2 = bf16[768,512]{1,0:T(8,128)(2,1)} custom-call(s32[2,1536]{1,0:T(2,128)S(1)} %copy-done.3, bf16[1536,1024]{1,0:T(8,128)(2,1)} %rows_ref.11), custom_call_target="tpu_custom_call" | custom-call | flops 4944999936 | bytes 15867000 | tf_op jit(solution)/shard_map/pack_first/pallas_call | solution.py:91
  6.5 3.4 %pack_first.3 = bf16[768,512]{1,0:T(8,128)(2,1)S(1)} custom-call(s32[2,1536]{1,0:T(2,128)S(1)} %copy-done.4, bf16[1536,1024]{1,0:T(8,128)(2,1)} %rows_ref.11), custom_call_target="tpu_custom_call" | custom-call | flops 4944999936 | bytes 15867000 | tf_op jit(solution)/shard_map/pack_first/pallas_call | solution.py:91
  13.8 6.5 %gram.1 = (f32[4,1152,128]{2,1,0:T(8,128)S(1)}, f32[4,1152,128]{2,1,0:T(8,128)}) custom-call(s32[1]{0:T(128)} %bitcast.7.flip_ref, s32[2,1536]{1,0:T(2,128)S(1)} %copy-done.4, bf16[1536,1024]{1,0:T(8,128)(2,1)S(1)} %copy-done), custom_call_target="tpu_custom_call" | custom-call | flops 9889999872 | bytes 31734000 | tf_op jit(solution)/shard_map/gram/pallas_call | solution.py:224
  20.4 4.8 %collective-permute-done.arrived_ref = bf16[768,512]{1,0:T(8,128)(2,1)S(1)} collective-permute-done((bf16[768,512]{1,0:T(8,128)(2,1)}, bf16[768,512]{1,0:T(8,128)(2,1)S(1)}, u32[]{:S(2)}, u32[]{:S(2)}) %collective-permute-start) | collective-permute-done | bytes 786464 | tf_op jit(solution)/shard_map/ppermute | solution.py:425
  26.0 4.1 %swap.2 = (bf16[1536,512]{1,0:T(8,128)(2,1)S(1)}, bf16[768,512]{1,0:T(8,128)(2,1)S(1)}) custom-call(f32[24,1536]{1,0:T(8,128)S(1)} %slots.1.row_ref, bf16[1536,1024]{1,0:T(8,128)(2,1)} %rows_ref.11, bf16[768,512]{1,0:T(8,128)(2,1)S(1)} %collective-permute-done.arrived_ref), custom_call_target="tpu_custom_call" | custom-call | flops 23000000512 | bytes 73800000 | tf_op jit(solution)/shard_map/swap/pallas_call | solution.py:151
  32.1 3.1 %add_bitcast_fusion = (f32[1152,128]{1,0:T(8,128)}, f32[1152,128]{1,0:T(8,128)}, f32[1152,128]{1,0:T(8,128)}, f32[1152,128]{1,0:T(8,128)}) fusion(f32[4,1152,128]{2,1,0:T(8,128)} %collective-permute-done.1, s32[]{:T(128)S(6)} %select_n.124, f32[4,1152,128]{2,1,0:T(8,128)S(1)} %get-tuple-element.45, s32[]{:T(128)S(6)} %select_n.122, s32[]{:T(128)S(6)} %select_n.120, ...), kind=kLoop, calls=%fused_computation.2 | loop fusion | flops 589824 | bytes 7077904 | tf_op jit(solution)/shard_map/add | solution.py:474
  36.7 2.9 %collective-permute-start.3 = (f32[1152,128]{1,0:T(8,128)}, f32[1152,128]{1,0:T(8,128)}, u32[]{:S(2)}, u32[]{:S(2)}) collective-permute-start(f32[1152,128]{1,0:T(8,128)} %get-tuple-element.53), channel_id=1, source_target_pairs={{0,8},{1,9},{2,10},{3,11},{4,12},{5,13},{6,14},{7,15},{8,0},{9,1},... | collective-permute-start | bytes 1769480 | tf_op jit(solution)/shard_map/ppermute | solution.py:408
  41.0 2.8 %collective-permute-done.6.arrived_ref = bf16[768,512]{1,0:T(8,128)(2,1)S(1)} collective-permute-done((bf16[768,512]{1,0:T(8,128)(2,1)}, bf16[768,512]{1,0:T(8,128)(2,1)S(1)}, u32[]{:S(2)}, u32[]{:S(2)}) %collective-permute-start.6) | collective-permute-done | bytes 786464 | tf_op jit(solution)/shard_map/ppermute | solution.py:425
  43.8 5.4 %swap.3 = (bf16[1536,512]{1,0:T(8,128)(2,1)}, bf16[768,512]{1,0:T(8,128)(2,1)}) custom-call(f32[24,1536]{1,0:T(8,128)S(1)} %slots.1.row_ref, bf16[1536,1024]{1,0:T(8,128)(2,1)} %rows_ref.11, bf16[768,512]{1,0:T(8,128)(2,1)S(1)} %collective-permute-done.6.arrived_ref), custom_call_target="tpu_custom_call" | custom-call | flops 6095000064 | bytes 19557000 | tf_op jit(solution)/shard_map/swap/pallas_call | solution.py:151
  51.1 7.9 %leaf_pack.2 = bf16[3072,512]{1,0:T(8,128)(2,1)} custom-call(f32[24,1536]{1,0:T(8,128)S(1)} %slots.1.row_ref, bf16[1536,512]{1,0:T(8,128)(2,1)S(1)} %get-tuple-element.55.rows_ref.left_ref, bf16[768,512]{1,0:T(8,128)(2,1)S(1)} %collective-permute-done.5.arrived_ref), custom_call_target="tpu_custom_call" | custom-call | flops 11269999616 | bytes 36162000 | tf_op jit(solution)/shard_map/leaf_pack/pallas_call | solution.py:183
  59.1 7.5 %all-to-all-start = ((bf16[16,192,512]{2,1,0:T(8,128)(2,1)}), bf16[16,192,512]{2,1,0:T(8,128)(2,1)S(1)}, u32[]{:S(2)}, u32[]{:S(2)}) async-start(bf16[16,192,512]{2,1,0:T(8,128)(2,1)} %bitcast.36), calls=%async_computation | async-start | bytes 6291456 | tf_op jit(solution)/shard_map/all_to_all | solution.py:484
  70.9 3.6 %collective-permute-start.9 = (f32[288,128]{1,0:T(8,128)S(1)}, f32[288,128]{1,0:T(8,128)S(1)}, u32[]{:S(2)}, u32[]{:S(2)}) collective-permute-start(f32[288,128]{1,0:T(8,128)S(1)} %get-tuple-element.65), channel_id=1, source_target_pairs={{0,64},{16,80},{32,96},{48,112},{64,0},{80,16},{96,32},{112,48},{1... | collective-permute-start | bytes 442376 | tf_op jit(solution)/shard_map/ppermute | solution.py:412
  75.5 9.0 %leaf_pack.3 = bf16[3072,512]{1,0:T(8,128)(2,1)} custom-call(f32[24,1536]{1,0:T(8,128)S(1)} %slots.1.row_ref, bf16[1536,512]{1,0:T(8,128)(2,1)S(1)} %copy-done.9, bf16[768,512]{1,0:T(8,128)(2,1)} %collective-permute-done.7.arrived_ref), custom_call_target="tpu_custom_call" | custom-call | flops 11269999616 | bytes 36162000 | tf_op jit(solution)/shard_map/leaf_pack/pallas_call | solution.py:183
  90.6 15.7 %collective-permute-done.14 = f32[288,128]{1,0:T(8,128)S(1)} collective-permute-done((f32[288,128]{1,0:T(8,128)S(1)}, f32[288,128]{1,0:T(8,128)S(1)}, u32[]{:S(2)}, u32[]{:S(2)}) %collective-permute-start.14) | collective-permute-done | bytes 147488 | tf_op jit(solution)/shard_map/ppermute | solution.py:421
  109.6 2.8 %collective-permute-start.15 = (f32[288,128]{1,0:T(8,128)S(1)}, f32[288,128]{1,0:T(8,128)}, u32[]{:S(2)}, u32[]{:S(2)}) collective-permute-start(f32[288,128]{1,0:T(8,128)S(1)} %add_add_fusion.1), channel_id=1, source_target_pairs={{0,8},{1,9},{2,10},{3,11},{4,12},{5,13},{6,14},{7,15},{8,0},{9,1},... | collective-permute-start | bytes 442376 | tf_op jit(solution)/shard_map/ppermute | solution.py:408
  114.4 7.0 %all-to-all-start.1 = ((bf16[16,192,512]{2,1,0:T(8,128)(2,1)}), bf16[16,192,512]{2,1,0:T(8,128)(2,1)}, u32[]{:S(2)}, u32[]{:S(2)}) async-start(bf16[16,192,512]{2,1,0:T(8,128)(2,1)} %bitcast.37), calls=%async_computation.1 | async-start | bytes 6291456 | tf_op jit(solution)/shard_map/all_to_all | solution.py:503
  126.0 5.5 %collective-permute-start.19 = (f32[4,288,128]{2,1,0:T(8,128)S(1)}, f32[4,288,128]{2,1,0:T(8,128)S(1)}, u32[]{:S(2)}, u32[]{:S(2)}) collective-permute-start(f32[4,288,128]{2,1,0:T(8,128)S(1)} %pad_maximum_fusion.a_ref), channel_id=1, source_target_pairs={{64,0},{66,2},{68,4},{70,6},{72,8},{74,10},{76,12},{78,14},{80,16}... | collective-permute-start | bytes 1769480 | tf_op jit(solution)/shard_map/ppermute | solution.py:437
  133.1 7.8 %collective-permute-done.18.b_ref = f32[4,288,128]{2,1,0:T(8,128)S(1)} collective-permute-done((f32[4,288,128]{2,1,0:T(8,128)S(1)}, f32[4,288,128]{2,1,0:T(8,128)S(1)}, u32[]{:S(2)}, u32[]{:S(2)}) %collective-permute-start.18) | collective-permute-done | bytes 589856 | tf_op jit(solution)/shard_map/ppermute | solution.py:437
  140.9 3.7 %collective-permute-done.19.c_ref = f32[4,288,128]{2,1,0:T(8,128)S(1)} collective-permute-done((f32[4,288,128]{2,1,0:T(8,128)S(1)}, f32[4,288,128]{2,1,0:T(8,128)S(1)}, u32[]{:S(2)}, u32[]{:S(2)}) %collective-permute-start.19) | collective-permute-done | bytes 589856 | tf_op jit(solution)/shard_map/ppermute | solution.py:437
  144.6 2.8 %collective-permute-done.20.d_ref = f32[4,288,128]{2,1,0:T(8,128)S(1)} collective-permute-done((f32[4,288,128]{2,1,0:T(8,128)S(1)}, f32[4,288,128]{2,1,0:T(8,128)S(1)}, u32[]{:S(2)}, u32[]{:S(2)}) %collective-permute-start.20) | collective-permute-done | bytes 589856 | tf_op jit(solution)/shard_map/ppermute | solution.py:437
  147.4 4.9 %power.1.own_ref = f32[8,1024]{1,0:T(8,128)S(1)} custom-call(s32[2]{0:T(128)S(1)} %pad_add_fusion.1.place_ref, f32[1]{0:T(128)} %bitcast.4.members_ref, f32[1,1024]{1,0:T(1,128)S(1)} %bitcast.35, f32[4,288,128]{2,1,0:T(8,128)S(1)} %pad_maximum_fusion.a_ref, f32[4,288,128]{2,1,0:T(8,128)S(1)} %collective-permute-done.18.b_ref, ...), custom_call_target="tpu_custom_call" | custom-call | flops 7590000128 | bytes 24354000 | tf_op jit(solution)/shard_map/power/pallas_call | solution.py:292
  157.0 3.2 %collective-permute-done.23.both_ref = f32[8,1024]{1,0:T(8,128)S(1)} collective-permute-done((f32[8,1024]{1,0:T(8,128)S(1)}, f32[8,1024]{1,0:T(8,128)S(1)}, u32[]{:S(2)}, u32[]{:S(2)}) %collective-permute-start.23) | collective-permute-done | bytes 32800 | tf_op jit(solution)/shard_map/ppermute | solution.py:442
  160.2 2.9 %scores.1 = f32[2,1536]{1,0:T(2,128)} custom-call(s32[2]{0:T(128)S(1)} %pad_add_fusion.flags_ref, f32[8,1024]{1,0:T(8,128)S(1)} %power.1.own_ref, f32[8,1024]{1,0:T(8,128)S(1)} %collective-permute-done.21.core_ref, f32[8,1024]{1,0:T(8,128)S(1)} %collective-permute-done.22.z_ref, f32[8,1024]{1,0:T(8,128)S(1)} %collective-permute-done.23.both_ref, ...), custom_call_target="tpu_custom_call" | custom-call | flops 5980000256 | bytes 19188000 | tf_op jit(solution)/shard_map/scores/pallas_call | solution.py:338
  163.1 2.8 %join_second.1 = bf16[3072,1024]{1,0:T(8,128)(2,1)} custom-call(bf16[3072,512]{1,0:T(8,128)(2,1)} %bitcast.24.part_ref, bf16[3072,1024]{1,0:T(8,128)(2,1)} %join_first.1.held_ref), custom_call_target="tpu_custom_call", output_to_operand_aliasing={{}: (1, {})} | custom-call | flops 5980000256 | bytes 19188000 | tf_op jit(solution)/shard_map/join_second/pallas_call | solution.py:390
  (71 shorter events, 40.5 us)
Async XLA Ops:
  5.7 19.5 %collective-permute-start = (bf16[768,512]{1,0:T(8,128)(2,1)}, bf16[768,512]{1,0:T(8,128)(2,1)S(1)}, u32[]{:S(2)}, u32[]{:S(2)}) collective-permute-start(bf16[768,512]{1,0:T(8,128)(2,1)} %pack_first.2), channel_id=1, source_target_pairs={{0,16},{16,0},{32,48},{48,32},{64,80},{80,64},{96,112},{112,96},{1... | collective-permute-start | bytes 2359304 | tf_op jit(solution)/shard_map/ppermute | solution.py:425
  20.4 11.7 %collective-permute-start.1 = (f32[4,1152,128]{2,1,0:T(8,128)}, f32[4,1152,128]{2,1,0:T(8,128)}, u32[]{:S(2)}, u32[]{:S(2)}) collective-permute-start(f32[4,1152,128]{2,1,0:T(8,128)} %get-tuple-element.46), channel_id=1, source_target_pairs={{0,1},{1,0},{2,3},{3,2},{4,5},{5,4},{6,7},{7,6},{8,9},{9,8},{10,11... | collective-permute-start | bytes 7077896 | tf_op jit(solution)/shard_map/ppermute | solution.py:425
  25.2 18.6 %collective-permute-start.6 = (bf16[768,512]{1,0:T(8,128)(2,1)}, bf16[768,512]{1,0:T(8,128)(2,1)S(1)}, u32[]{:S(2)}, u32[]{:S(2)}) collective-permute-start(bf16[768,512]{1,0:T(8,128)(2,1)} %copy-done.2), channel_id=1, source_target_pairs={{0,16},{16,0},{32,48},{48,32},{64,80},{80,64},{96,112},{112,96},{1... | collective-permute-start | bytes 2359304 | tf_op jit(solution)/shard_map/ppermute | solution.py:425
  30.1 21.1 %collective-permute-start.5 = (bf16[768,512]{1,0:T(8,128)(2,1)S(1)}, bf16[768,512]{1,0:T(8,128)(2,1)S(1)}, u32[]{:S(2)}, u32[]{:S(2)}) collective-permute-start(bf16[768,512]{1,0:T(8,128)(2,1)S(1)} %get-tuple-element.49), channel_id=1, source_target_pairs={{0,32},{16,48},{32,0},{48,16},{64,96},{80,112},{96,64},{112,80},{1... | collective-permute-start | bytes 2359304 | tf_op jit(solution)/shard_map/ppermute | solution.py:425
  35.1 31.4 %collective-permute-start.2 = (f32[1152,128]{1,0:T(8,128)}, f32[1152,128]{1,0:T(8,128)}, u32[]{:S(2)}, u32[]{:S(2)}) collective-permute-start(f32[1152,128]{1,0:T(8,128)} %get-tuple-element.52), channel_id=1, source_target_pairs={{0,4},{1,5},{2,6},{3,7},{4,8},{5,9},{6,10},{7,11},{8,12},{9,13},{1... | collective-permute-start | bytes 1769480 | tf_op jit(solution)/shard_map/ppermute | solution.py:408
  36.7 29.8 %collective-permute-start.3 = (f32[1152,128]{1,0:T(8,128)}, f32[1152,128]{1,0:T(8,128)}, u32[]{:S(2)}, u32[]{:S(2)}) collective-permute-start(f32[1152,128]{1,0:T(8,128)} %get-tuple-element.53), channel_id=1, source_target_pairs={{0,8},{1,9},{2,10},{3,11},{4,12},{5,13},{6,14},{7,15},{8,0},{9,1},... | collective-permute-start | bytes 1769480 | tf_op jit(solution)/shard_map/ppermute | solution.py:408
  39.6 26.9 %collective-permute-start.4 = (f32[1152,128]{1,0:T(8,128)}, f32[1152,128]{1,0:T(8,128)}, u32[]{:S(2)}, u32[]{:S(2)}) collective-permute-start(f32[1152,128]{1,0:T(8,128)} %get-tuple-element.54), channel_id=1, source_target_pairs={{0,12},{1,13},{2,14},{3,15},{4,0},{5,1},{6,2},{7,3},{8,4},{9,5},{1... | collective-permute-start | bytes 1769480 | tf_op jit(solution)/shard_map/ppermute | solution.py:408
  49.2 18.1 %collective-permute-start.7 = (bf16[768,512]{1,0:T(8,128)(2,1)}, bf16[768,512]{1,0:T(8,128)(2,1)}, u32[]{:S(2)}, u32[]{:S(2)}) collective-permute-start(bf16[768,512]{1,0:T(8,128)(2,1)} %get-tuple-element.58), channel_id=1, source_target_pairs={{0,32},{16,48},{32,0},{48,16},{64,96},{80,112},{96,64},{112,80},{1... | collective-permute-start | bytes 2359304 | tf_op jit(solution)/shard_map/ppermute | solution.py:425
  59.1 55.4 %all-to-all-start = ((bf16[16,192,512]{2,1,0:T(8,128)(2,1)}), bf16[16,192,512]{2,1,0:T(8,128)(2,1)S(1)}, u32[]{:S(2)}, u32[]{:S(2)}) async-start(bf16[16,192,512]{2,1,0:T(8,128)(2,1)} %bitcast.36), calls=%async_computation | async-start | bytes 6291456 | tf_op jit(solution)/shard_map/all_to_all | solution.py:484
  69.1 15.4 %collective-permute-start.8 = (f32[288,128]{1,0:T(8,128)S(1)}, f32[288,128]{1,0:T(8,128)S(1)}, u32[]{:S(2)}, u32[]{:S(2)}) collective-permute-start(f32[288,128]{1,0:T(8,128)S(1)} %get-tuple-element.64), channel_id=1, source_target_pairs={{0,32},{16,48},{32,64},{48,80},{64,96},{80,112},{96,0},{112,16},{1... | collective-permute-start | bytes 442376 | tf_op jit(solution)/shard_map/ppermute | solution.py:412
  70.9 13.6 %collective-permute-start.9 = (f32[288,128]{1,0:T(8,128)S(1)}, f32[288,128]{1,0:T(8,128)S(1)}, u32[]{:S(2)}, u32[]{:S(2)}) collective-permute-start(f32[288,128]{1,0:T(8,128)S(1)} %get-tuple-element.65), channel_id=1, source_target_pairs={{0,64},{16,80},{32,96},{48,112},{64,0},{80,16},{96,32},{112,48},{1... | collective-permute-start | bytes 442376 | tf_op jit(solution)/shard_map/ppermute | solution.py:412
  74.5 10.1 %collective-permute-start.10 = (f32[288,128]{1,0:T(8,128)S(1)}, f32[288,128]{1,0:T(8,128)S(1)}, u32[]{:S(2)}, u32[]{:S(2)}) collective-permute-start(f32[288,128]{1,0:T(8,128)S(1)} %get-tuple-element.66), channel_id=1, source_target_pairs={{0,96},{16,112},{32,0},{48,16},{64,32},{80,48},{96,64},{112,80},{1... | collective-permute-start | bytes 442376 | tf_op jit(solution)/shard_map/ppermute | solution.py:412
  87.1 19.2 %collective-permute-start.14 = (f32[288,128]{1,0:T(8,128)S(1)}, f32[288,128]{1,0:T(8,128)S(1)}, u32[]{:S(2)}, u32[]{:S(2)}) collective-permute-start(f32[288,128]{1,0:T(8,128)S(1)} %get-tuple-element.89), channel_id=1, source_target_pairs={{0,18},{1,19},{2,16},{3,17},{4,22},{5,23},{6,20},{7,21},{8,26},{9,... | collective-permute-start | bytes 442376 | tf_op jit(solution)/shard_map/ppermute | solution.py:421
  88.0 19.0 %collective-permute-start.13 = (f32[288,128]{1,0:T(8,128)S(1)}, f32[288,128]{1,0:T(8,128)S(1)}, u32[]{:S(2)}, u32[]{:S(2)}) collective-permute-start(f32[288,128]{1,0:T(8,128)S(1)} %get-tuple-element.89), channel_id=1, source_target_pairs={{0,16},{1,17},{2,18},{3,19},{4,20},{5,21},{6,22},{7,23},{8,24},{9,... | collective-permute-start | bytes 442376 | tf_op jit(solution)/shard_map/ppermute | solution.py:421
  90.4 19.1 %collective-permute-start.12 = (f32[288,128]{1,0:T(8,128)S(1)}, f32[288,128]{1,0:T(8,128)S(1)}, u32[]{:S(2)}, u32[]{:S(2)}) collective-permute-start(f32[288,128]{1,0:T(8,128)S(1)} %get-tuple-element.88), channel_id=1, source_target_pairs={{0,2},{1,3},{2,0},{3,1},{4,6},{5,7},{6,4},{7,5},{8,10},{9,11},{10,... | collective-permute-start | bytes 442376 | tf_op jit(solution)/shard_map/ppermute | solution.py:421
  109.6 14.0 %collective-permute-start.15 = (f32[288,128]{1,0:T(8,128)S(1)}, f32[288,128]{1,0:T(8,128)}, u32[]{:S(2)}, u32[]{:S(2)}) collective-permute-start(f32[288,128]{1,0:T(8,128)S(1)} %add_add_fusion.1), channel_id=1, source_target_pairs={{0,8},{1,9},{2,10},{3,11},{4,12},{5,13},{6,14},{7,15},{8,0},{9,1},... | collective-permute-start | bytes 442376 | tf_op jit(solution)/shard_map/ppermute | solution.py:408
  112.4 11.2 %collective-permute-start.16 = (f32[288,128]{1,0:T(8,128)S(1)}, f32[288,128]{1,0:T(8,128)}, u32[]{:S(2)}, u32[]{:S(2)}) collective-permute-start(f32[288,128]{1,0:T(8,128)S(1)} %add_add_fusion.1), channel_id=1, source_target_pairs={{0,12},{1,13},{2,14},{3,15},{4,0},{5,1},{6,2},{7,3},{8,4},{9,5},{1... | collective-permute-start | bytes 442376 | tf_op jit(solution)/shard_map/ppermute | solution.py:408
  112.7 10.9 %collective-permute-start.17 = (f32[288,128]{1,0:T(8,128)S(1)}, f32[288,128]{1,0:T(8,128)}, u32[]{:S(2)}, u32[]{:S(2)}) collective-permute-start(f32[288,128]{1,0:T(8,128)S(1)} %add_add_fusion.1), channel_id=1, source_target_pairs={{0,4},{1,5},{2,6},{3,7},{4,8},{5,9},{6,10},{7,11},{8,12},{9,13},{1... | collective-permute-start | bytes 442376 | tf_op jit(solution)/shard_map/ppermute | solution.py:408
  114.4 48.7 %all-to-all-start.1 = ((bf16[16,192,512]{2,1,0:T(8,128)(2,1)}), bf16[16,192,512]{2,1,0:T(8,128)(2,1)}, u32[]{:S(2)}, u32[]{:S(2)}) async-start(bf16[16,192,512]{2,1,0:T(8,128)(2,1)} %bitcast.37), calls=%async_computation.1 | async-start | bytes 6291456 | tf_op jit(solution)/shard_map/all_to_all | solution.py:503
  124.7 16.2 %collective-permute-start.18 = (f32[4,288,128]{2,1,0:T(8,128)S(1)}, f32[4,288,128]{2,1,0:T(8,128)S(1)}, u32[]{:S(2)}, u32[]{:S(2)}) collective-permute-start(f32[4,288,128]{2,1,0:T(8,128)S(1)} %pad_maximum_fusion.a_ref), channel_id=1, source_target_pairs={{32,0},{34,2},{36,4},{38,6},{40,8},{42,10},{44,12},{46,14},{48,16}... | collective-permute-start | bytes 1769480 | tf_op jit(solution)/shard_map/ppermute | solution.py:437
  126.0 18.6 %collective-permute-start.19 = (f32[4,288,128]{2,1,0:T(8,128)S(1)}, f32[4,288,128]{2,1,0:T(8,128)S(1)}, u32[]{:S(2)}, u32[]{:S(2)}) collective-permute-start(f32[4,288,128]{2,1,0:T(8,128)S(1)} %pad_maximum_fusion.a_ref), channel_id=1, source_target_pairs={{64,0},{66,2},{68,4},{70,6},{72,8},{74,10},{76,12},{78,14},{80,16}... | collective-permute-start | bytes 1769480 | tf_op jit(solution)/shard_map/ppermute | solution.py:437
  131.5 15.9 %collective-permute-start.20 = (f32[4,288,128]{2,1,0:T(8,128)S(1)}, f32[4,288,128]{2,1,0:T(8,128)S(1)}, u32[]{:S(2)}, u32[]{:S(2)}) collective-permute-start(f32[4,288,128]{2,1,0:T(8,128)S(1)} %pad_maximum_fusion.a_ref), channel_id=1, source_target_pairs={{96,0},{98,2},{100,4},{102,6},{104,8},{106,10},{108,12},{110,14},{... | collective-permute-start | bytes 1769480 | tf_op jit(solution)/shard_map/ppermute | solution.py:437
  152.4 4.7 %collective-permute-start.21 = (f32[8,1024]{1,0:T(8,128)S(1)}, f32[8,1024]{1,0:T(8,128)S(1)}, u32[]{:S(2)}, u32[]{:S(2)}) collective-permute-start(f32[8,1024]{1,0:T(8,128)S(1)} %power.1.own_ref), channel_id=1, source_target_pairs={{0,1},{2,3},{4,5},{6,7},{8,9},{10,11},{12,13},{14,15},{16,17},{18,... | collective-permute-start | bytes 98312 | tf_op jit(solution)/shard_map/ppermute | solution.py:442
  155.0 5.2 %collective-permute-start.23 = (f32[8,1024]{1,0:T(8,128)S(1)}, f32[8,1024]{1,0:T(8,128)S(1)}, u32[]{:S(2)}, u32[]{:S(2)}) collective-permute-start(f32[8,1024]{1,0:T(8,128)S(1)} %power.1.own_ref), channel_id=1, source_target_pairs={{0,33},{2,35},{4,37},{6,39},{8,41},{10,43},{12,45},{14,47},{16,49}... | collective-permute-start | bytes 98312 | tf_op jit(solution)/shard_map/ppermute | solution.py:442
  (13 other events, 112.3 us)
